TPU v7x, 512 devices: a whole 4x8x8 slice. The times are simulated.
512 devices in a mesh: member: 32 (over z, x), tensor: 16 (over y, core).
Axes of the slice: x: 4, y: 8, z: 8, core: 2. Of those that a mesh axis runs over, the one named last changes fastest.
Arguments:
- query: bfloat16 [16, 32, 8192], P(None, 'member'), may hold values from -106.06602 to 106.06602
- new_kv: bfloat16 [2, 16, 32, 1024], P(None, None, 'member'), may hold values from -20 to 20
- cache: bfloat16 [2, 32, 1024, 1024], P(None, 'member', 'tensor'), may hold values from -6 to 6
- lengths: int32 [32], P('member'), may hold values from 600 to 1024, as said below
- w_out: bfloat16 [8192, 8192], P('tensor', 'member'), may hold values from -0.625 to 0.625
- resid: bfloat16 [16, 32, 8192], P(None, None, 'member'), may hold values from -20 to 20
- norm_gain: float32 [8192], P('member'), may hold values from 0.5 to 1.5
- head: bfloat16 [8192, 65536], P(None, ('member', 'tensor')), may hold values from -0.198873782 to 0.198873782
- noise: float32 [16, 65536], P(None, ('member', 'tensor')), may hold values from -6 to 6
Outputs:
- noisy_scores: float32 [16, 65536], P(None, ('member', 'tensor'))
Inputs may be any that keep to these rules, and one draw needn't show every extreme that they name: `lengths`: at least one prompt fills its whole cache, and at least one has the fewest valid positions.
All inputs are finite; a program needn't handle non-finite values.
Results may differ from a plain program's by a relative error of at most 0.025.
Values may be sent and summed in bfloat16 or wider, within the bound.
No kernel may reach another device: no remote copies, remote signals or barrier semaphores. Data moves between devices by JAX's collectives and lax.ppermute only.
A program may use at most 64 MiB of HBM per device.

v0:
```python
import jax
import jax.numpy as jnp
from jax import lax
from jax.sharding import PartitionSpec as P

D = 8192
NH = 64
KVH = 8
HD = 128


def on_device(query, new_kv, cache, lengths, w_out, resid, norm_gain, head, noise):
    queries, prompt_count, _ = query.shape
    cache_rows = cache.shape[2]
    group = NH // KVH
    score_scale = HD ** (-0.5)
    tensor_index = lax.axis_index("tensor")
    tensor_count = lax.axis_size("tensor")
    local_heads = NH // tensor_count
    grouped = query.reshape(queries, prompt_count, KVH, group, HD)
    key_block = cache[0].reshape(prompt_count, cache_rows, KVH, HD)
    value_block = cache[1].reshape(prompt_count, cache_rows, KVH, HD)
    scores = (
        jnp.einsum("qpgrd,pkgd->qpgrk", grouped, key_block, preferred_element_type=jnp.float32)
        * score_scale
    )
    own_key = new_kv[0].reshape(queries, prompt_count, KVH, HD)
    own_score = (
        jnp.einsum("qpgrd,qpgd->qpgr", grouped, own_key, preferred_element_type=jnp.float32)
        * score_scale
    )
    positions = tensor_index * cache_rows + jnp.arange(cache_rows, dtype=jnp.int32)
    valid_mask = positions[None, :] < lengths[:, None]
    scores = jnp.where(valid_mask[None, :, None, None, :], scores, -jnp.inf)
    local_top = jnp.maximum(jnp.max(scores, axis=-1), own_score)
    row_top = lax.pmax(local_top, "tensor")
    weights = jnp.exp(scores - row_top[..., None])
    denominator = jnp.sum(weights, axis=-1).reshape(queries, prompt_count, NH)
    numerator = jnp.einsum(
        "qpgrk,pkgd->qpgrd",
        weights.astype(jnp.bfloat16),
        value_block,
        preferred_element_type=jnp.float32,
    ).reshape(queries, prompt_count, NH, HD)
    numer_mine, denom_mine = (
        lax.psum_scatter(
            numerator.astype(jnp.bfloat16), "tensor", scatter_dimension=2, tiled=True
        ).astype(jnp.float32),
        lax.psum_scatter(
            denominator.astype(jnp.bfloat16), "tensor", scatter_dimension=2, tiled=True
        ).astype(jnp.float32),
    )
    own_weight = jnp.exp(own_score - row_top).reshape(queries, prompt_count, NH)
    own_weight = lax.dynamic_slice_in_dim(own_weight, tensor_index * local_heads, local_heads, 2)
    own_value = jnp.broadcast_to(
        new_kv[1].reshape(queries, prompt_count, KVH, 1, HD),
        (queries, prompt_count, KVH, group, HD),
    ).reshape(queries, prompt_count, NH, HD)
    own_value = lax.dynamic_slice_in_dim(own_value, tensor_index * local_heads, local_heads, 2)
    own_rounded = lax.optimization_barrier(own_weight.astype(jnp.bfloat16)).astype(jnp.float32)
    numer_mine = numer_mine + own_rounded[..., None] * own_value.astype(jnp.float32)
    denom_mine = denom_mine + own_weight
    attended = (
        (numer_mine / denom_mine[..., None])
        .astype(jnp.bfloat16)
        .reshape(queries, prompt_count, local_heads * HD)
    )
    partial_value = jnp.einsum(
        "qpc,cd->qpd",
        lax.all_gather(attended, "member", axis=1, tiled=True),
        w_out,
        preferred_element_type=jnp.float32,
    )
    projected = lax.psum(partial_value.astype(jnp.bfloat16), "tensor").astype(jnp.float32)
    hidden = (resid.astype(jnp.float32) + projected).astype(jnp.bfloat16)
    full_rows, full_gain = (
        lax.all_gather(hidden, "member", axis=2, tiled=True),
        lax.all_gather(norm_gain.astype(jnp.bfloat16), "member", axis=0, tiled=True).astype(
            norm_gain.dtype
        ),
    )
    square_total = jnp.einsum(
        "qpd,qpd->qp", full_rows, full_rows, preferred_element_type=jnp.float32
    )
    factor = lax.rsqrt(square_total / D + 1e-05)
    normed = (full_rows.astype(jnp.float32) * factor[..., None] * full_gain).astype(jnp.bfloat16)
    logits = jnp.einsum("qpd,dv->qpv", normed, head, preferred_element_type=jnp.float32)
    logit_top = lax.pmax(jnp.max(logits, axis=-1), ("member", "tensor"))
    exp_terms = jnp.exp(logits - logit_top[..., None])
    mass_total = lax.psum(jnp.sum(exp_terms, axis=-1), ("member", "tensor"))
    probabilities = exp_terms / mass_total[..., None]
    averaged = jnp.mean(probabilities, axis=1)
    vocab_total = head.shape[1] * lax.axis_size("member") * lax.axis_size("tensor")
    return jnp.log(vocab_total * averaged) + noise


def solution(mesh):
    placed = (
        P(None, "member", None),
        P(None, None, "member", None),
        P(None, "member", "tensor", None),
        P("member"),
        P("tensor", "member"),
        P(None, None, "member"),
        P("member"),
        P(None, ("member", "tensor")),
        P(None, ("member", "tensor")),
    )
    return jax.shard_map(
        on_device,
        mesh=mesh,
        in_specs=placed,
        out_specs=P(None, ("member", "tensor")),
        check_vma=False,
    )
```

profile of v0, /device:TPU:1, one launch (start us, length us, event | category | flops | bytes accessed | tf_op | source)
XLA Modules:
  0.0 606.2 jit_solution(17225016094610878798)
XLA Ops:
  7.3 0.8 slice_bitcast_fusion.2
  8.2 1.0 copy.47
  9.2 0.3 fusion.29
  9.5 1.0 slice_bitcast_fusion
  10.6 0.4 fusion.27
  11.0 49.0 %pmax.14 = f32[16,1,8,8]{0,3,2,1:T(8,128)S(1)} all-reduce(f32[16,1,8,8]{0,3,2,1:T(8,128)S(1)} %maximum_bitcast_fusion), channel_id=1, replica_groups=mesh['member'=32,'tensor'=16] {'tensor'}, use_global_device_ids=true, to_apply=%region_1.2 | all-reduce | flops 1024 | bytes 8192 | tf_op jit(solution)/shard_map/pmax | solution.py:36
  60.0 0.4 fusion.15
  60.7 0.9 copy.27
  61.8 1.3 dynamic-slice.4
  63.7 45.8 %all-reduce = bf16[16,1,64]{0,2,1:T(8,128)(2,1)S(1)} all-reduce(bf16[16,1,64]{0,2,1:T(8,128)(2,1)S(1)} %bitcast.113), channel_id=3, replica_groups=mesh['member'=32,'tensor'=16] {'tensor'}, use_global_device_ids=true, to_apply=%region_4.5.clone | all-reduce | flops 1024 | bytes 4096
  109.5 11.3 %reduce-scatter.3.cloned.1.call-done = bf16[16,1,4,128]{3,0,1,2:T(8,128)(2,1)} async-done(((bf16[16,1,64,128]{3,0,1,2:T(8,128)(2,1)}), bf16[16,1,4,128]{3,0,1,2:T(8,128)(2,1)}) %reduce-scatter.3.cloned.1.call-update) | async-done | bytes 16400 | tf_op jit(solution)/shard_map/reduce_scatter | solution.py:46
  120.8 0.8 copy_bitcast_fusion.1
  121.7 37.9 %all_gather.9 = bf16[16,32,512]{2,0,1:T(8,128)(2,1)S(1)} all-gather(bf16[16,1,512]{2,0,1:T(8,128)(2,1)S(1)} %copy_bitcast_fusion.1), channel_id=1, replica_groups=mesh['member'=32,'tensor'=16] {'member'}, dimensions={1}, use_global_device_ids=true | all-gather | bytes 540672 | tf_op jit(solution)/shard_map/all_gather | solution.py:70
  159.6 2.1 convolution_convert_fusion
  161.7 123.9 %all-reduce.3.cloned.1.call-done = bf16[16,32,256]{2,1,0:T(8,128)(2,1)} async-done(((bf16[16,32,256]{2,1,0:T(8,128)(2,1)}), bf16[16,32,256]{2,1,0:T(8,128)(2,1)}) %all-reduce.3.cloned.1.call-update) | async-done | bytes 262160 | tf_op jit(solution)/shard_map/psum | solution.py:74
  285.7 1.7 add_convert_fusion
  287.5 35.3 %all-gather = bf16[32,1,256]{2,1,0:T(2,128)(2,1)S(1)} all-gather(bf16[1,1,256]{2,1,0:T(2,128)(2,1)S(1)} %reshape.112), channel_id=1, replica_groups=mesh['member'=32,'tensor'=16] {'member'}, dimensions={0}, use_global_device_ids=true | all-gather | bytes 16896 | tf_op jit(solution)/shard_map/all_gather | solution.py:78
  322.8 74.1 %all-gather.3.cloned.1.call-done = bf16[16,32,8192]{2,1,0:T(8,128)(2,1)} async-done(((bf16[16,32,256]{2,1,0:T(8,128)(2,1)}), bf16[16,32,8192]{2,1,0:T(8,128)(2,1)}) %all-gather.3.cloned.1.call-update) | async-done | bytes 8388624 | tf_op jit(solution)/shard_map/all_gather | solution.py:77
  396.9 5.2 fusion.2
  402.2 0.5 copy-done.1
  402.7 2.5 fusion.28
  405.2 98.4 %pmax.15 = f32[16,32]{1,0:T(8,128)S(1)} all-reduce(f32[16,32]{1,0:T(8,128)S(1)} %get-tuple-element.13), channel_id=1, replica_groups=mesh['member'=32,'tensor'=16] {'member','tensor'}, use_global_device_ids=true, to_apply=%region_7.8 | all-reduce | flops 512 | bytes 4096 | tf_op jit(solution)/shard_map/pmax | solution.py:88
  503.9 95.0 %psum.15 = f32[16,32]{1,0:T(8,128)S(1)} all-reduce(f32[16,32]{1,0:T(8,128)S(1)} %fusion.19), channel_id=1, replica_groups=mesh['member'=32,'tensor'=16] {'member','tensor'}, use_global_device_ids=true, to_apply=%region_9.10 | all-reduce | flops 512 | bytes 4096 | tf_op jit(solution)/shard_map/psum | solution.py:90
  599.1 0.6 log_add_fusion
  (36 shorter events, 1.2 us)
Async XLA Ops:
  6.5 395.6 %copy-start = (bf16[8192,128]{1,0:T(8,128)(2,1)S(1)}, bf16[8192,128]{1,0:T(8,128)(2,1)}, u32[]{:S(2)}) copy-start(bf16[8192,128]{1,0:T(8,128)(2,1)} %param.16) | copy-start | bytes 6291460
  6.5 279.1 %copy-start.2 = (bf16[16,32,256]{2,1,0:T(8,128)(2,1)S(1)}, bf16[16,32,256]{2,1,0:T(8,128)(2,1)}, u32[]{:S(2)}) copy-start(bf16[16,32,256]{2,1,0:T(8,128)(2,1)} %param.14) | copy-start | bytes 786436
  6.5 280.9 %copy-start.4 = (f32[256]{0:T(256)S(1)}, f32[256]{0:T(256)}, u32[]{:S(2)}) copy-start(f32[256]{0:T(256)} %param.15) | copy-start | bytes 3076
  6.5 114.3 %reduce-scatter.3.cloned.1.call-start = ((), (), s32[]{:S(2)}) async-start(), calls=%async_computation.1 | async-start | bytes 278528 | tf_op jit(solution)/shard_map/reduce_scatter | solution.py:46
  61.6 224.1 %all-reduce.3.cloned.1.call-start = ((), (), s32[]{:S(2)}) async-start(), calls=%async_computation.2 | async-start | bytes 524288 | tf_op jit(solution)/shard_map/psum | solution.py:74
  161.7 235.2 %all-gather.3.cloned.1.call-start = ((), (), s32[]{:S(2)}) async-start(), calls=%async_computation.3 | async-start | bytes 8650752 | tf_op jit(solution)/shard_map/all_gather | solution.py:77
  396.9 5.8 copy-start.1
  402.7 196.4 %copy-start.3 = (f32[16,128]{1,0:T(8,128)S(1)}, f32[16,128]{1,0:T(8,128)}, u32[]{:S(2)}) copy-start(f32[16,128]{1,0:T(8,128)} %param.17) | copy-start | bytes 24580
Sparse Core Ops, SparseCore 0:
  61.7 59.0 reduce-scatter.2
  161.8 123.8 all-reduce.2
  288.7 108.1 all-gather.2
where the time goes:
time: 607 us; the launch traced here: 606 us
  blocking collectives  361 us (59%)
  waiting for transfers between devices  209 us (34%)
  between operations  14.8 us (2%)
  other arithmetic  9.38 us (2%)
    psum x1, waiting for transfers between devices, on_device(): lax.psum(partial_value.astype(jnp.bfloat16), 'tensor').astype(jnp.float32)  124 us
    pmax x1, blocking collectives, on_device(): logit_top = lax.pmax(jnp.max(logits, axis=-1), ('member', 'tensor'))  98.4 us
    psum x1, blocking collectives, on_device(): mass_total = lax.psum(jnp.sum(exp_terms, axis=-1), ('member', 'tensor'))  95 us
    all_gather x1, waiting for transfers between devices, on_device(): lax.all_gather(hidden, 'member', axis=2, tiled=True)  74.1 us
    pmax x1, blocking collectives, on_device(): row_top = lax.pmax(local_top, 'tensor')  49 us
    unnamed x1, blocking collectives  45.8 us
    all_gather x1, blocking collectives, on_device(): lax.all_gather(attended, 'member', axis=1, tiled=True)  37.9 us
    all_gather x1, blocking collectives, on_device(): lax.all_gather(norm_gain.astype(jnp.bfloat16), 'member', axis=0, tiled=True)  35.3 us
  transfers between devices with their start and end apart: 3, of which 3 were waited for; matrix products, arithmetic and copies ran while one was open for 0% of the time, Pallas kernels for 0%

commit v1 on v0

v1 whole, which is shorter than its diff:
```python
import functools

import jax
import jax.numpy as jnp
from jax import lax
from jax.experimental import pallas as pl
from jax.experimental.pallas import tpu as pltpu
from jax.sharding import Mesh
from jax.sharding import PartitionSpec as P

NZ, NX, NY, NC = 8, 4, 8, 2
MEMBER = ("z", "x")
TENSOR = ("y", "c")

D = 8192
KVH = 8
GROUP = 8
HD = 128
QUERIES = 16
PROMPTS = 32
VOCAB = 65536
ROWS = PROMPTS * QUERIES
CACHE_ROWS = 64
LOW = -1e30

BF16 = jnp.bfloat16
F32 = jnp.float32


def call(body, out_shape, operands, spaces=None):
    vmem = pl.BlockSpec(memory_space=pltpu.VMEM)
    smem = pl.BlockSpec(memory_space=pltpu.SMEM)
    spaces = spaces or "v" * len(operands)
    return pl.pallas_call(
        body,
        out_shape=out_shape,
        in_specs=[smem if s == "s" else vmem for s in spaces],
        out_specs=jax.tree.map(lambda _: vmem, out_shape),
    )(*operands)


def shape(dims, dtype=BF16):
    return jax.ShapeDtypeStruct(dims, dtype)


def split_pair(value):
    high = value.astype(BF16).astype(F32)
    return high, value - high


def diagonal(rows):
    return lax.broadcasted_iota(jnp.int32, (rows, 128), 0) == lax.broadcasted_iota(
        jnp.int32, (rows, 128), 1
    )


def to_row(column):
    return jnp.sum(jnp.where(diagonal(column.shape[0]), column, 0.0), axis=0, keepdims=True)


def to_column(row):
    return jnp.sum(jnp.where(diagonal(128), row, 0.0), axis=1, keepdims=True)


def attend_kernel(length_ref, query_ref, new_ref, cache_ref, out_ref):
    tensor_index = lax.axis_index("y") * NC + lax.axis_index("c")
    valid_rows = length_ref[0] - tensor_index * CACHE_ROWS
    positions = CACHE_ROWS + QUERIES
    row = lax.broadcasted_iota(jnp.int32, (positions, 128), 0)
    lane = lax.broadcasted_iota(jnp.int32, (positions, 128), 1)
    own_from = jnp.where(tensor_index == 0, CACHE_ROWS, positions)
    valid = ((row < CACHE_ROWS) & (row < valid_rows)) | (
        (row >= own_from) & (row - CACHE_ROWS == lane % QUERIES)
    )
    stat_row = lax.broadcasted_iota(jnp.int32, (16, 128), 0)
    for g in range(KVH):
        columns = slice(g * HD, (g + 1) * HD)
        heads = [
            query_ref[:, (g * GROUP + r) * HD : (g * GROUP + r + 1) * HD] for r in range(GROUP)
        ]
        rows = jnp.concatenate(heads, axis=0)
        keys = jnp.concatenate([cache_ref[0, :, columns], new_ref[0, :, columns]], axis=0)
        values = jnp.concatenate([cache_ref[1, :, columns], new_ref[1, :, columns]], axis=0)
        scores = lax.dot_general(
            keys, rows, (((1,), (1,)), ((), ())), preferred_element_type=F32
        ) * HD ** (-0.5)
        scores = jnp.where(valid, scores, LOW)
        top = jnp.max(scores, axis=0, keepdims=True).astype(BF16).astype(F32)
        weights = jnp.where(valid, jnp.exp(scores - top), 0.0)
        high, low = split_pair(jnp.sum(weights, axis=0, keepdims=True))
        totals = lax.dot_general(
            weights.astype(BF16), values, (((0,), (0,)), ((), ())), preferred_element_type=F32
        ).astype(BF16)
        stats = jnp.where(
            stat_row == 0,
            top,
            jnp.where(stat_row == 1, high, jnp.where(stat_row == 2, low, 0.0)),
        ).astype(BF16)
        for half in range(2):
            out_ref[2 * g + half, 0:64, :] = totals[64 * half : 64 * half + 64]
            out_ref[2 * g + half, 64:80, :] = stats


def combine_kernel(parts_ref, out_ref):
    core = lax.axis_index("c")
    stats = parts_ref[:, 64:80, :].astype(F32)
    tops, totals = stats[:, 0, :], stats[:, 1, :] + stats[:, 2, :]
    weight = jnp.exp(tops - jnp.max(tops, axis=0, keepdims=True))
    scale = weight / jnp.sum(weight * totals, axis=0, keepdims=True)
    scale = jnp.concatenate([scale, jnp.zeros((112, 128), F32)], axis=0).T
    scale = jnp.where(core == 1, scale[64:, :], scale[:64, :])
    attended = jnp.zeros((64, 128), F32)
    for source in range(NY * NC):
        attended += scale[:, source : source + 1] * parts_ref[source, 0:64, :].astype(F32)
    attended = attended.astype(BF16)
    for target in range(NZ * NX):
        out_ref[target] = attended


def project_kernel(attended_ref, weight_ref, out_ref):
    features = jnp.concatenate(
        [attended_ref[:, 16 * r : 16 * r + 16, :].reshape(ROWS, HD) for r in range(4)], axis=1
    )
    partial = jnp.dot(features, weight_ref[...], preferred_element_type=F32).astype(BF16)
    for y in range(NY):
        for c in range(NC):
            out_ref[NC * y + c] = partial[64 * y : 64 * y + 64, 128 * c : 128 * c + 128]


def residual_kernel(parts_ref, resid_ref, gain_ref, out_ref):
    core = lax.axis_index("c")
    hidden = resid_ref[...].astype(F32)
    projected = parts_ref[0].astype(F32)
    for source in range(1, NY * NC):
        projected += parts_ref[source].astype(F32)
    hidden += projected
    gain = jnp.where(core == 1, gain_ref[1:2, :], gain_ref[0:1, :])
    high, low = split_pair(to_row(jnp.sum(hidden * hidden, axis=1, keepdims=True)))
    stat_row = lax.broadcasted_iota(jnp.int32, (16, 128), 0)
    stats = jnp.where(stat_row == 0, high, jnp.where(stat_row == 1, low, 0.0)).astype(BF16)
    scaled = (hidden * gain).astype(BF16)
    for target in range(out_ref.shape[0]):
        out_ref[target, 0:64, :] = scaled
        out_ref[target, 64:80, :] = stats


def relay_kernel(parts_ref, out_ref):
    total = jnp.zeros((1, 128), F32)
    for z in range(NZ):
        total += jnp.sum(parts_ref[z, 64:80, :].astype(F32), axis=0, keepdims=True)
    high, low = split_pair(total)
    stat_row = lax.broadcasted_iota(jnp.int32, (16, 128), 0)
    stats = jnp.where(stat_row == 0, high, jnp.where(stat_row == 1, low, 0.0)).astype(BF16)
    for y in range(NY):
        for z in range(NZ):
            out_ref[y, 64 * z : 64 * z + 64, :] = parts_ref[z, 0:64, :]
        out_ref[y, 512:528, :] = stats


def head_kernel(rows_ref, head_ref, out_ref):
    features = jnp.concatenate(
        [
            jnp.concatenate([rows_ref[y, 64 * z : 64 * z + 64, :] for z in range(NZ)], axis=1)
            for y in range(NY)
        ],
        axis=0,
    )
    stat_row = lax.broadcasted_iota(jnp.int32, (16, 128), 0)
    stats = jnp.zeros((16, 128), F32)
    for y in range(NY):
        pair = rows_ref[y, 512:528, :].astype(F32)
        stats = jnp.where(
            stat_row == y, pair[0:1], jnp.where(stat_row == NY + y, pair[1:2], stats)
        )
    stats = stats.astype(BF16)
    for pair in range(4):
        block = jnp.concatenate(
            [head_ref[2 * pair + k].reshape(NZ * 128, 128) for k in range(2)], axis=1
        )
        partial = jnp.dot(features, block, preferred_element_type=F32).astype(BF16)
        for k in range(2):
            out_ref[2 * pair + k, 0:ROWS, :] = partial[:, 128 * k : 128 * k + 128]
            out_ref[2 * pair + k, ROWS : ROWS + 16, :] = stats


def logit_kernel(parts_ref, logits_ref, out_ref):
    stats = parts_ref[0, ROWS : ROWS + 16, :].astype(F32)
    for source in range(1, NX * NC):
        stats += parts_ref[source, ROWS : ROWS + 16, :].astype(F32)
    factor = lax.rsqrt((stats[0:NY] + stats[NY:]) / D + 1e-05)
    tops, totals = [], []
    for block in range(4):
        rows = slice(128 * block, 128 * block + 128)
        logits = parts_ref[0, rows, :].astype(F32)
        for source in range(1, NX * NC):
            logits += parts_ref[source, rows, :].astype(F32)
        column = jnp.concatenate(
            [to_column(factor[2 * block + k : 2 * block + k + 1])[0:64] for k in range(2)], axis=0
        )
        logits = logits * column
        logits_ref[rows, :] = logits
        top = jnp.max(logits, axis=1, keepdims=True)
        tops.append(to_row(top))
        totals.append(to_row(jnp.sum(jnp.exp(logits - top), axis=1, keepdims=True)))
    packed = jnp.concatenate(tops + totals, axis=0)
    for target in range(NY * NC):
        out_ref[target] = packed


def merge_stats(parts):
    tops = parts[:, 0:4, :]
    top = jnp.max(tops, axis=0)
    total = jnp.sum(jnp.exp(tops - top[None]) * parts[:, 4:8, :], axis=0)
    return top, total


def merge_kernel(parts_ref, out_ref):
    top, total = merge_stats(parts_ref[...])
    packed = jnp.concatenate([top, total], axis=0)
    for target in range(NZ * NX):
        out_ref[target] = packed


def vote_kernel(parts_ref, logits_ref, noise_ref, out_ref):
    top, total = merge_stats(parts_ref[...])
    averaged = jnp.zeros((QUERIES, 128), F32)
    for block in range(4):
        mass = jnp.exp(
            logits_ref[128 * block : 128 * block + 128, :] - to_column(top[block : block + 1])
        ) / to_column(total[block : block + 1])
        averaged += jnp.sum(mass.reshape(8, QUERIES, 128), axis=0)
    out_ref[...] = jnp.log(VOCAB * (averaged / PROMPTS)) + noise_ref[...]


def exchange(array, axes):
    return lax.all_to_all(array, axes, 0, 0, tiled=True)


def on_device(query, new_kv, cache, lengths, w_out, resid, norm_gain, head, noise):
    y, c = lax.axis_index("y"), lax.axis_index("c")
    head_rows = lax.all_to_all(
        head.reshape(NZ, NX * NC, 128, 128), ("x", "c"), split_axis=1, concat_axis=0
    )
    resid_mine = jnp.swapaxes(
        lax.dynamic_slice(resid, (0, 4 * y, 128 * c), (QUERIES, 4, 128)), 0, 1
    ).reshape(64, 128)

    parts = call(
        attend_kernel,
        shape((NY * NC, 80, 128)),
        (lengths, query[:, 0, :], new_kv[:, :, 0, :], cache[:, 0]),
        "svvv",
    )
    parts = exchange(parts, TENSOR)
    attended = call(combine_kernel, shape((NZ * NX, 64, 128)), (parts,))
    attended = exchange(attended, MEMBER)
    partial = call(project_kernel, shape((NY * NC, 64, 128)), (attended, w_out))
    partial = exchange(partial, TENSOR)
    hidden = call(
        residual_kernel, shape((NZ, 80, 128)), (partial, resid_mine, norm_gain.reshape(2, 128))
    )
    hidden = exchange(hidden, ("z",))
    rows = call(relay_kernel, shape((NY, 528, 128)), (hidden,))
    rows = exchange(rows, ("y",))
    logits = call(head_kernel, shape((NX * NC, ROWS + 16, 128)), (rows, head_rows))
    logits = exchange(logits, ("x", "c"))
    logits, stats = call(
        logit_kernel, (shape((ROWS, 128), F32), shape((NY * NC, 8, 128), F32)), (logits,)
    )
    stats = exchange(stats, TENSOR)
    stats = call(merge_kernel, shape((NZ * NX, 8, 128), F32), (stats,))
    stats = exchange(stats, MEMBER)
    return call(vote_kernel, shape((QUERIES, 128), F32), (stats, logits, noise))


def solution(mesh):
    torus = Mesh(mesh.devices.reshape(NZ, NX, NY, NC), MEMBER + TENSOR)
    placed = (
        P(None, MEMBER, None),
        P(None, None, MEMBER, None),
        P(None, MEMBER, TENSOR, None),
        P(MEMBER),
        P(TENSOR, MEMBER),
        P(None, None, MEMBER),
        P(MEMBER),
        P(None, MEMBER + TENSOR),
        P(None, MEMBER + TENSOR),
    )
    return jax.shard_map(
        on_device,
        mesh=torus,
        in_specs=placed,
        out_specs=P(None, MEMBER + TENSOR),
        check_vma=False,
    )
```

time: 607 us -> 217 us (0.36)
  blocking collectives: 361 us -> 134 us
  waiting for transfers between devices: 209 us -> 44.1 us
  Pallas kernels: 0 us -> 22 us
  between operations: 14.8 us -> 0.72 us
  starting transfers between devices: 0.09 us -> 12 us
  other arithmetic: 9.38 us -> 0 us
    pmax x2 -> x0, blocking collectives: 147 us -> none  [the longest x1 98.4 us: on_device(): logit_top = lax.pmax(jnp.max(logits, axis=-1), ('member', 'tensor'))]
    all_to_all x0 -> x6, blocking collectives: none -> 134 us  [exchange(): return lax.all_to_all(array, axes, 0, 0, tiled=True)]
    psum x1 -> x0, waiting for transfers between devices: 124 us -> none  [on_device(): lax.psum(partial_value.astype(jnp.bfloat16), 'tensor').astype(jnp.float32)]
    psum x1 -> x0, blocking collectives: 95 us -> none  [on_device(): mass_total = lax.psum(jnp.sum(exp_terms, axis=-1), ('member', 'tensor'))]
    all_gather x1 -> x0, waiting for transfers between devices: 74.1 us -> none  [on_device(): lax.all_gather(hidden, 'member', axis=2, tiled=True)]
    all_gather x2 -> x0, blocking collectives: 73.2 us -> none  [the longest x1 37.9 us: on_device(): lax.all_gather(attended, 'member', axis=1, tiled=True)]
    unnamed x1 -> x0, blocking collectives: 45.8 us -> none
    all_to_all x0 -> x3, waiting for transfers between devices: none -> 44.1 us  [the longest x1 24.3 us: on_device(): lax.all_to_all(head.reshape(NZ, NX * NC, 128, 128), ('x', 'c'), split_axi...]
  transfers between devices with their start and end apart: 3 -> 3, of which waited for: 3 -> 3; matrix products, arithmetic and copies ran while one was open for 0% -> 1% of each run, Pallas kernels for 0% -> 1%
where the time goes in v1:
time: 217 us; the launch traced here: 216 us
  blocking collectives  134 us (62%)
  waiting for transfers between devices  44.1 us (20%)
  Pallas kernels  22 us (10%)
  starting transfers between devices  12 us (6%)
  local copies, waits for them, and re-layouts  3.55 us (2%)
    all_to_all x6, blocking collectives, exchange(): return lax.all_to_all(array, axes, 0, 0, tiled=True)  134 us
    all_to_all x1, waiting for transfers between devices, on_device(): lax.all_to_all(head.reshape(NZ, NX * NC, 128, 128), ('x', 'c'), split_axi...  24.3 us
    pallas_call x9, Pallas kernels, call(): pl.pallas_call(body, out_shape=out_shape, in_specs=[smem if s == 's' else...  22 us
    all_to_all x2, waiting for transfers between devices, exchange(): return lax.all_to_all(array, axes, 0, 0, tiled=True)  19.9 us
    all_to_all x2, starting transfers between devices, exchange(): return lax.all_to_all(array, axes, 0, 0, tiled=True)  7.71 us
  transfers between devices with their start and end apart: 3, of which 3 were waited for; matrix products, arithmetic and copies ran while one was open for 1% of the time, Pallas kernels for 1%

profile of v1, /device:TPU:1, one launch (start us, length us, event | category | flops | bytes accessed | tf_op | source)
XLA Modules:
  0.0 215.9 jit_solution(4181578988952750331)
XLA Ops:
  0.7 3.7 %shard_map.91 = bf16[16,80,128]{2,1,0:T(8,128)(2,1)} custom-call(s32[1]{0:T(128)S(6)} %copy.15.length_ref, bf16[16,8192]{1,0:T(8,128)(2,1)} %bitcast.15, bf16[2,16,1024]{2,1,0:T(8,128)(2,1)} %bitcast.18, bf16[2,64,1024]{2,1,0:T(8,128)(2,1)} %bitcast.16), custom_call_target="tpu_custom_call" | custom-call | tf_op jit(solution)/shard_map/pallas_call | solution.py:34
  4.4 23.9 %all_to_all.55.parts_ref = bf16[16,80,128]{2,1,0:T(8,128)(2,1)} all-to-all(bf16[16,80,128]{2,1,0:T(8,128)(2,1)} %shard_map.91), channel_id=1, replica_groups=mesh['z'=8,'x'=4,'y'=8,'c'=2] {'y','c'}, dimensions={0} | all-to-all | bytes 655360 | tf_op jit(solution)/shard_map/all_to_all | solution.py:236
  28.3 2.2 %shard_map.92 = bf16[32,64,128]{2,1,0:T(8,128)(2,1)} custom-call(bf16[16,80,128]{2,1,0:T(8,128)(2,1)} %all_to_all.55.parts_ref), custom_call_target="tpu_custom_call" | custom-call | tf_op jit(solution)/shard_map/pallas_call | solution.py:34
  30.5 28.2 %all_to_all.56.attended_ref = bf16[32,64,128]{2,1,0:T(8,128)(2,1)} all-to-all(bf16[32,64,128]{2,1,0:T(8,128)(2,1)} %shard_map.92), channel_id=1, replica_groups=mesh['z'=8,'x'=4,'y'=8,'c'=2] {'z','x'}, dimensions={0} | all-to-all | bytes 1048576 | tf_op jit(solution)/shard_map/all_to_all | solution.py:236
  58.7 2.3 %shard_map.93 = bf16[16,64,128]{2,1,0:T(8,128)(2,1)} custom-call(bf16[32,64,128]{2,1,0:T(8,128)(2,1)} %all_to_all.56.attended_ref, bf16[512,256]{1,0:T(8,128)(2,1)} %weight_ref.1), custom_call_target="tpu_custom_call" | custom-call | tf_op jit(solution)/shard_map/pallas_call | solution.py:34
  61.0 3.9 %all-to-all-start.2 = ((bf16[16,64,128]{2,1,0:T(8,128)(2,1)}), bf16[16,64,128]{2,1,0:T(8,128)(2,1)S(1)}, u32[]{:S(2)}, u32[]{:S(2)}) async-start(bf16[16,64,128]{2,1,0:T(8,128)(2,1)} %shard_map.93), calls=%async_computation.2 | async-start | bytes 524288 | tf_op jit(solution)/shard_map/all_to_all | solution.py:236
  65.6 11.0 %all-to-all-done.2.parts_ref = bf16[16,64,128]{2,1,0:T(8,128)(2,1)S(1)} async-done(((bf16[16,64,128]{2,1,0:T(8,128)(2,1)}), bf16[16,64,128]{2,1,0:T(8,128)(2,1)S(1)}, u32[]{:S(2)}, u32[]{:S(2)}) %all-to-all-start.2) | async-done | bytes 262176 | tf_op jit(solution)/shard_map/all_to_all | solution.py:236
  76.6 0.7 copy-done.3
  77.3 1.8 shard_map.94
  79.1 3.8 %all-to-all-start.3 = ((bf16[8,80,128]{2,1,0:T(8,128)(2,1)}), bf16[8,80,128]{2,1,0:T(8,128)(2,1)S(1)}, u32[]{:S(2)}, u32[]{:S(2)}) async-start(bf16[8,80,128]{2,1,0:T(8,128)(2,1)} %shard_map.94), calls=%async_computation.3 | async-start | bytes 327680 | tf_op jit(solution)/shard_map/all_to_all | solution.py:236
  82.9 1.5 copy.14
  84.3 8.9 %all-to-all-done.3.parts_ref = bf16[8,80,128]{2,1,0:T(8,128)(2,1)S(1)} async-done(((bf16[8,80,128]{2,1,0:T(8,128)(2,1)}), bf16[8,80,128]{2,1,0:T(8,128)(2,1)S(1)}, u32[]{:S(2)}, u32[]{:S(2)}) %all-to-all-start.3) | async-done | bytes 163872 | tf_op jit(solution)/shard_map/all_to_all | solution.py:236
  93.2 0.7 copy-done.4
  93.9 4.3 %all-to-all-start.5 = ((bf16[1,8,8,128,128]{4,3,1,0,2:T(8,128)(2,1)}), bf16[1,8,8,128,128]{4,3,1,0,2:T(8,128)(2,1)S(1)}, u32[]{:S(2)}, u32[]{:S(2)}) async-start(bf16[1,8,8,128,128]{4,3,1,0,2:T(8,128)(2,1)} %copy.14), calls=%async_computation.5 | async-start | bytes 4194304 | tf_op jit(solution)/shard_map/all_to_all | solution.py:241
  98.1 2.0 shard_map.95
  100.1 24.3 %all-to-all-done.5 = bf16[1,8,8,128,128]{4,3,1,0,2:T(8,128)(2,1)S(1)} async-done(((bf16[1,8,8,128,128]{4,3,1,0,2:T(8,128)(2,1)}), bf16[1,8,8,128,128]{4,3,1,0,2:T(8,128)(2,1)S(1)}, u32[]{:S(2)}, u32[]{:S(2)}) %all-to-all-start.5) | async-done | bytes 2097184 | tf_op jit(solution)/shard_map/all_to_all | solution.py:241
  124.4 32.2 %all_to_all.57.rows_ref = bf16[8,528,128]{2,1,0:T(8,128)(2,1)} all-to-all(bf16[8,528,128]{2,1,0:T(8,128)(2,1)} %shard_map.95), channel_id=1, replica_groups=mesh['z'=8,'x'=4,'y'=8,'c'=2] {'y'}, dimensions={0} | all-to-all | bytes 2162688 | tf_op jit(solution)/shard_map/all_to_all | solution.py:236
  156.7 4.2 %shard_map.96 = bf16[8,528,128]{2,1,0:T(8,128)(2,1)} custom-call(bf16[8,528,128]{2,1,0:T(8,128)(2,1)} %all_to_all.57.rows_ref, bf16[8,8,128,128]{3,2,1,0:T(8,128)(2,1)} %bitcast.13), custom_call_target="tpu_custom_call" | custom-call | tf_op jit(solution)/shard_map/pallas_call | solution.py:34
  160.8 22.5 %all_to_all.58.parts_ref = bf16[8,528,128]{2,1,0:T(8,128)(2,1)} all-to-all(bf16[8,528,128]{2,1,0:T(8,128)(2,1)} %shard_map.96), channel_id=1, replica_groups=mesh['z'=8,'x'=4,'y'=8,'c'=2] {'x','c'}, dimensions={0} | all-to-all | bytes 2162688 | tf_op jit(solution)/shard_map/all_to_all | solution.py:236
  183.3 2.5 %shard_map.97 = (f32[512,128]{1,0:T(8,128)}, f32[16,8,128]{2,1,0:T(8,128)}) custom-call(bf16[8,528,128]{2,1,0:T(8,128)(2,1)} %all_to_all.58.parts_ref), custom_call_target="tpu_custom_call" | custom-call | tf_op jit(solution)/shard_map/pallas_call | solution.py:34
  185.8 12.4 %all_to_all.59.parts_ref = f32[16,8,128]{2,1,0:T(8,128)} all-to-all(f32[16,8,128]{2,1,0:T(8,128)} %get-tuple-element.7), channel_id=1, replica_groups=mesh['z'=8,'x'=4,'y'=8,'c'=2] {'y','c'}, dimensions={0} | all-to-all | bytes 131072 | tf_op jit(solution)/shard_map/all_to_all | solution.py:236
  198.2 1.5 shard_map.98
  199.7 14.4 %all_to_all.60.parts_ref = f32[32,8,128]{2,1,0:T(8,128)} all-to-all(f32[32,8,128]{2,1,0:T(8,128)} %shard_map.98), channel_id=1, replica_groups=mesh['z'=8,'x'=4,'y'=8,'c'=2] {'z','x'}, dimensions={0} | all-to-all | bytes 262144 | tf_op jit(solution)/shard_map/all_to_all | solution.py:236
  214.1 1.8 shard_map.99
  (10 shorter events, 0.7 us)
Async XLA Ops:
  0.0 64.9 %copy-start = (bf16[16,32,256]{2,1,0:T(8,128)(2,1)S(1)}, bf16[16,32,256]{2,1,0:T(8,128)(2,1)}, u32[]{:S(2)}) copy-start(bf16[16,32,256]{2,1,0:T(8,128)(2,1)} %param.14) | copy-start | bytes 786436
  58.7 24.1 %copy-start.2 = (bf16[8192,128]{1,0:T(8,128)(2,1)S(1)}, bf16[8192,128]{1,0:T(8,128)(2,1)}, u32[]{:S(2)}) copy-start(bf16[8192,128]{1,0:T(8,128)(2,1)} %param.16) | copy-start | bytes 6291460
  61.0 15.7 %all-to-all-start.2 = ((bf16[16,64,128]{2,1,0:T(8,128)(2,1)}), bf16[16,64,128]{2,1,0:T(8,128)(2,1)S(1)}, u32[]{:S(2)}, u32[]{:S(2)}) async-start(bf16[16,64,128]{2,1,0:T(8,128)(2,1)} %shard_map.93), calls=%async_computation.2 | async-start | bytes 524288 | tf_op jit(solution)/shard_map/all_to_all | solution.py:236
  76.6 0.7 copy-start.3
  79.1 14.1 %all-to-all-start.3 = ((bf16[8,80,128]{2,1,0:T(8,128)(2,1)}), bf16[8,80,128]{2,1,0:T(8,128)(2,1)S(1)}, u32[]{:S(2)}, u32[]{:S(2)}) async-start(bf16[8,80,128]{2,1,0:T(8,128)(2,1)} %shard_map.94), calls=%async_computation.3 | async-start | bytes 327680 | tf_op jit(solution)/shard_map/all_to_all | solution.py:236
  93.2 0.7 copy-start.4
  93.9 30.6 %all-to-all-start.5 = ((bf16[1,8,8,128,128]{4,3,1,0,2:T(8,128)(2,1)}), bf16[1,8,8,128,128]{4,3,1,0,2:T(8,128)(2,1)S(1)}, u32[]{:S(2)}, u32[]{:S(2)}) async-start(bf16[1,8,8,128,128]{4,3,1,0,2:T(8,128)(2,1)} %copy.14), calls=%async_computation.5 | async-start | bytes 4194304 | tf_op jit(solution)/shard_map/all_to_all | solution.py:241
  124.4 32.2 %copy-start.1 = (bf16[1,8,8,128,128]{4,3,1,0,2:T(8,128)(2,1)}, bf16[1,8,8,128,128]{4,3,1,0,2:T(8,128)(2,1)S(1)}, u32[]{:S(2)}) copy-start(bf16[1,8,8,128,128]{4,3,1,0,2:T(8,128)(2,1)S(1)} %all-to-all-done.5) | copy-start | bytes 6291460

commit v2 on v1

--- a/solution.py
+++ b/solution.py
@@ -1,5 +1,3 @@
-import functools
-
 import jax
 import jax.numpy as jnp
 from jax import lax
@@ -27,15 +25,21 @@
 F32 = jnp.float32
 
 
-def call(body, out_shape, operands, spaces=None):
+def call(body, out_shape, operands, spaces=None, scratch=(), mebibytes=8):
     vmem = pl.BlockSpec(memory_space=pltpu.VMEM)
-    smem = pl.BlockSpec(memory_space=pltpu.SMEM)
-    spaces = spaces or "v" * len(operands)
+    kinds = {
+        "v": vmem,
+        "s": pl.BlockSpec(memory_space=pltpu.SMEM),
+        "a": pl.BlockSpec(memory_space=pltpu.HBM),
+        "w": pl.BlockSpec(memory_space=pl.ANY),
+    }
     return pl.pallas_call(
         body,
         out_shape=out_shape,
-        in_specs=[smem if s == "s" else vmem for s in spaces],
+        in_specs=[kinds[s] for s in spaces or "v" * len(operands)],
         out_specs=jax.tree.map(lambda _: vmem, out_shape),
+        scratch_shapes=scratch,
+        compiler_params=pltpu.CompilerParams(vmem_limit_bytes=mebibytes * 2**20),
     )(*operands)
 
 
@@ -62,7 +66,15 @@
     return jnp.sum(jnp.where(diagonal(128), row, 0.0), axis=1, keepdims=True)
 
 
-def attend_kernel(length_ref, query_ref, new_ref, cache_ref, out_ref):
+def attend_kernel(length_ref, *refs):
+    sources, out_ref, buffers, semaphores = refs[:3], refs[3], refs[4:7], refs[7]
+    copies = [
+        pltpu.make_async_copy(source, buffer, semaphores.at[i])
+        for i, (source, buffer) in enumerate(zip(sources, buffers))
+    ]
+    for copy in copies:
+        copy.start()
+    query_ref, new_ref, cache_ref = buffers
     tensor_index = lax.axis_index("y") * NC + lax.axis_index("c")
     valid_rows = length_ref[0] - tensor_index * CACHE_ROWS
     positions = CACHE_ROWS + QUERIES
@@ -73,6 +85,8 @@
         (row >= own_from) & (row - CACHE_ROWS == lane % QUERIES)
     )
     stat_row = lax.broadcasted_iota(jnp.int32, (16, 128), 0)
+    for copy in copies:
+        copy.wait()
     for g in range(KVH):
         columns = slice(g * HD, (g + 1) * HD)
         heads = [
@@ -136,63 +150,83 @@
     hidden += projected
     gain = jnp.where(core == 1, gain_ref[1:2, :], gain_ref[0:1, :])
     high, low = split_pair(to_row(jnp.sum(hidden * hidden, axis=1, keepdims=True)))
-    stat_row = lax.broadcasted_iota(jnp.int32, (16, 128), 0)
+    stat_row = lax.broadcasted_iota(jnp.int32, (8, 128), 0)
     stats = jnp.where(stat_row == 0, high, jnp.where(stat_row == 1, low, 0.0)).astype(BF16)
     scaled = (hidden * gain).astype(BF16)
-    for target in range(out_ref.shape[0]):
+    for target in range(NZ * NY):
         out_ref[target, 0:64, :] = scaled
-        out_ref[target, 64:80, :] = stats
-
-
-def relay_kernel(parts_ref, out_ref):
-    total = jnp.zeros((1, 128), F32)
-    for z in range(NZ):
-        total += jnp.sum(parts_ref[z, 64:80, :].astype(F32), axis=0, keepdims=True)
-    high, low = split_pair(total)
-    stat_row = lax.broadcasted_iota(jnp.int32, (16, 128), 0)
-    stats = jnp.where(stat_row == 0, high, jnp.where(stat_row == 1, low, 0.0)).astype(BF16)
-    for y in range(NY):
-        for z in range(NZ):
-            out_ref[y, 64 * z : 64 * z + 64, :] = parts_ref[z, 0:64, :]
-        out_ref[y, 512:528, :] = stats
-
-
-def head_kernel(rows_ref, head_ref, out_ref):
-    features = jnp.concatenate(
+        out_ref[target, 64:72, :] = stats
+
+
+def gathered(ref):
+    return jnp.concatenate(
         [
-            jnp.concatenate([rows_ref[y, 64 * z : 64 * z + 64, :] for z in range(NZ)], axis=1)
+            jnp.concatenate([ref[NY * z + y, 0:64, :] for z in range(NZ)], axis=1)
             for y in range(NY)
         ],
         axis=0,
     )
+
+
+def square_totals(ref):
+    return [sum(ref[NY * z + y, 64:72, :].astype(F32) for z in range(NZ)) for y in range(NY)]
+
+
+def head_block(refs, start):
+    rows = pl.ds(pl.multiple_of(start, 128), 128)
+    return jnp.concatenate([ref[:, rows, :].reshape(NZ * 128, 128) for ref in refs], axis=1)
+
+
+def near_kernel(mine_ref, head_ref, *refs):
+    swapped_refs, (out_ref, block_ref, semaphore) = refs[:3], refs[3:]
+    fetch = pltpu.make_async_copy(head_ref.at[:, lax.axis_index("x")], block_ref, semaphore)
+    fetch.start()
+    start = lax.axis_index("c") * 128
+    mine = gathered(mine_ref)
+    fetch.wait()
+    blocks = (block_ref,) + swapped_refs
+    for pair in range(NX // 2):
+        out_ref[pair] = jnp.dot(
+            mine, head_block(blocks[2 * pair : 2 * pair + 2], start), preferred_element_type=F32
+        )
+
+
+def far_kernel(mine_ref, other_ref, near_ref, head_ref, *refs):
+    swapped_refs, (out_ref, block_ref, semaphore) = refs[:3], refs[3:]
+    x = lax.axis_index("x")
+    fetch = pltpu.make_async_copy(head_ref.at[:, x], block_ref, semaphore)
+    fetch.start()
+    start = (1 - lax.axis_index("c")) * 128
     stat_row = lax.broadcasted_iota(jnp.int32, (16, 128), 0)
     stats = jnp.zeros((16, 128), F32)
-    for y in range(NY):
-        pair = rows_ref[y, 512:528, :].astype(F32)
-        stats = jnp.where(
-            stat_row == y, pair[0:1], jnp.where(stat_row == NY + y, pair[1:2], stats)
+    for y, (mine, other) in enumerate(zip(square_totals(mine_ref), square_totals(other_ref))):
+        high, low = split_pair(jnp.sum(mine + other, axis=0, keepdims=True))
+        stats = jnp.where(stat_row == y, high, jnp.where(stat_row == NY + y, low, stats))
+    stats = stats.astype(BF16)
+    other = gathered(other_ref)
+    fetch.wait()
+    blocks = (block_ref,) + swapped_refs
+    for pair in range(NX // 2):
+        partial = near_ref[pair] + jnp.dot(
+            other, head_block(blocks[2 * pair : 2 * pair + 2], start), preferred_element_type=F32
         )
-    stats = stats.astype(BF16)
-    for pair in range(4):
-        block = jnp.concatenate(
-            [head_ref[2 * pair + k].reshape(NZ * 128, 128) for k in range(2)], axis=1
-        )
-        partial = jnp.dot(features, block, preferred_element_type=F32).astype(BF16)
+        partial = partial.astype(BF16)
         for k in range(2):
-            out_ref[2 * pair + k, 0:ROWS, :] = partial[:, 128 * k : 128 * k + 128]
-            out_ref[2 * pair + k, ROWS : ROWS + 16, :] = stats
+            target = lax.rem(x + NX - (2 * pair + k), NX)
+            out_ref[target, 0:ROWS, :] = partial[:, 128 * k : 128 * k + 128]
+            out_ref[target, ROWS : ROWS + 16, :] = stats
 
 
 def logit_kernel(parts_ref, logits_ref, out_ref):
     stats = parts_ref[0, ROWS : ROWS + 16, :].astype(F32)
-    for source in range(1, NX * NC):
+    for source in range(1, NX):
         stats += parts_ref[source, ROWS : ROWS + 16, :].astype(F32)
     factor = lax.rsqrt((stats[0:NY] + stats[NY:]) / D + 1e-05)
     tops, totals = [], []
     for block in range(4):
         rows = slice(128 * block, 128 * block + 128)
         logits = parts_ref[0, rows, :].astype(F32)
-        for source in range(1, NX * NC):
+        for source in range(1, NX):
             logits += parts_ref[source, rows, :].astype(F32)
         column = jnp.concatenate(
             [to_column(factor[2 * block + k : 2 * block + k + 1])[0:64] for k in range(2)], axis=0
@@ -238,9 +272,16 @@
 
 def on_device(query, new_kv, cache, lengths, w_out, resid, norm_gain, head, noise):
     y, c = lax.axis_index("y"), lax.axis_index("c")
-    head_rows = lax.all_to_all(
-        head.reshape(NZ, NX * NC, 128, 128), ("x", "c"), split_axis=1, concat_axis=0
-    )
+    x = lax.axis_index("x")
+    blocks = head.reshape(NZ, NX, 256, 128)
+    swapped = [
+        lax.ppermute(
+            lax.dynamic_index_in_dim(blocks, (x + k) % NX, 1, keepdims=False),
+            "x",
+            [(i, (i + k) % NX) for i in range(NX)],
+        )
+        for k in range(1, NX)
+    ]
     resid_mine = jnp.swapaxes(
         lax.dynamic_slice(resid, (0, 4 * y, 128 * c), (QUERIES, 4, 128)), 0, 1
     ).reshape(64, 128)
@@ -249,7 +290,13 @@
         attend_kernel,
         shape((NY * NC, 80, 128)),
         (lengths, query[:, 0, :], new_kv[:, :, 0, :], cache[:, 0]),
-        "svvv",
+        "saaa",
+        (
+            pltpu.VMEM((QUERIES, D), BF16),
+            pltpu.VMEM((2, QUERIES, KVH * HD), BF16),
+            pltpu.VMEM((2, CACHE_ROWS, KVH * HD), BF16),
+            pltpu.SemaphoreType.DMA((3,)),
+        ),
     )
     parts = exchange(parts, TENSOR)
     attended = call(combine_kernel, shape((NZ * NX, 64, 128)), (parts,))
@@ -257,13 +304,31 @@
     partial = call(project_kernel, shape((NY * NC, 64, 128)), (attended, w_out))
     partial = exchange(partial, TENSOR)
     hidden = call(
-        residual_kernel, shape((NZ, 80, 128)), (partial, resid_mine, norm_gain.reshape(2, 128))
-    )
-    hidden = exchange(hidden, ("z",))
-    rows = call(relay_kernel, shape((NY, 528, 128)), (hidden,))
-    rows = exchange(rows, ("y",))
-    logits = call(head_kernel, shape((NX * NC, ROWS + 16, 128)), (rows, head_rows))
-    logits = exchange(logits, ("x", "c"))
+        residual_kernel,
+        shape((NZ * NY, 72, 128)),
+        (partial, resid_mine, norm_gain.reshape(2, 128)),
+    )
+    mine = exchange(hidden, ("z", "y"))
+    mine, *_ = lax.optimization_barrier((mine, *swapped))
+    other = lax.ppermute(mine, "c", [(0, 1), (1, 0)])
+    scratch = (pltpu.VMEM((NZ, 256, 128), BF16), pltpu.SemaphoreType.DMA)
+    near = call(
+        near_kernel,
+        shape((NX // 2, ROWS, 256), F32),
+        (mine, blocks, *swapped),
+        "vavvv",
+        scratch,
+        12,
+    )
+    logits = call(
+        far_kernel,
+        shape((NX, ROWS + 16, 128)),
+        (mine, other, near, blocks, *swapped),
+        "vvvavvv",
+        scratch,
+        12,
+    )
+    logits = exchange(logits, ("x",))
     logits, stats = call(
         logit_kernel, (shape((ROWS, 128), F32), shape((NY * NC, 8, 128), F32)), (logits,)
     )

time: 217 us -> 169 us (0.78)
  blocking collectives: 134 us -> 95.8 us
  Pallas kernels: 22 us -> 6.79 us
  waiting for transfers between devices: 44.1 us -> 33.5 us
  starting transfers between devices: 12 us -> 20.7 us
  local copies, waits for them, and re-layouts: 3.55 us -> 10.1 us
    all_to_all x6 -> x5, blocking collectives: 134 us -> 95.8 us  [exchange(): return lax.all_to_all(array, axes, 0, 0, tiled=True)]
    all_to_all x1 -> x0, waiting for transfers between devices: 24.3 us -> none  [on_device(): lax.all_to_all(head.reshape(NZ, NX * NC, 128, 128), ('x', 'c'), split_axi...]
    ppermute x0 -> x4, waiting for transfers between devices: none -> 21.9 us  [the longest x3 21.9 us: on_device(): lax.ppermute(lax.dynamic_index_in_dim(blocks, (x + k) % NX, 1, keepdims=F...]
    pallas_call x9, Pallas kernels: 22 us -> 6.79 us  [call(): pl.pallas_call(body, out_shape=out_shape, in_specs=[kinds[s] for s in spa...]
    ppermute x0 -> x4, starting transfers between devices: none -> 11.3 us  [the longest x3 8.92 us: on_device(): lax.ppermute(lax.dynamic_index_in_dim(blocks, (x + k) % NX, 1, keepdims=F...]
    unnamed x10 -> x36, local copies, waits for them, and re-layouts: 1.38 us -> 9.83 us
    all_to_all x2, waiting for transfers between devices: 19.9 us -> 11.6 us  [exchange(): return lax.all_to_all(array, axes, 0, 0, tiled=True)]
    all_to_all x1 -> x0, starting transfers between devices: 4.25 us -> none  [on_device(): lax.all_to_all(head.reshape(NZ, NX * NC, 128, 128), ('x', 'c'), split_axi...]
  transfers between devices with their start and end apart: 3 -> 6, of which waited for: 3 -> 3; matrix products, arithmetic and copies ran while one was open for 1% -> 0% of each run, Pallas kernels for 1% -> 0%
where the time goes in v2:
time: 169 us; the launch traced here: 168 us
  blocking collectives  95.8 us (57%)
  waiting for transfers between devices  33.5 us (20%)
  starting transfers between devices  20.7 us (12%)
  local copies, waits for them, and re-layouts  10.1 us (6%)
  Pallas kernels  6.79 us (4%)
    all_to_all x5, blocking collectives, exchange(): return lax.all_to_all(array, axes, 0, 0, tiled=True)  95.8 us
    ppermute x3, waiting for transfers between devices, on_device(): lax.ppermute(lax.dynamic_index_in_dim(blocks, (x + k) % NX, 1, keepdims=F...  21.9 us
    all_to_all x2, waiting for transfers between devices, exchange(): return lax.all_to_all(array, axes, 0, 0, tiled=True)  11.6 us
    unnamed x36, local copies, waits for them, and re-layouts  9.83 us
    all_to_all x2, starting transfers between devices, exchange(): return lax.all_to_all(array, axes, 0, 0, tiled=True)  9.38 us
    ppermute x3, starting transfers between devices, on_device(): lax.ppermute(lax.dynamic_index_in_dim(blocks, (x + k) % NX, 1, keepdims=F...  8.92 us
    pallas_call x9, Pallas kernels, call(): pl.pallas_call(body, out_shape=out_shape, in_specs=[kinds[s] for s in spa...  6.79 us
  transfers between devices with their start and end apart: 6, of which 3 were waited for; matrix products, arithmetic and copies ran while one was open for 0% of the time, Pallas kernels for 0%

profile of v2, /device:TPU:1, one launch (start us, length us, event | category | flops | bytes accessed | tf_op | source)
XLA Modules:
  0.0 167.8 jit_solution(248129317249194448)
XLA Ops:
  0.7 0.9 copy-done.12
  1.7 0.9 copy-done.13
  3.4 2.1 %shard_map.91 = bf16[16,80,128]{2,1,0:T(8,128)(2,1)S(1)} custom-call(s32[1]{0:T(128)S(6)} %copy.11.length_ref, bf16[16,8192]{1,0:T(8,128)(2,1)S(1)} %bitcast.17, bf16[2,16,1024]{2,1,0:T(8,128)(2,1)S(1)} %bitcast.20, bf16[2,64,1024]{2,1,0:T(8,128)(2,1)S(1)} %bitcast.18), custom_call_target="tpu_custom_call" | custom-call | tf_op jit(solution)/shard_map/pallas_call | solution.py:36
  5.5 22.5 %all_to_all.35.parts_ref = bf16[16,80,128]{2,1,0:T(8,128)(2,1)S(1)} all-to-all(bf16[16,80,128]{2,1,0:T(8,128)(2,1)S(1)} %shard_map.91), channel_id=1, replica_groups=mesh['z'=8,'x'=4,'y'=8,'c'=2] {'y','c'}, dimensions={0} | all-to-all | bytes 655360 | tf_op jit(solution)/shard_map/all_to_all | solution.py:270
  28.4 29.2 %all_to_all.36.attended_ref = bf16[32,64,128]{2,1,0:T(8,128)(2,1)S(1)} all-to-all(bf16[32,64,128]{2,1,0:T(8,128)(2,1)S(1)} %shard_map.92), channel_id=1, replica_groups=mesh['z'=8,'x'=4,'y'=8,'c'=2] {'z','x'}, dimensions={0} | all-to-all | bytes 1048576 | tf_op jit(solution)/shard_map/all_to_all | solution.py:270
  57.6 1.0 shard_map.93
  58.6 3.9 %all-to-all-start.2 = ((bf16[16,64,128]{2,1,0:T(8,128)(2,1)}), bf16[16,64,128]{2,1,0:T(8,128)(2,1)S(1)}, u32[]{:S(2)}, u32[]{:S(2)}) async-start(bf16[16,64,128]{2,1,0:T(8,128)(2,1)} %shard_map.93), calls=%async_computation.2 | async-start | bytes 524288 | tf_op jit(solution)/shard_map/all_to_all | solution.py:270
  62.7 11.6 %all-to-all-done.2.parts_ref = bf16[16,64,128]{2,1,0:T(8,128)(2,1)S(1)} async-done(((bf16[16,64,128]{2,1,0:T(8,128)(2,1)}), bf16[16,64,128]{2,1,0:T(8,128)(2,1)S(1)}, u32[]{:S(2)}, u32[]{:S(2)}) %all-to-all-start.2) | async-done | bytes 262176 | tf_op jit(solution)/shard_map/all_to_all | solution.py:270
  74.4 1.0 copy-done.2
  75.5 5.4 %all-to-all-start.3 = ((bf16[64,72,128]{2,1,0:T(8,128)(2,1)}), bf16[64,72,128]{2,1,0:T(8,128)(2,1)S(1)}, u32[]{:S(2)}, u32[]{:S(2)}) async-start(bf16[64,72,128]{2,1,0:T(8,128)(2,1)} %copy-done.2), calls=%async_computation.3 | async-start | bytes 2359296 | tf_op jit(solution)/shard_map/all_to_all | solution.py:270
  81.1 3.9 %collective-permute-start.2 = (bf16[8,256,128]{2,1,0:T(8,128)(2,1)S(1)}, bf16[8,256,128]{2,1,0:T(8,128)(2,1)S(1)}, u32[]{:S(2)}, u32[]{:S(2)}) collective-permute-start(bf16[8,256,128]{2,1,0:T(8,128)(2,1)S(1)} %get-tuple-element.11), channel_id=1, source_target_pairs={{0,48},{16,0},{32,16},{48,32},{1,49},{17,1},{33,17},{49,33},{2,50}... | collective-permute-start | bytes 1572872 | tf_op jit(solution)/shard_map/ppermute | solution.py:278
  85.1 2.5 %collective-permute-start.1 = (bf16[8,256,128]{2,1,0:T(8,128)(2,1)S(1)}, bf16[8,256,128]{2,1,0:T(8,128)(2,1)S(1)}, u32[]{:S(2)}, u32[]{:S(2)}) collective-permute-start(bf16[8,256,128]{2,1,0:T(8,128)(2,1)S(1)} %get-tuple-element.12), channel_id=1, source_target_pairs={{0,32},{16,48},{32,0},{48,16},{1,33},{17,49},{33,1},{49,17},{2,34}... | collective-permute-start | bytes 1572872 | tf_op jit(solution)/shard_map/ppermute | solution.py:278
  87.6 2.5 %collective-permute-start = (bf16[8,256,128]{2,1,0:T(8,128)(2,1)S(1)}, bf16[8,256,128]{2,1,0:T(8,128)(2,1)S(1)}, u32[]{:S(2)}, u32[]{:S(2)}) collective-permute-start(bf16[8,256,128]{2,1,0:T(8,128)(2,1)S(1)} %get-tuple-element.13), channel_id=1, source_target_pairs={{0,16},{16,32},{32,48},{48,0},{1,17},{17,33},{33,49},{49,1},{2,18}... | collective-permute-start | bytes 1572872 | tf_op jit(solution)/shard_map/ppermute | solution.py:278
  90.1 18.0 %collective-permute-done.2.refs_2_ = bf16[8,256,128]{2,1,0:T(8,128)(2,1)S(1)} collective-permute-done((bf16[8,256,128]{2,1,0:T(8,128)(2,1)S(1)}, bf16[8,256,128]{2,1,0:T(8,128)(2,1)S(1)}, u32[]{:S(2)}, u32[]{:S(2)}) %collective-permute-start.2) | collective-permute-done | bytes 524320 | tf_op jit(solution)/shard_map/ppermute | solution.py:278
  109.7 3.9 %collective-permute-done.refs_0_ = bf16[8,256,128]{2,1,0:T(8,128)(2,1)S(1)} collective-permute-done((bf16[8,256,128]{2,1,0:T(8,128)(2,1)S(1)}, bf16[8,256,128]{2,1,0:T(8,128)(2,1)S(1)}, u32[]{:S(2)}, u32[]{:S(2)}) %collective-permute-start) | collective-permute-done | bytes 524320 | tf_op jit(solution)/shard_map/ppermute | solution.py:278
  114.4 2.4 %collective-permute-start.3 = (bf16[64,72,128]{2,1,0:T(8,128)(2,1)S(1)}, bf16[64,72,128]{2,1,0:T(8,128)(2,1)S(1)}, u32[]{:S(2)}, u32[]{:S(2)}) collective-permute-start(bf16[64,72,128]{2,1,0:T(8,128)(2,1)S(1)} %all-to-all-done.3.mine_ref), channel_id=1, source_target_pairs={{0,1},{1,0},{2,3},{3,2},{4,5},{5,4},{6,7},{7,6},{8,9},{9,8},{10,11... | collective-permute-start | bytes 3538952 | tf_op jit(solution)/shard_map/ppermute | solution.py:313
  116.8 1.0 copy-done.4
  117.8 1.0 copy-done.7
  118.9 1.0 copy-done.10
  121.3 0.8 shard_map.96
  122.1 12.5 %all_to_all.37.parts_ref = bf16[4,528,128]{2,1,0:T(8,128)(2,1)S(1)} all-to-all(bf16[4,528,128]{2,1,0:T(8,128)(2,1)S(1)} %shard_map.96), channel_id=1, replica_groups=mesh['z'=8,'x'=4,'y'=8,'c'=2] {'x'}, dimensions={0} | all-to-all | bytes 1081344 | tf_op jit(solution)/shard_map/all_to_all | solution.py:270
  135.2 14.8 %all_to_all.38.parts_ref = f32[16,8,128]{2,1,0:T(8,128)S(1)} all-to-all(f32[16,8,128]{2,1,0:T(8,128)S(1)} %get-tuple-element.9), channel_id=1, replica_groups=mesh['z'=8,'x'=4,'y'=8,'c'=2] {'y','c'}, dimensions={0} | all-to-all | bytes 131072 | tf_op jit(solution)/shard_map/all_to_all | solution.py:270
  150.0 16.9 %all_to_all.39.parts_ref = f32[32,8,128]{2,1,0:T(8,128)S(1)} all-to-all(f32[32,8,128]{2,1,0:T(8,128)S(1)} %shard_map.98), channel_id=1, replica_groups=mesh['z'=8,'x'=4,'y'=8,'c'=2] {'z','x'}, dimensions={0} | all-to-all | bytes 262144 | tf_op jit(solution)/shard_map/all_to_all | solution.py:270
  166.9 0.9 shard_map.99
  (41 shorter events, 6.1 us)
Async XLA Ops:
  0.0 62.6 %copy-start = (bf16[16,32,256]{2,1,0:T(8,128)(2,1)S(1)}, bf16[16,32,256]{2,1,0:T(8,128)(2,1)}, u32[]{:S(2)}) copy-start(bf16[16,32,256]{2,1,0:T(8,128)(2,1)} %param.14) | copy-start | bytes 786436
  0.7 1.0 copy-start.12
  1.6 0.9 copy-start.13
  2.6 0.8 copy-start.15
  5.5 52.1 %copy-start.14 = (bf16[512,256]{1,0:T(8,128)(2,1)S(1)}, bf16[512,256]{1,0:T(8,128)(2,1)}, u32[]{:S(2)}) copy-start(bf16[512,256]{1,0:T(8,128)(2,1)} %weight_ref.1) | copy-start | bytes 786436
  28.4 45.8 %copy-start.17 = (f32[256]{0:T(256)S(1)}, f32[256]{0:T(256)}, u32[]{:S(2)}) copy-start(f32[256]{0:T(256)} %param.15) | copy-start | bytes 3076
  58.6 15.7 %all-to-all-start.2 = ((bf16[16,64,128]{2,1,0:T(8,128)(2,1)}), bf16[16,64,128]{2,1,0:T(8,128)(2,1)S(1)}, u32[]{:S(2)}, u32[]{:S(2)}) async-start(bf16[16,64,128]{2,1,0:T(8,128)(2,1)} %shard_map.93), calls=%async_computation.2 | async-start | bytes 524288 | tf_op jit(solution)/shard_map/all_to_all | solution.py:270
  74.4 1.0 copy-start.2
  75.5 5.5 %copy-start.1 = (bf16[8192,128]{1,0:T(8,128)(2,1)S(1)}, bf16[8192,128]{1,0:T(8,128)(2,1)}, u32[]{:S(2)}) copy-start(bf16[8192,128]{1,0:T(8,128)(2,1)} %param.16) | copy-start | bytes 6291460
  75.5 38.9 %all-to-all-start.3 = ((bf16[64,72,128]{2,1,0:T(8,128)(2,1)}), bf16[64,72,128]{2,1,0:T(8,128)(2,1)S(1)}, u32[]{:S(2)}, u32[]{:S(2)}) async-start(bf16[64,72,128]{2,1,0:T(8,128)(2,1)} %copy-done.2), calls=%async_computation.3 | async-start | bytes 2359296 | tf_op jit(solution)/shard_map/all_to_all | solution.py:270
  81.1 26.9 %collective-permute-start.2 = (bf16[8,256,128]{2,1,0:T(8,128)(2,1)S(1)}, bf16[8,256,128]{2,1,0:T(8,128)(2,1)S(1)}, u32[]{:S(2)}, u32[]{:S(2)}) collective-permute-start(bf16[8,256,128]{2,1,0:T(8,128)(2,1)S(1)} %get-tuple-element.11), channel_id=1, source_target_pairs={{0,48},{16,0},{32,16},{48,32},{1,49},{17,1},{33,17},{49,33},{2,50}... | collective-permute-start | bytes 1572872 | tf_op jit(solution)/shard_map/ppermute | solution.py:278
  85.1 23.8 %collective-permute-start.1 = (bf16[8,256,128]{2,1,0:T(8,128)(2,1)S(1)}, bf16[8,256,128]{2,1,0:T(8,128)(2,1)S(1)}, u32[]{:S(2)}, u32[]{:S(2)}) collective-permute-start(bf16[8,256,128]{2,1,0:T(8,128)(2,1)S(1)} %get-tuple-element.12), channel_id=1, source_target_pairs={{0,32},{16,48},{32,0},{48,16},{1,33},{17,49},{33,1},{49,17},{2,34}... | collective-permute-start | bytes 1572872 | tf_op jit(solution)/shard_map/ppermute | solution.py:278
  87.6 26.0 %collective-permute-start = (bf16[8,256,128]{2,1,0:T(8,128)(2,1)S(1)}, bf16[8,256,128]{2,1,0:T(8,128)(2,1)S(1)}, u32[]{:S(2)}, u32[]{:S(2)}) collective-permute-start(bf16[8,256,128]{2,1,0:T(8,128)(2,1)S(1)} %get-tuple-element.13), channel_id=1, source_target_pairs={{0,16},{16,32},{32,48},{48,0},{1,17},{17,33},{33,49},{49,1},{2,18}... | collective-permute-start | bytes 1572872 | tf_op jit(solution)/shard_map/ppermute | solution.py:278
  108.1 0.8 copy-start.3
  108.9 0.8 copy-start.6
  113.6 0.8 copy-start.9
  114.4 6.4 %collective-permute-start.3 = (bf16[64,72,128]{2,1,0:T(8,128)(2,1)S(1)}, bf16[64,72,128]{2,1,0:T(8,128)(2,1)S(1)}, u32[]{:S(2)}, u32[]{:S(2)}) collective-permute-start(bf16[64,72,128]{2,1,0:T(8,128)(2,1)S(1)} %all-to-all-done.3.mine_ref), channel_id=1, source_target_pairs={{0,1},{1,0},{2,3},{3,2},{4,5},{5,4},{6,7},{7,6},{8,9},{9,8},{10,11... | collective-permute-start | bytes 3538952 | tf_op jit(solution)/shard_map/ppermute | solution.py:313
  116.8 1.0 copy-start.4
  117.8 1.0 copy-start.7
  118.9 1.0 copy-start.10
  119.9 1.0 copy-start.5
  119.9 1.2 copy-start.8
  119.9 1.4 copy-start.11
  122.1 44.8 %copy-start.16 = (f32[16,128]{1,0:T(8,128)S(1)}, f32[16,128]{1,0:T(8,128)}, u32[]{:S(2)}) copy-start(f32[16,128]{1,0:T(8,128)} %noise_ref.1) | copy-start | bytes 24580

commit v3 on v2

--- a/solution.py
+++ b/solution.py
@@ -84,7 +84,7 @@
     valid = ((row < CACHE_ROWS) & (row < valid_rows)) | (
         (row >= own_from) & (row - CACHE_ROWS == lane % QUERIES)
     )
-    stat_row = lax.broadcasted_iota(jnp.int32, (16, 128), 0)
+    stat_row = lax.broadcasted_iota(jnp.int32, (8, 128), 0)
     for copy in copies:
         copy.wait()
     for g in range(KVH):
@@ -111,13 +111,13 @@
             jnp.where(stat_row == 1, high, jnp.where(stat_row == 2, low, 0.0)),
         ).astype(BF16)
         for half in range(2):
-            out_ref[2 * g + half, 0:64, :] = totals[64 * half : 64 * half + 64]
-            out_ref[2 * g + half, 64:80, :] = stats
+            out_ref[NY * half + g, 0:64, :] = totals[64 * half : 64 * half + 64]
+            out_ref[NY * half + g, 64:72, :] = stats
 
 
 def combine_kernel(parts_ref, out_ref):
     core = lax.axis_index("c")
-    stats = parts_ref[:, 64:80, :].astype(F32)
+    stats = parts_ref[:, 64:72, :].astype(F32)
     tops, totals = stats[:, 0, :], stats[:, 1, :] + stats[:, 2, :]
     weight = jnp.exp(tops - jnp.max(tops, axis=0, keepdims=True))
     scale = weight / jnp.sum(weight * totals, axis=0, keepdims=True)
@@ -137,8 +137,11 @@
     )
     partial = jnp.dot(features, weight_ref[...], preferred_element_type=F32).astype(BF16)
     for y in range(NY):
+        rows = jnp.concatenate(
+            [partial[16 * (NZ * x + y) : 16 * (NZ * x + y) + 16] for x in range(NX)], axis=0
+        )
         for c in range(NC):
-            out_ref[NC * y + c] = partial[64 * y : 64 * y + 64, 128 * c : 128 * c + 128]
+            out_ref[NY * c + y] = rows[:, 128 * c : 128 * c + 128]
 
 
 def residual_kernel(parts_ref, resid_ref, gain_ref, out_ref):
@@ -161,7 +164,7 @@
 def gathered(ref):
     return jnp.concatenate(
         [
-            jnp.concatenate([ref[NY * z + y, 0:64, :] for z in range(NZ)], axis=1)
+            jnp.concatenate([ref[NZ * y + z, 0:64, :] for z in range(NZ)], axis=1)
             for y in range(NY)
         ],
         axis=0,
@@ -169,7 +172,7 @@
 
 
 def square_totals(ref):
-    return [sum(ref[NY * z + y, 64:72, :].astype(F32) for z in range(NZ)) for y in range(NY)]
+    return [sum(ref[NZ * y + z, 64:72, :].astype(F32) for z in range(NZ)) for y in range(NY)]
 
 
 def head_block(refs, start):
@@ -288,7 +291,7 @@
 
     parts = call(
         attend_kernel,
-        shape((NY * NC, 80, 128)),
+        shape((NY * NC, 72, 128)),
         (lengths, query[:, 0, :], new_kv[:, :, 0, :], cache[:, 0]),
         "saaa",
         (
@@ -297,18 +300,19 @@
             pltpu.VMEM((2, CACHE_ROWS, KVH * HD), BF16),
             pltpu.SemaphoreType.DMA((3,)),
         ),
-    )
-    parts = exchange(parts, TENSOR)
+        60,
+    )
+    parts = exchange(parts, ("c", "y"))
     attended = call(combine_kernel, shape((NZ * NX, 64, 128)), (parts,))
-    attended = exchange(attended, MEMBER)
+    attended = exchange(attended, ("x", "z"))
     partial = call(project_kernel, shape((NY * NC, 64, 128)), (attended, w_out))
-    partial = exchange(partial, TENSOR)
+    partial = exchange(partial, ("c", "y"))
     hidden = call(
         residual_kernel,
         shape((NZ * NY, 72, 128)),
         (partial, resid_mine, norm_gain.reshape(2, 128)),
     )
-    mine = exchange(hidden, ("z", "y"))
+    mine = exchange(hidden, ("y", "z"))
     mine, *_ = lax.optimization_barrier((mine, *swapped))
     other = lax.ppermute(mine, "c", [(0, 1), (1, 0)])
     scratch = (pltpu.VMEM((NZ, 256, 128), BF16), pltpu.SemaphoreType.DMA)
@@ -332,9 +336,9 @@
     logits, stats = call(
         logit_kernel, (shape((ROWS, 128), F32), shape((NY * NC, 8, 128), F32)), (logits,)
     )
-    stats = exchange(stats, TENSOR)
+    stats = exchange(stats, ("c", "y"))
     stats = call(merge_kernel, shape((NZ * NX, 8, 128), F32), (stats,))
-    stats = exchange(stats, MEMBER)
+    stats = exchange(stats, ("x", "z"))
     return call(vote_kernel, shape((QUERIES, 128), F32), (stats, logits, noise))
 
 

time: 169 us -> 164 us (0.970)
  blocking collectives: 95.8 us -> 87.8 us
  starting transfers between devices: 20.7 us -> 27.5 us
  local copies, waits for them, and re-layouts: 10.1 us -> 7.34 us
  waiting for transfers between devices: 33.5 us -> 31 us
    all_to_all x5, blocking collectives: 95.8 us -> 87.8 us  [exchange(): return lax.all_to_all(array, axes, 0, 0, tiled=True)]
    all_to_all x2, starting transfers between devices: 9.38 us -> 17 us  [exchange(): return lax.all_to_all(array, axes, 0, 0, tiled=True)]
    unnamed x36 -> x30, local copies, waits for them, and re-layouts: 9.83 us -> 7.09 us
    all_to_all x2, waiting for transfers between devices: 11.6 us -> 9.27 us  [exchange(): return lax.all_to_all(array, axes, 0, 0, tiled=True)]
  transfers between devices with their start and end apart: 6 -> 6, of which waited for: 3 -> 4; matrix products, arithmetic and copies ran while one was open for 0% -> 0% of each run, Pallas kernels for 0% -> 1%
where the time goes in v3:
time: 164 us; the launch traced here: 163 us
  blocking collectives  87.8 us (54%)
  waiting for transfers between devices  31 us (19%)
  starting transfers between devices  27.5 us (17%)
  Pallas kernels  8.45 us (5%)
  local copies, waits for them, and re-layouts  7.34 us (4%)
    all_to_all x5, blocking collectives, exchange(): return lax.all_to_all(array, axes, 0, 0, tiled=True)  87.8 us
    ppermute x3, waiting for transfers between devices, on_device(): lax.ppermute(lax.dynamic_index_in_dim(blocks, (x + k) % NX, 1, keepdims=F...  21.8 us
    all_to_all x2, starting transfers between devices, exchange(): return lax.all_to_all(array, axes, 0, 0, tiled=True)  17 us
    all_to_all x2, waiting for transfers between devices, exchange(): return lax.all_to_all(array, axes, 0, 0, tiled=True)  9.27 us
    pallas_call x9, Pallas kernels, call(): pl.pallas_call(body, out_shape=out_shape, in_specs=[kinds[s] for s in spa...  8.45 us
    ppermute x3, starting transfers between devices, on_device(): lax.ppermute(lax.dynamic_index_in_dim(blocks, (x + k) % NX, 1, keepdims=F...  7.84 us
    unnamed x30, local copies, waits for them, and re-layouts  7.09 us
  transfers between devices with their start and end apart: 6, of which 4 were waited for; matrix products, arithmetic and copies ran while one was open for 0% of the time, Pallas kernels for 1%

profile of v3, /device:TPU:1, one launch (start us, length us, event | category | flops | bytes accessed | tf_op | source)
XLA Modules:
  0.0 163.1 jit_solution(13823083933585402074)
XLA Ops:
  0.7 3.7 %shard_map.91 = bf16[16,72,128]{2,1,0:T(8,128)(2,1)} custom-call(s32[1]{0:T(128)S(6)} %copy.11.length_ref, bf16[16,8192]{1,0:T(8,128)(2,1)} %bitcast.19, bf16[2,16,1024]{2,1,0:T(8,128)(2,1)} %bitcast.21, bf16[2,64,1024]{2,1,0:T(8,128)(2,1)} %bitcast.20), custom_call_target="tpu_custom_call" | custom-call | tf_op jit(solution)/shard_map/pallas_call | solution.py:36
  4.4 20.4 %all_to_all.35.parts_ref = bf16[16,72,128]{2,1,0:T(8,128)(2,1)S(1)} all-to-all(bf16[16,72,128]{2,1,0:T(8,128)(2,1)} %shard_map.91), channel_id=1, replica_groups=mesh['z'=8,'x'=4,'y'=8,'c'=2] {'c','y'}, dimensions={0} | all-to-all | bytes 589824 | tf_op jit(solution)/shard_map/all_to_all | solution.py:273
  25.2 24.8 %all_to_all.36.attended_ref = bf16[32,64,128]{2,1,0:T(8,128)(2,1)S(1)} all-to-all(bf16[32,64,128]{2,1,0:T(8,128)(2,1)S(1)} %shard_map.92), channel_id=1, replica_groups=mesh['z'=8,'x'=4,'y'=8,'c'=2] {'x','z'}, dimensions={0} | all-to-all | bytes 1048576 | tf_op jit(solution)/shard_map/all_to_all | solution.py:273
  50.0 1.0 shard_map.93
  51.1 8.8 %all-to-all-start.2 = ((bf16[16,64,128]{2,1,0:T(8,128)(2,1)}), bf16[16,64,128]{2,1,0:T(8,128)(2,1)S(1)}, u32[]{:S(2)}, u32[]{:S(2)}) async-start(bf16[16,64,128]{2,1,0:T(8,128)(2,1)} %shard_map.93), calls=%async_computation.2 | async-start | bytes 524288 | tf_op jit(solution)/shard_map/all_to_all | solution.py:273
  60.0 9.3 %all-to-all-done.2.parts_ref = bf16[16,64,128]{2,1,0:T(8,128)(2,1)S(1)} async-done(((bf16[16,64,128]{2,1,0:T(8,128)(2,1)}), bf16[16,64,128]{2,1,0:T(8,128)(2,1)S(1)}, u32[]{:S(2)}, u32[]{:S(2)}) %all-to-all-start.2) | async-done | bytes 262176 | tf_op jit(solution)/shard_map/all_to_all | solution.py:273
  69.4 1.0 copy-done.2
  70.5 8.2 %all-to-all-start.3 = ((bf16[64,72,128]{2,1,0:T(8,128)(2,1)}), bf16[64,72,128]{2,1,0:T(8,128)(2,1)S(1)}, u32[]{:S(2)}, u32[]{:S(2)}) async-start(bf16[64,72,128]{2,1,0:T(8,128)(2,1)} %copy-done.2), calls=%async_computation.3 | async-start | bytes 2359296 | tf_op jit(solution)/shard_map/all_to_all | solution.py:273
  78.9 2.8 %collective-permute-start.2 = (bf16[8,256,128]{2,1,0:T(8,128)(2,1)S(1)}, bf16[8,256,128]{2,1,0:T(8,128)(2,1)S(1)}, u32[]{:S(2)}, u32[]{:S(2)}) collective-permute-start(bf16[8,256,128]{2,1,0:T(8,128)(2,1)S(1)} %get-tuple-element.11), channel_id=1, source_target_pairs={{0,48},{16,0},{32,16},{48,32},{1,49},{17,1},{33,17},{49,33},{2,50}... | collective-permute-start | bytes 1572872 | tf_op jit(solution)/shard_map/ppermute | solution.py:281
  81.6 3.2 %collective-permute-start.1 = (bf16[8,256,128]{2,1,0:T(8,128)(2,1)S(1)}, bf16[8,256,128]{2,1,0:T(8,128)(2,1)S(1)}, u32[]{:S(2)}, u32[]{:S(2)}) collective-permute-start(bf16[8,256,128]{2,1,0:T(8,128)(2,1)S(1)} %get-tuple-element.12), channel_id=1, source_target_pairs={{0,32},{16,48},{32,0},{48,16},{1,33},{17,49},{33,1},{49,17},{2,34}... | collective-permute-start | bytes 1572872 | tf_op jit(solution)/shard_map/ppermute | solution.py:281
  84.8 1.9 %collective-permute-start = (bf16[8,256,128]{2,1,0:T(8,128)(2,1)S(1)}, bf16[8,256,128]{2,1,0:T(8,128)(2,1)S(1)}, u32[]{:S(2)}, u32[]{:S(2)}) collective-permute-start(bf16[8,256,128]{2,1,0:T(8,128)(2,1)S(1)} %get-tuple-element.13), channel_id=1, source_target_pairs={{0,16},{16,32},{32,48},{48,0},{1,17},{17,33},{33,49},{49,1},{2,18}... | collective-permute-start | bytes 1572872 | tf_op jit(solution)/shard_map/ppermute | solution.py:281
  86.8 6.7 %collective-permute-done.2.refs_2_ = bf16[8,256,128]{2,1,0:T(8,128)(2,1)S(1)} collective-permute-done((bf16[8,256,128]{2,1,0:T(8,128)(2,1)S(1)}, bf16[8,256,128]{2,1,0:T(8,128)(2,1)S(1)}, u32[]{:S(2)}, u32[]{:S(2)}) %collective-permute-start.2) | collective-permute-done | bytes 524320 | tf_op jit(solution)/shard_map/ppermute | solution.py:281
  94.3 3.2 %collective-permute-done.1.refs_1_ = bf16[8,256,128]{2,1,0:T(8,128)(2,1)S(1)} collective-permute-done((bf16[8,256,128]{2,1,0:T(8,128)(2,1)S(1)}, bf16[8,256,128]{2,1,0:T(8,128)(2,1)S(1)}, u32[]{:S(2)}, u32[]{:S(2)}) %collective-permute-start.1) | collective-permute-done | bytes 524320 | tf_op jit(solution)/shard_map/ppermute | solution.py:281
  98.2 11.9 %collective-permute-done.refs_0_ = bf16[8,256,128]{2,1,0:T(8,128)(2,1)S(1)} collective-permute-done((bf16[8,256,128]{2,1,0:T(8,128)(2,1)S(1)}, bf16[8,256,128]{2,1,0:T(8,128)(2,1)S(1)}, u32[]{:S(2)}, u32[]{:S(2)}) %collective-permute-start) | collective-permute-done | bytes 524320 | tf_op jit(solution)/shard_map/ppermute | solution.py:281
  110.9 2.6 %collective-permute-start.3 = (bf16[64,72,128]{2,1,0:T(8,128)(2,1)S(1)}, bf16[64,72,128]{2,1,0:T(8,128)(2,1)S(1)}, u32[]{:S(2)}, u32[]{:S(2)}) collective-permute-start(bf16[64,72,128]{2,1,0:T(8,128)(2,1)S(1)} %all-to-all-done.3.mine_ref), channel_id=1, source_target_pairs={{0,1},{1,0},{2,3},{3,2},{4,5},{5,4},{6,7},{7,6},{8,9},{9,8},{10,11... | collective-permute-start | bytes 3538952 | tf_op jit(solution)/shard_map/ppermute | solution.py:317
  113.6 1.0 copy-done.4
  114.6 1.0 copy-done.7
  115.6 1.0 copy-done.10
  116.7 0.8 shard_map.95.near_ref
  118.0 0.8 shard_map.96
  118.9 11.8 %all_to_all.37.parts_ref = bf16[4,528,128]{2,1,0:T(8,128)(2,1)S(1)} all-to-all(bf16[4,528,128]{2,1,0:T(8,128)(2,1)S(1)} %shard_map.96), channel_id=1, replica_groups=mesh['z'=8,'x'=4,'y'=8,'c'=2] {'x'}, dimensions={0} | all-to-all | bytes 1081344 | tf_op jit(solution)/shard_map/all_to_all | solution.py:273
  131.3 14.5 %all_to_all.38.parts_ref = f32[16,8,128]{2,1,0:T(8,128)S(1)} all-to-all(f32[16,8,128]{2,1,0:T(8,128)S(1)} %get-tuple-element.9), channel_id=1, replica_groups=mesh['z'=8,'x'=4,'y'=8,'c'=2] {'c','y'}, dimensions={0} | all-to-all | bytes 131072 | tf_op jit(solution)/shard_map/all_to_all | solution.py:273
  145.8 16.3 %all_to_all.39.parts_ref = f32[32,8,128]{2,1,0:T(8,128)S(1)} all-to-all(f32[32,8,128]{2,1,0:T(8,128)S(1)} %shard_map.98), channel_id=1, replica_groups=mesh['z'=8,'x'=4,'y'=8,'c'=2] {'x','z'}, dimensions={0} | all-to-all | bytes 262144 | tf_op jit(solution)/shard_map/all_to_all | solution.py:273
  162.2 0.9 shard_map.99
  (35 shorter events, 4.4 us)
Async XLA Ops:
  0.0 59.9 %copy-start = (bf16[16,32,256]{2,1,0:T(8,128)(2,1)S(1)}, bf16[16,32,256]{2,1,0:T(8,128)(2,1)}, u32[]{:S(2)}) copy-start(bf16[16,32,256]{2,1,0:T(8,128)(2,1)} %param.14) | copy-start | bytes 786436
  4.4 45.7 %copy-start.12 = (bf16[512,256]{1,0:T(8,128)(2,1)S(1)}, bf16[512,256]{1,0:T(8,128)(2,1)}, u32[]{:S(2)}) copy-start(bf16[512,256]{1,0:T(8,128)(2,1)} %weight_ref.1) | copy-start | bytes 786436
  25.2 44.1 %copy-start.14 = (f32[256]{0:T(256)S(1)}, f32[256]{0:T(256)}, u32[]{:S(2)}) copy-start(f32[256]{0:T(256)} %param.15) | copy-start | bytes 3076
  51.1 18.2 %all-to-all-start.2 = ((bf16[16,64,128]{2,1,0:T(8,128)(2,1)}), bf16[16,64,128]{2,1,0:T(8,128)(2,1)S(1)}, u32[]{:S(2)}, u32[]{:S(2)}) async-start(bf16[16,64,128]{2,1,0:T(8,128)(2,1)} %shard_map.93), calls=%async_computation.2 | async-start | bytes 524288 | tf_op jit(solution)/shard_map/all_to_all | solution.py:273
  69.4 1.0 copy-start.2
  70.5 8.3 %copy-start.1 = (bf16[8192,128]{1,0:T(8,128)(2,1)S(1)}, bf16[8192,128]{1,0:T(8,128)(2,1)}, u32[]{:S(2)}) copy-start(bf16[8192,128]{1,0:T(8,128)(2,1)} %param.16) | copy-start | bytes 6291460
  70.5 40.5 %all-to-all-start.3 = ((bf16[64,72,128]{2,1,0:T(8,128)(2,1)}), bf16[64,72,128]{2,1,0:T(8,128)(2,1)S(1)}, u32[]{:S(2)}, u32[]{:S(2)}) async-start(bf16[64,72,128]{2,1,0:T(8,128)(2,1)} %copy-done.2), calls=%async_computation.3 | async-start | bytes 2359296 | tf_op jit(solution)/shard_map/all_to_all | solution.py:273
  78.9 14.6 %collective-permute-start.2 = (bf16[8,256,128]{2,1,0:T(8,128)(2,1)S(1)}, bf16[8,256,128]{2,1,0:T(8,128)(2,1)S(1)}, u32[]{:S(2)}, u32[]{:S(2)}) collective-permute-start(bf16[8,256,128]{2,1,0:T(8,128)(2,1)S(1)} %get-tuple-element.11), channel_id=1, source_target_pairs={{0,48},{16,0},{32,16},{48,32},{1,49},{17,1},{33,17},{49,33},{2,50}... | collective-permute-start | bytes 1572872 | tf_op jit(solution)/shard_map/ppermute | solution.py:281
  81.6 15.8 %collective-permute-start.1 = (bf16[8,256,128]{2,1,0:T(8,128)(2,1)S(1)}, bf16[8,256,128]{2,1,0:T(8,128)(2,1)S(1)}, u32[]{:S(2)}, u32[]{:S(2)}) collective-permute-start(bf16[8,256,128]{2,1,0:T(8,128)(2,1)S(1)} %get-tuple-element.12), channel_id=1, source_target_pairs={{0,32},{16,48},{32,0},{48,16},{1,33},{17,49},{33,1},{49,17},{2,34}... | collective-permute-start | bytes 1572872 | tf_op jit(solution)/shard_map/ppermute | solution.py:281
  84.8 25.3 %collective-permute-start = (bf16[8,256,128]{2,1,0:T(8,128)(2,1)S(1)}, bf16[8,256,128]{2,1,0:T(8,128)(2,1)S(1)}, u32[]{:S(2)}, u32[]{:S(2)}) collective-permute-start(bf16[8,256,128]{2,1,0:T(8,128)(2,1)S(1)} %get-tuple-element.13), channel_id=1, source_target_pairs={{0,16},{16,32},{32,48},{48,0},{1,17},{17,33},{33,49},{49,1},{2,18}... | collective-permute-start | bytes 1572872 | tf_op jit(solution)/shard_map/ppermute | solution.py:281
  93.5 0.8 copy-start.3
  97.4 0.8 copy-start.6
  110.1 0.8 copy-start.9
  110.9 6.6 %collective-permute-start.3 = (bf16[64,72,128]{2,1,0:T(8,128)(2,1)S(1)}, bf16[64,72,128]{2,1,0:T(8,128)(2,1)S(1)}, u32[]{:S(2)}, u32[]{:S(2)}) collective-permute-start(bf16[64,72,128]{2,1,0:T(8,128)(2,1)S(1)} %all-to-all-done.3.mine_ref), channel_id=1, source_target_pairs={{0,1},{1,0},{2,3},{3,2},{4,5},{5,4},{6,7},{7,6},{8,9},{9,8},{10,11... | collective-permute-start | bytes 3538952 | tf_op jit(solution)/shard_map/ppermute | solution.py:317
  113.6 1.0 copy-start.4
  114.6 1.0 copy-start.7
  115.6 1.0 copy-start.10
  116.7 1.0 copy-start.5
  116.7 1.2 copy-start.8
  116.7 1.4 copy-start.11
  118.9 43.3 %copy-start.13 = (f32[16,128]{1,0:T(8,128)S(1)}, f32[16,128]{1,0:T(8,128)}, u32[]{:S(2)}) copy-start(f32[16,128]{1,0:T(8,128)} %noise_ref.1) | copy-start | bytes 24580

commit v4 on v3

--- a/solution.py
+++ b/solution.py
@@ -115,7 +115,7 @@
             out_ref[NY * half + g, 64:72, :] = stats
 
 
-def combine_kernel(parts_ref, out_ref):
+def combine_kernel(parts_ref, _, out_ref):
     core = lax.axis_index("c")
     stats = parts_ref[:, 64:72, :].astype(F32)
     tops, totals = stats[:, 0, :], stats[:, 1, :] + stats[:, 2, :]
@@ -131,7 +131,7 @@
         out_ref[target] = attended
 
 
-def project_kernel(attended_ref, weight_ref, out_ref):
+def project_kernel(attended_ref, weight_ref, _, out_ref):
     features = jnp.concatenate(
         [attended_ref[:, 16 * r : 16 * r + 16, :].reshape(ROWS, HD) for r in range(4)], axis=1
     )
@@ -144,35 +144,32 @@
             out_ref[NY * c + y] = rows[:, 128 * c : 128 * c + 128]
 
 
-def residual_kernel(parts_ref, resid_ref, gain_ref, out_ref):
-    core = lax.axis_index("c")
-    hidden = resid_ref[...].astype(F32)
+def residual_kernel(parts_ref, resid_ref, _, __, out_ref):
     projected = parts_ref[0].astype(F32)
     for source in range(1, NY * NC):
         projected += parts_ref[source].astype(F32)
-    hidden += projected
-    gain = jnp.where(core == 1, gain_ref[1:2, :], gain_ref[0:1, :])
-    high, low = split_pair(to_row(jnp.sum(hidden * hidden, axis=1, keepdims=True)))
-    stat_row = lax.broadcasted_iota(jnp.int32, (8, 128), 0)
-    stats = jnp.where(stat_row == 0, high, jnp.where(stat_row == 1, low, 0.0)).astype(BF16)
-    scaled = (hidden * gain).astype(BF16)
+    hidden = (resid_ref[...].astype(F32) + projected).astype(BF16)
     for target in range(NZ * NY):
-        out_ref[target, 0:64, :] = scaled
-        out_ref[target, 64:72, :] = stats
-
-
-def gathered(ref):
-    return jnp.concatenate(
-        [
-            jnp.concatenate([ref[NZ * y + z, 0:64, :] for z in range(NZ)], axis=1)
-            for y in range(NY)
-        ],
-        axis=0,
-    )
-
-
-def square_totals(ref):
-    return [sum(ref[NZ * y + z, 64:72, :].astype(F32) for z in range(NZ)) for y in range(NY)]
+        out_ref[target] = hidden
+
+
+def scaled_rows(ref, gains_ref, core):
+    table = jnp.where(core == 1, gains_ref[:, 128:], gains_ref[:, :128])
+    back = lax.rem(
+        lax.axis_index("z") + NZ - lax.broadcasted_iota(jnp.int32, (NZ, 128), 0), NZ
+    )
+    gains = [jnp.sum(jnp.where(back == z, table, 0.0), axis=0, keepdims=True) for z in range(NZ)]
+    rows, squares = [], []
+    for y in range(NY):
+        total = jnp.zeros((64, 128), F32)
+        blocks = []
+        for z in range(NZ):
+            hidden = ref[NZ * y + z].astype(F32)
+            total += hidden * hidden
+            blocks.append((hidden * gains[z]).astype(BF16))
+        rows.append(jnp.concatenate(blocks, axis=1))
+        squares.append(to_row(jnp.sum(total, axis=1, keepdims=True)))
+    return jnp.concatenate(rows, axis=0), jnp.concatenate(squares, axis=0)
 
 
 def head_block(refs, start):
@@ -180,35 +177,31 @@
     return jnp.concatenate([ref[:, rows, :].reshape(NZ * 128, 128) for ref in refs], axis=1)
 
 
-def near_kernel(mine_ref, head_ref, *refs):
-    swapped_refs, (out_ref, block_ref, semaphore) = refs[:3], refs[3:]
+def near_kernel(mine_ref, gains_ref, head_ref, swapped_ref, out_ref, squares_ref, block_ref, semaphore):
     fetch = pltpu.make_async_copy(head_ref.at[:, lax.axis_index("x")], block_ref, semaphore)
     fetch.start()
-    start = lax.axis_index("c") * 128
-    mine = gathered(mine_ref)
+    core = lax.axis_index("c")
+    start = core * 128
+    mine, squares_ref[...] = scaled_rows(mine_ref, gains_ref, core)
     fetch.wait()
-    blocks = (block_ref,) + swapped_refs
+    blocks = [block_ref] + [swapped_ref.at[k] for k in range(NX - 1)]
     for pair in range(NX // 2):
         out_ref[pair] = jnp.dot(
             mine, head_block(blocks[2 * pair : 2 * pair + 2], start), preferred_element_type=F32
         )
 
 
-def far_kernel(mine_ref, other_ref, near_ref, head_ref, *refs):
-    swapped_refs, (out_ref, block_ref, semaphore) = refs[:3], refs[3:]
-    x = lax.axis_index("x")
+def far_kernel(
+    other_ref, gains_ref, near_ref, squares_ref, head_ref, swapped_ref, out_ref, block_ref, semaphore
+):
+    x, core = lax.axis_index("x"), 1 - lax.axis_index("c")
     fetch = pltpu.make_async_copy(head_ref.at[:, x], block_ref, semaphore)
     fetch.start()
-    start = (1 - lax.axis_index("c")) * 128
-    stat_row = lax.broadcasted_iota(jnp.int32, (16, 128), 0)
-    stats = jnp.zeros((16, 128), F32)
-    for y, (mine, other) in enumerate(zip(square_totals(mine_ref), square_totals(other_ref))):
-        high, low = split_pair(jnp.sum(mine + other, axis=0, keepdims=True))
-        stats = jnp.where(stat_row == y, high, jnp.where(stat_row == NY + y, low, stats))
-    stats = stats.astype(BF16)
-    other = gathered(other_ref)
+    start = core * 128
+    other, squares = scaled_rows(other_ref, gains_ref, core)
+    stats = jnp.concatenate(split_pair(squares + squares_ref[...]), axis=0).astype(BF16)
     fetch.wait()
-    blocks = (block_ref,) + swapped_refs
+    blocks = [block_ref] + [swapped_ref.at[k] for k in range(NX - 1)]
     for pair in range(NX // 2):
         partial = near_ref[pair] + jnp.dot(
             other, head_block(blocks[2 * pair : 2 * pair + 2], start), preferred_element_type=F32
@@ -269,6 +262,11 @@
     out_ref[...] = jnp.log(VOCAB * (averaged / PROMPTS)) + noise_ref[...]
 
 
+def shift(array, axis, step):
+    count = lax.axis_size(axis)
+    return lax.ppermute(array, axis, [(i, (i + step) % count) for i in range(count)])
+
+
 def exchange(array, axes):
     return lax.all_to_all(array, axes, 0, 0, tiled=True)
 
@@ -278,13 +276,12 @@
     x = lax.axis_index("x")
     blocks = head.reshape(NZ, NX, 256, 128)
     swapped = [
-        lax.ppermute(
-            lax.dynamic_index_in_dim(blocks, (x + k) % NX, 1, keepdims=False),
-            "x",
-            [(i, (i + k) % NX) for i in range(NX)],
-        )
+        shift(lax.dynamic_index_in_dim(blocks, (x + k) % NX, 1, keepdims=False), "x", k)
         for k in range(1, NX)
     ]
+    gains = [norm_gain.reshape(1, 256)]
+    for step in (1, 2, 4):
+        gains.append(jnp.concatenate([gains[-1], shift(gains[-1], "z", step)]))
     resid_mine = jnp.swapaxes(
         lax.dynamic_slice(resid, (0, 4 * y, 128 * c), (QUERIES, 4, 128)), 0, 1
     ).reshape(64, 128)
@@ -303,32 +300,33 @@
         60,
     )
     parts = exchange(parts, ("c", "y"))
-    attended = call(combine_kernel, shape((NZ * NX, 64, 128)), (parts,))
+    attended = call(combine_kernel, shape((NZ * NX, 64, 128)), (parts, gains[1]), "vw")
     attended = exchange(attended, ("x", "z"))
-    partial = call(project_kernel, shape((NY * NC, 64, 128)), (attended, w_out))
+    partial = call(project_kernel, shape((NY * NC, 64, 128)), (attended, w_out, gains[2]), "vvw")
     partial = exchange(partial, ("c", "y"))
     hidden = call(
         residual_kernel,
-        shape((NZ * NY, 72, 128)),
-        (partial, resid_mine, norm_gain.reshape(2, 128)),
+        shape((NZ * NY, 64, 128)),
+        (partial, resid_mine, swapped[1], gains[3]),
+        "vvww",
     )
     mine = exchange(hidden, ("y", "z"))
-    mine, *_ = lax.optimization_barrier((mine, *swapped))
-    other = lax.ppermute(mine, "c", [(0, 1), (1, 0)])
+    mine, swapped = lax.optimization_barrier((mine, jnp.stack(swapped)))
+    other = shift(mine, "c", 1)
     scratch = (pltpu.VMEM((NZ, 256, 128), BF16), pltpu.SemaphoreType.DMA)
-    near = call(
+    near, squares = call(
         near_kernel,
-        shape((NX // 2, ROWS, 256), F32),
-        (mine, blocks, *swapped),
-        "vavvv",
+        (shape((NX // 2, ROWS, 256), F32), shape((NY, 128), F32)),
+        (mine, gains[3], blocks, swapped),
+        "vvav",
         scratch,
         12,
     )
     logits = call(
         far_kernel,
         shape((NX, ROWS + 16, 128)),
-        (mine, other, near, blocks, *swapped),
-        "vvvavvv",
+        (other, gains[3], near, squares, blocks, swapped),
+        "vvvvav",
         scratch,
         12,
     )

time: 164 us -> 158 us (0.963)
  blocking collectives: 87.8 us -> 37.3 us
  starting transfers between devices: 27.5 us -> 64.4 us
  waiting for transfers between devices: 31 us -> 36.2 us
  other arithmetic: 0 us -> 3.09 us
  local copies, waits for them, and re-layouts: 7.34 us -> 4.36 us
  Pallas kernels: 8.45 us -> 10.2 us
    all_to_all x5 -> x3, blocking collectives: 87.8 us -> 37.3 us  [exchange(): return lax.all_to_all(array, axes, 0, 0, tiled=True)]
    all_to_all x2 -> x4, starting transfers between devices: 17 us -> 38.2 us  [exchange(): return lax.all_to_all(array, axes, 0, 0, tiled=True)]
    ppermute x4 -> x7, starting transfers between devices: 10.5 us -> 26.1 us  [shift(): lax.ppermute(array, axis, [(i, (i + step) % count) for i in range(count)])]
    ppermute x4 -> x7, waiting for transfers between devices: 21.8 us -> 27.6 us  [shift(): lax.ppermute(array, axis, [(i, (i + step) % count) for i in range(count)])]
    unnamed x30 -> x16, local copies, waits for them, and re-layouts: 7.09 us -> 3.08 us
    another operation x0 -> x1, other arithmetic: none -> 2.38 us  [on_device(): mine, swapped = lax.optimization_barrier((mine, jnp.stack(swapped)))]
    pallas_call x9, Pallas kernels: 8.45 us -> 10.2 us  [call(): pl.pallas_call(body, out_shape=out_shape, in_specs=[kinds[s] for s in spa...]
    all_to_all x2 -> x4, waiting for transfers between devices: 9.27 us -> 8.56 us  [exchange(): return lax.all_to_all(array, axes, 0, 0, tiled=True)]
  transfers between devices with their start and end apart: 6 -> 11, of which waited for: 4 -> 8; matrix products, arithmetic and copies ran while one was open for 0% -> 3% of each run, Pallas kernels for 1% -> 1%
where the time goes in v4:
time: 158 us; the launch traced here: 156 us
  starting transfers between devices  64.4 us (41%)
  blocking collectives  37.3 us (24%)
  waiting for transfers between devices  36.2 us (23%)
  Pallas kernels  10.2 us (6%)
  local copies, waits for them, and re-layouts  4.36 us (3%)
  other arithmetic  3.09 us (2%)
    all_to_all x4, starting transfers between devices, exchange(): return lax.all_to_all(array, axes, 0, 0, tiled=True)  38.2 us
    all_to_all x3, blocking collectives, exchange(): return lax.all_to_all(array, axes, 0, 0, tiled=True)  37.3 us
    ppermute x7, waiting for transfers between devices, shift(): lax.ppermute(array, axis, [(i, (i + step) % count) for i in range(count)])  27.6 us
    ppermute x7, starting transfers between devices, shift(): lax.ppermute(array, axis, [(i, (i + step) % count) for i in range(count)])  26.1 us
    pallas_call x9, Pallas kernels, call(): pl.pallas_call(body, out_shape=out_shape, in_specs=[kinds[s] for s in spa...  10.2 us
    all_to_all x4, waiting for transfers between devices, exchange(): return lax.all_to_all(array, axes, 0, 0, tiled=True)  8.56 us
  transfers between devices with their start and end apart: 11, of which 8 were waited for; matrix products, arithmetic and copies ran while one was open for 3% of the time, Pallas kernels for 1%

profile of v4, /device:TPU:1, one launch (start us, length us, event | category | flops | bytes accessed | tf_op | source)
XLA Modules:
  0.0 156.4 jit_solution(1431422070428275763)
XLA Ops:
  0.7 3.8 %shard_map.91 = bf16[16,72,128]{2,1,0:T(8,128)(2,1)} custom-call(s32[1]{0:T(128)S(6)} %copy.11.length_ref, bf16[16,8192]{1,0:T(8,128)(2,1)} %bitcast.24, bf16[2,16,1024]{2,1,0:T(8,128)(2,1)} %bitcast.26, bf16[2,64,1024]{2,1,0:T(8,128)(2,1)} %bitcast.25), custom_call_target="tpu_custom_call" | custom-call | tf_op jit(solution)/shard_map/pallas_call | solution.py:36
  4.5 10.3 %all-to-all-start = ((bf16[16,72,128]{2,1,0:T(8,128)(2,1)}), bf16[16,72,128]{2,1,0:T(8,128)(2,1)S(1)}, u32[]{:S(2)}, u32[]{:S(2)}) async-start(bf16[16,72,128]{2,1,0:T(8,128)(2,1)} %shard_map.91), calls=%async_computation | async-start | bytes 589824 | tf_op jit(solution)/shard_map/all_to_all | solution.py:271
  14.8 2.4 %collective-permute-start = (f32[1,256]{1,0:T(1,128)}, f32[1,256]{1,0:T(1,128)S(1)}, u32[]{:S(2)}, u32[]{:S(2)}) collective-permute-start(f32[1,256]{1,0:T(1,128)} %bitcast.27), channel_id=1, source_target_pairs={{0,64},{64,128},{128,192},{192,256},{256,320},{320,384},{384,448},... | collective-permute-start | bytes 3080 | tf_op jit(solution)/shard_map/ppermute | solution.py:267
  17.2 8.1 %collective-permute-done = f32[1,256]{1,0:T(1,128)S(1)} collective-permute-done((f32[1,256]{1,0:T(1,128)}, f32[1,256]{1,0:T(1,128)S(1)}, u32[]{:S(2)}, u32[]{:S(2)}) %collective-permute-start) | collective-permute-done | bytes 1056 | tf_op jit(solution)/shard_map/ppermute | solution.py:267
  27.2 10.1 %all-to-all-start.1 = ((bf16[32,64,128]{2,1,0:T(8,128)(2,1)}), bf16[32,64,128]{2,1,0:T(8,128)(2,1)S(1)}, u32[]{:S(2)}, u32[]{:S(2)}) async-start(bf16[32,64,128]{2,1,0:T(8,128)(2,1)} %shard_map.92), calls=%async_computation.1 | async-start | bytes 1048576 | tf_op jit(solution)/shard_map/all_to_all | solution.py:271
  37.4 4.0 %collective-permute-start.1 = (f32[2,256]{1,0:T(2,128)S(1)}, f32[2,256]{1,0:T(2,128)S(1)}, u32[]{:S(2)}, u32[]{:S(2)}) collective-permute-start(f32[2,256]{1,0:T(2,128)S(1)} %pad_maximum_fusion.3._), channel_id=1, source_target_pairs={{0,128},{64,192},{128,256},{192,320},{256,384},{320,448},{384,0},{... | collective-permute-start | bytes 6152 | tf_op jit(solution)/shard_map/ppermute | solution.py:267
  42.6 4.6 %collective-permute-start.2 = (bf16[8,256,128]{2,1,0:T(8,128)(2,1)}, bf16[8,256,128]{2,1,0:T(8,128)(2,1)S(1)}, u32[]{:S(2)}, u32[]{:S(2)}) collective-permute-start(bf16[8,256,128]{2,1,0:T(8,128)(2,1)} %get-tuple-element.19), channel_id=1, source_target_pairs={{0,32},{16,48},{32,0},{48,16},{1,33},{17,49},{33,1},{49,17},{2,34}... | collective-permute-start | bytes 1572872 | tf_op jit(solution)/shard_map/ppermute | solution.py:267
  47.2 2.6 %collective-permute-done.1 = f32[2,256]{1,0:T(2,128)S(1)} collective-permute-done((f32[2,256]{1,0:T(2,128)S(1)}, f32[2,256]{1,0:T(2,128)S(1)}, u32[]{:S(2)}, u32[]{:S(2)}) %collective-permute-start.1) | collective-permute-done | bytes 2080 | tf_op jit(solution)/shard_map/ppermute | solution.py:267
  49.8 1.3 all-to-all-done.1.attended_ref
  53.1 9.1 %all-to-all-start.2 = ((bf16[16,64,128]{2,1,0:T(8,128)(2,1)}), bf16[16,64,128]{2,1,0:T(8,128)(2,1)S(1)}, u32[]{:S(2)}, u32[]{:S(2)}) async-start(bf16[16,64,128]{2,1,0:T(8,128)(2,1)} %copy-done.4), calls=%async_computation.2 | async-start | bytes 524288 | tf_op jit(solution)/shard_map/all_to_all | solution.py:271
  62.2 3.9 %collective-permute-start.3 = (f32[4,256]{1,0:T(4,128)S(1)}, f32[4,256]{1,0:T(4,128)S(1)}, u32[]{:S(2)}, u32[]{:S(2)}) collective-permute-start(f32[4,256]{1,0:T(4,128)S(1)} %pad_maximum_fusion.2._), channel_id=1, source_target_pairs={{0,256},{64,320},{128,384},{192,448},{256,0},{320,64},{384,128},{4... | collective-permute-start | bytes 12296 | tf_op jit(solution)/shard_map/ppermute | solution.py:267
  66.3 4.5 %collective-permute-done.3 = f32[4,256]{1,0:T(4,128)S(1)} collective-permute-done((f32[4,256]{1,0:T(4,128)S(1)}, f32[4,256]{1,0:T(4,128)S(1)}, u32[]{:S(2)}, u32[]{:S(2)}) %collective-permute-start.3) | collective-permute-done | bytes 4128 | tf_op jit(solution)/shard_map/ppermute | solution.py:267
  72.7 8.8 %all-to-all-start.3 = ((bf16[64,64,128]{2,1,0:T(8,128)(2,1)}), bf16[64,64,128]{2,1,0:T(8,128)(2,1)S(1)}, u32[]{:S(2)}, u32[]{:S(2)}) async-start(bf16[64,64,128]{2,1,0:T(8,128)(2,1)} %shard_map.94), calls=%async_computation.3 | async-start | bytes 2097152 | tf_op jit(solution)/shard_map/all_to_all | solution.py:271
  81.5 3.0 %collective-permute-start.5 = (bf16[8,256,128]{2,1,0:T(8,128)(2,1)}, bf16[8,256,128]{2,1,0:T(8,128)(2,1)S(1)}, u32[]{:S(2)}, u32[]{:S(2)}) collective-permute-start(bf16[8,256,128]{2,1,0:T(8,128)(2,1)} %get-tuple-element.18), channel_id=1, source_target_pairs={{0,48},{16,0},{32,16},{48,32},{1,49},{17,1},{33,17},{49,33},{2,50}... | collective-permute-start | bytes 1572872 | tf_op jit(solution)/shard_map/ppermute | solution.py:267
  84.5 2.3 %collective-permute-start.4 = (bf16[8,256,128]{2,1,0:T(8,128)(2,1)}, bf16[8,256,128]{2,1,0:T(8,128)(2,1)S(1)}, u32[]{:S(2)}, u32[]{:S(2)}) collective-permute-start(bf16[8,256,128]{2,1,0:T(8,128)(2,1)} %get-tuple-element.17), channel_id=1, source_target_pairs={{0,16},{16,32},{32,48},{48,0},{1,17},{17,33},{33,49},{49,1},{2,18}... | collective-permute-start | bytes 1572872 | tf_op jit(solution)/shard_map/ppermute | solution.py:267
  86.8 8.4 %collective-permute-done.5 = bf16[8,256,128]{2,1,0:T(8,128)(2,1)S(1)} collective-permute-done((bf16[8,256,128]{2,1,0:T(8,128)(2,1)}, bf16[8,256,128]{2,1,0:T(8,128)(2,1)S(1)}, u32[]{:S(2)}, u32[]{:S(2)}) %collective-permute-start.5) | collective-permute-done | bytes 524320 | tf_op jit(solution)/shard_map/ppermute | solution.py:267
  95.2 4.0 %collective-permute-done.4 = bf16[8,256,128]{2,1,0:T(8,128)(2,1)S(1)} collective-permute-done((bf16[8,256,128]{2,1,0:T(8,128)(2,1)}, bf16[8,256,128]{2,1,0:T(8,128)(2,1)S(1)}, u32[]{:S(2)}, u32[]{:S(2)}) %collective-permute-start.4) | collective-permute-done | bytes 524320 | tf_op jit(solution)/shard_map/ppermute | solution.py:267
  99.2 2.4 %pad_maximum_fusion.swapped_ref = bf16[3,8,256,128]{3,2,1,0:T(8,128)(2,1)} fusion(bf16[1,8,256,128]{3,2,1,0:T(8,128)(2,1)S(1)} %bitcast.22, bf16[1,8,256,128]{3,2,1,0:T(8,128)(2,1)} %bitcast.20, bf16[1,8,256,128]{3,2,1,0:T(8,128)(2,1)S(1)} %bitcast.23), kind=kLoop, calls=%fused_computation | loop fusion | flops 1572864 | bytes 3145728 | tf_op jit(solution)/shard_map/stack | solution.py:314
  101.6 6.5 %all-to-all-done.3.mine_ref = bf16[64,64,128]{2,1,0:T(8,128)(2,1)S(1)} async-done(((bf16[64,64,128]{2,1,0:T(8,128)(2,1)}), bf16[64,64,128]{2,1,0:T(8,128)(2,1)S(1)}, u32[]{:S(2)}, u32[]{:S(2)}) %all-to-all-start.3) | async-done | bytes 1048608 | tf_op jit(solution)/shard_map/all_to_all | solution.py:271
  108.0 5.9 %collective-permute-start.6 = (bf16[64,64,128]{2,1,0:T(8,128)(2,1)S(1)}, bf16[64,64,128]{2,1,0:T(8,128)(2,1)S(1)}, u32[]{:S(2)}, u32[]{:S(2)}) collective-permute-start(bf16[64,64,128]{2,1,0:T(8,128)(2,1)S(1)} %all-to-all-done.3.mine_ref), channel_id=1, source_target_pairs={{0,1},{1,0},{2,3},{3,2},{4,5},{5,4},{6,7},{7,6},{8,9},{9,8},{10,11... | collective-permute-start | bytes 3145736 | tf_op jit(solution)/shard_map/ppermute | solution.py:267
  114.0 1.4 copy-done.2
  117.6 11.7 %all_to_all.35.parts_ref = bf16[4,528,128]{2,1,0:T(8,128)(2,1)S(1)} all-to-all(bf16[4,528,128]{2,1,0:T(8,128)(2,1)S(1)} %shard_map.96), channel_id=1, replica_groups=mesh['z'=8,'x'=4,'y'=8,'c'=2] {'x'}, dimensions={0} | all-to-all | bytes 1081344 | tf_op jit(solution)/shard_map/all_to_all | solution.py:271
  129.9 13.2 %all_to_all.36.parts_ref = f32[16,8,128]{2,1,0:T(8,128)S(1)} all-to-all(f32[16,8,128]{2,1,0:T(8,128)S(1)} %get-tuple-element.15), channel_id=1, replica_groups=mesh['z'=8,'x'=4,'y'=8,'c'=2] {'c','y'}, dimensions={0} | all-to-all | bytes 131072 | tf_op jit(solution)/shard_map/all_to_all | solution.py:271
  143.1 12.5 %all_to_all.37.parts_ref = f32[32,8,128]{2,1,0:T(8,128)S(1)} all-to-all(f32[32,8,128]{2,1,0:T(8,128)S(1)} %shard_map.98), channel_id=1, replica_groups=mesh['z'=8,'x'=4,'y'=8,'c'=2] {'x','z'}, dimensions={0} | all-to-all | bytes 262144 | tf_op jit(solution)/shard_map/all_to_all | solution.py:271
  (33 shorter events, 10.8 us)
Async XLA Ops:
  0.0 66.1 %copy-start = (bf16[16,32,256]{2,1,0:T(8,128)(2,1)S(1)}, bf16[16,32,256]{2,1,0:T(8,128)(2,1)}, u32[]{:S(2)}) copy-start(bf16[16,32,256]{2,1,0:T(8,128)(2,1)} %param.14) | copy-start | bytes 786436
  0.7 40.7 %copy-start.1 = (bf16[8192,128]{1,0:T(8,128)(2,1)S(1)}, bf16[8192,128]{1,0:T(8,128)(2,1)}, u32[]{:S(2)}) copy-start(bf16[8192,128]{1,0:T(8,128)(2,1)} %param.16) | copy-start | bytes 6291460
  4.5 21.4 %all-to-all-start = ((bf16[16,72,128]{2,1,0:T(8,128)(2,1)}), bf16[16,72,128]{2,1,0:T(8,128)(2,1)S(1)}, u32[]{:S(2)}, u32[]{:S(2)}) async-start(bf16[16,72,128]{2,1,0:T(8,128)(2,1)} %shard_map.91), calls=%async_computation | async-start | bytes 589824 | tf_op jit(solution)/shard_map/all_to_all | solution.py:271
  14.8 10.5 %collective-permute-start = (f32[1,256]{1,0:T(1,128)}, f32[1,256]{1,0:T(1,128)S(1)}, u32[]{:S(2)}, u32[]{:S(2)}) collective-permute-start(f32[1,256]{1,0:T(1,128)} %bitcast.27), channel_id=1, source_target_pairs={{0,64},{64,128},{128,192},{192,256},{256,320},{320,384},{384,448},... | collective-permute-start | bytes 3080 | tf_op jit(solution)/shard_map/ppermute | solution.py:267
  27.2 23.9 %all-to-all-start.1 = ((bf16[32,64,128]{2,1,0:T(8,128)(2,1)}), bf16[32,64,128]{2,1,0:T(8,128)(2,1)S(1)}, u32[]{:S(2)}, u32[]{:S(2)}) async-start(bf16[32,64,128]{2,1,0:T(8,128)(2,1)} %shard_map.92), calls=%async_computation.1 | async-start | bytes 1048576 | tf_op jit(solution)/shard_map/all_to_all | solution.py:271
  37.4 12.4 %collective-permute-start.1 = (f32[2,256]{1,0:T(2,128)S(1)}, f32[2,256]{1,0:T(2,128)S(1)}, u32[]{:S(2)}, u32[]{:S(2)}) collective-permute-start(f32[2,256]{1,0:T(2,128)S(1)} %pad_maximum_fusion.3._), channel_id=1, source_target_pairs={{0,128},{64,192},{128,256},{192,320},{256,384},{320,448},{384,0},{... | collective-permute-start | bytes 6152 | tf_op jit(solution)/shard_map/ppermute | solution.py:267
  41.4 8.4 %copy-start.7 = (f32[256]{0:T(256)S(1)}, f32[256]{0:T(256)}, u32[]{:S(2)}) copy-start(f32[256]{0:T(256)} %param.15) | copy-start | bytes 3076
  42.6 28.2 %collective-permute-start.2 = (bf16[8,256,128]{2,1,0:T(8,128)(2,1)}, bf16[8,256,128]{2,1,0:T(8,128)(2,1)S(1)}, u32[]{:S(2)}, u32[]{:S(2)}) collective-permute-start(bf16[8,256,128]{2,1,0:T(8,128)(2,1)} %get-tuple-element.19), channel_id=1, source_target_pairs={{0,32},{16,48},{32,0},{48,16},{1,33},{17,49},{33,1},{49,17},{2,34}... | collective-permute-start | bytes 1572872 | tf_op jit(solution)/shard_map/ppermute | solution.py:267
  51.1 1.0 copy-start.5
  52.4 0.7 copy-start.4
  53.1 18.5 %all-to-all-start.2 = ((bf16[16,64,128]{2,1,0:T(8,128)(2,1)}), bf16[16,64,128]{2,1,0:T(8,128)(2,1)S(1)}, u32[]{:S(2)}, u32[]{:S(2)}) async-start(bf16[16,64,128]{2,1,0:T(8,128)(2,1)} %copy-done.4), calls=%async_computation.2 | async-start | bytes 524288 | tf_op jit(solution)/shard_map/all_to_all | solution.py:271
  62.2 8.6 %collective-permute-start.3 = (f32[4,256]{1,0:T(4,128)S(1)}, f32[4,256]{1,0:T(4,128)S(1)}, u32[]{:S(2)}, u32[]{:S(2)}) collective-permute-start(f32[4,256]{1,0:T(4,128)S(1)} %pad_maximum_fusion.2._), channel_id=1, source_target_pairs={{0,256},{64,320},{128,384},{192,448},{256,0},{320,64},{384,128},{4... | collective-permute-start | bytes 12296 | tf_op jit(solution)/shard_map/ppermute | solution.py:267
  70.8 1.9 %copy-start.3 = (bf16[8,256,128]{2,1,0:T(8,128)(2,1)}, bf16[8,256,128]{2,1,0:T(8,128)(2,1)S(1)}, u32[]{:S(2)}) copy-start(bf16[8,256,128]{2,1,0:T(8,128)(2,1)S(1)} %collective-permute-done.2._) | copy-start | bytes 1572868
  72.7 35.3 %all-to-all-start.3 = ((bf16[64,64,128]{2,1,0:T(8,128)(2,1)}), bf16[64,64,128]{2,1,0:T(8,128)(2,1)S(1)}, u32[]{:S(2)}, u32[]{:S(2)}) async-start(bf16[64,64,128]{2,1,0:T(8,128)(2,1)} %shard_map.94), calls=%async_computation.3 | async-start | bytes 2097152 | tf_op jit(solution)/shard_map/all_to_all | solution.py:271
  81.5 13.7 %collective-permute-start.5 = (bf16[8,256,128]{2,1,0:T(8,128)(2,1)}, bf16[8,256,128]{2,1,0:T(8,128)(2,1)S(1)}, u32[]{:S(2)}, u32[]{:S(2)}) collective-permute-start(bf16[8,256,128]{2,1,0:T(8,128)(2,1)} %get-tuple-element.18), channel_id=1, source_target_pairs={{0,48},{16,0},{32,16},{48,32},{1,49},{17,1},{33,17},{49,33},{2,50}... | collective-permute-start | bytes 1572872 | tf_op jit(solution)/shard_map/ppermute | solution.py:267
  84.5 14.7 %collective-permute-start.4 = (bf16[8,256,128]{2,1,0:T(8,128)(2,1)}, bf16[8,256,128]{2,1,0:T(8,128)(2,1)S(1)}, u32[]{:S(2)}, u32[]{:S(2)}) collective-permute-start(bf16[8,256,128]{2,1,0:T(8,128)(2,1)} %get-tuple-element.17), channel_id=1, source_target_pairs={{0,16},{16,32},{32,48},{48,0},{1,17},{17,33},{33,49},{49,1},{2,18}... | collective-permute-start | bytes 1572872 | tf_op jit(solution)/shard_map/ppermute | solution.py:267
  108.0 8.4 %collective-permute-start.6 = (bf16[64,64,128]{2,1,0:T(8,128)(2,1)S(1)}, bf16[64,64,128]{2,1,0:T(8,128)(2,1)S(1)}, u32[]{:S(2)}, u32[]{:S(2)}) collective-permute-start(bf16[64,64,128]{2,1,0:T(8,128)(2,1)S(1)} %all-to-all-done.3.mine_ref), channel_id=1, source_target_pairs={{0,1},{1,0},{2,3},{3,2},{4,5},{5,4},{6,7},{7,6},{8,9},{9,8},{10,11... | collective-permute-start | bytes 3145736 | tf_op jit(solution)/shard_map/ppermute | solution.py:267
  114.0 1.4 copy-start.2
  117.6 38.0 %copy-start.6 = (f32[16,128]{1,0:T(8,128)S(1)}, f32[16,128]{1,0:T(8,128)}, u32[]{:S(2)}) copy-start(f32[16,128]{1,0:T(8,128)} %noise_ref.1) | copy-start | bytes 24580

commit v5 on v4

--- a/solution.py
+++ b/solution.py
@@ -7,7 +7,8 @@
 from jax.sharding import PartitionSpec as P
 
 NZ, NX, NY, NC = 8, 4, 8, 2
-MEMBER = ("z", "x")
+X = ("far", "near")
+MEMBER = ("z",) + X
 TENSOR = ("y", "c")
 
 D = 8192
@@ -41,6 +42,10 @@
         scratch_shapes=scratch,
         compiler_params=pltpu.CompilerParams(vmem_limit_bytes=mebibytes * 2**20),
     )(*operands)
+
+
+def x_index():
+    return 2 * lax.axis_index("far") + lax.axis_index("near")
 
 
 def shape(dims, dtype=BF16):
@@ -84,7 +89,7 @@
     valid = ((row < CACHE_ROWS) & (row < valid_rows)) | (
         (row >= own_from) & (row - CACHE_ROWS == lane % QUERIES)
     )
-    stat_row = lax.broadcasted_iota(jnp.int32, (8, 128), 0)
+    stat_row = lax.broadcasted_iota(jnp.int32, (16, 128), 0)
     for copy in copies:
         copy.wait()
     for g in range(KVH):
@@ -112,12 +117,12 @@
         ).astype(BF16)
         for half in range(2):
             out_ref[NY * half + g, 0:64, :] = totals[64 * half : 64 * half + 64]
-            out_ref[NY * half + g, 64:72, :] = stats
-
-
-def combine_kernel(parts_ref, _, out_ref):
+            out_ref[NY * half + g, 64:80, :] = stats
+
+
+def combine_kernel(parts_ref, _, __, out_ref):
     core = lax.axis_index("c")
-    stats = parts_ref[:, 64:72, :].astype(F32)
+    stats = parts_ref[:, 64:80, :].astype(F32)
     tops, totals = stats[:, 0, :], stats[:, 1, :] + stats[:, 2, :]
     weight = jnp.exp(tops - jnp.max(tops, axis=0, keepdims=True))
     scale = weight / jnp.sum(weight * totals, axis=0, keepdims=True)
@@ -127,27 +132,37 @@
     for source in range(NY * NC):
         attended += scale[:, source : source + 1] * parts_ref[source, 0:64, :].astype(F32)
     attended = attended.astype(BF16)
-    for target in range(NZ * NX):
+    for target in range(2 * NZ):
         out_ref[target] = attended
 
 
-def project_kernel(attended_ref, weight_ref, _, out_ref):
+def project_kernel(attended_ref, mine_ref, other_ref, out_ref):
     features = jnp.concatenate(
-        [attended_ref[:, 16 * r : 16 * r + 16, :].reshape(ROWS, HD) for r in range(4)], axis=1
-    )
-    partial = jnp.dot(features, weight_ref[...], preferred_element_type=F32).astype(BF16)
-    for y in range(NY):
-        rows = jnp.concatenate(
-            [partial[16 * (NZ * x + y) : 16 * (NZ * x + y) + 16] for x in range(NX)], axis=0
-        )
-        for c in range(NC):
-            out_ref[NY * c + y] = rows[:, 128 * c : 128 * c + 128]
+        [attended_ref[:, 16 * r : 16 * r + 16, :].reshape(ROWS // 2, HD) for r in range(4)], axis=1
+    )
+    near = lax.axis_index("near")
+    for target, weight_ref in ((near, mine_ref), (1 - near, other_ref)):
+        partial = jnp.dot(features, weight_ref[...], preferred_element_type=F32).astype(BF16)
+        for y in range(NY):
+            rows = jnp.concatenate(
+                [partial[16 * (NZ * far + y) : 16 * (NZ * far + y) + 16] for far in range(2)],
+                axis=0,
+            )
+            for c in range(NC):
+                index = NC * NY * target + NY * c + y
+                out_ref[index] = rows[:, 128 * c : 128 * c + 128]
 
 
 def residual_kernel(parts_ref, resid_ref, _, __, out_ref):
-    projected = parts_ref[0].astype(F32)
-    for source in range(1, NY * NC):
-        projected += parts_ref[source].astype(F32)
+    sums = []
+    for near in range(2):
+        total = parts_ref[NC * NY * near].astype(F32)
+        for source in range(1, NC * NY):
+            total += parts_ref[NC * NY * near + source].astype(F32)
+        sums.append(total)
+    projected = jnp.concatenate(
+        [sums[x % 2][16 * (x // 2) : 16 * (x // 2) + 16] for x in range(NX)], axis=0
+    )
     hidden = (resid_ref[...].astype(F32) + projected).astype(BF16)
     for target in range(NZ * NY):
         out_ref[target] = hidden
@@ -178,7 +193,7 @@
 
 
 def near_kernel(mine_ref, gains_ref, head_ref, swapped_ref, out_ref, squares_ref, block_ref, semaphore):
-    fetch = pltpu.make_async_copy(head_ref.at[:, lax.axis_index("x")], block_ref, semaphore)
+    fetch = pltpu.make_async_copy(head_ref.at[:, x_index()], block_ref, semaphore)
     fetch.start()
     core = lax.axis_index("c")
     start = core * 128
@@ -194,7 +209,7 @@
 def far_kernel(
     other_ref, gains_ref, near_ref, squares_ref, head_ref, swapped_ref, out_ref, block_ref, semaphore
 ):
-    x, core = lax.axis_index("x"), 1 - lax.axis_index("c")
+    x, core = x_index(), 1 - lax.axis_index("c")
     fetch = pltpu.make_async_copy(head_ref.at[:, x], block_ref, semaphore)
     fetch.start()
     start = core * 128
@@ -273,22 +288,24 @@
 
 def on_device(query, new_kv, cache, lengths, w_out, resid, norm_gain, head, noise):
     y, c = lax.axis_index("y"), lax.axis_index("c")
-    x = lax.axis_index("x")
+    x = x_index()
     blocks = head.reshape(NZ, NX, 256, 128)
     swapped = [
-        shift(lax.dynamic_index_in_dim(blocks, (x + k) % NX, 1, keepdims=False), "x", k)
+        shift(lax.dynamic_index_in_dim(blocks, (x + k) % NX, 1, keepdims=False), X, k)
         for k in range(1, NX)
     ]
-    gains = [norm_gain.reshape(1, 256)]
+    gains, arrived = norm_gain.reshape(1, 256), []
     for step in (1, 2, 4):
-        gains.append(jnp.concatenate([gains[-1], shift(gains[-1], "z", step)]))
+        arrived.append(shift(gains, "z", step))
+        gains = jnp.concatenate([gains, arrived[-1]])
     resid_mine = jnp.swapaxes(
         lax.dynamic_slice(resid, (0, 4 * y, 128 * c), (QUERIES, 4, 128)), 0, 1
     ).reshape(64, 128)
 
+    other_w = shift(w_out, "near", 1)
     parts = call(
         attend_kernel,
-        shape((NY * NC, 72, 128)),
+        shape((NY * NC, 80, 128)),
         (lengths, query[:, 0, :], new_kv[:, :, 0, :], cache[:, 0]),
         "saaa",
         (
@@ -300,24 +317,28 @@
         60,
     )
     parts = exchange(parts, ("c", "y"))
-    attended = call(combine_kernel, shape((NZ * NX, 64, 128)), (parts, gains[1]), "vw")
-    attended = exchange(attended, ("x", "z"))
-    partial = call(project_kernel, shape((NY * NC, 64, 128)), (attended, w_out, gains[2]), "vvw")
-    partial = exchange(partial, ("c", "y"))
+    attended = call(combine_kernel, shape((2 * NZ, 64, 128)), (parts, arrived[0], other_w), "vww")
+    attended = exchange(attended, ("far", "z"))
+    partial = call(
+        project_kernel,
+        shape((2 * NC * NY, 32, 128)),
+        (attended, w_out, other_w),
+    )
+    partial = exchange(partial, ("near", "c", "y"))
     hidden = call(
         residual_kernel,
         shape((NZ * NY, 64, 128)),
-        (partial, resid_mine, swapped[1], gains[3]),
+        (partial, resid_mine, swapped[1], arrived[1]),
         "vvww",
     )
     mine = exchange(hidden, ("y", "z"))
-    mine, swapped = lax.optimization_barrier((mine, jnp.stack(swapped)))
+    mine, gains, swapped = lax.optimization_barrier((mine, gains, jnp.stack(swapped)))
     other = shift(mine, "c", 1)
     scratch = (pltpu.VMEM((NZ, 256, 128), BF16), pltpu.SemaphoreType.DMA)
     near, squares = call(
         near_kernel,
         (shape((NX // 2, ROWS, 256), F32), shape((NY, 128), F32)),
-        (mine, gains[3], blocks, swapped),
+        (mine, gains, blocks, swapped),
         "vvav",
         scratch,
         12,
@@ -325,23 +346,23 @@
     logits = call(
         far_kernel,
         shape((NX, ROWS + 16, 128)),
-        (other, gains[3], near, squares, blocks, swapped),
+        (other, gains, near, squares, blocks, swapped),
         "vvvvav",
         scratch,
         12,
     )
-    logits = exchange(logits, ("x",))
+    logits = exchange(logits, X)
     logits, stats = call(
         logit_kernel, (shape((ROWS, 128), F32), shape((NY * NC, 8, 128), F32)), (logits,)
     )
     stats = exchange(stats, ("c", "y"))
     stats = call(merge_kernel, shape((NZ * NX, 8, 128), F32), (stats,))
-    stats = exchange(stats, ("x", "z"))
+    stats = exchange(stats, X + ("z",))
     return call(vote_kernel, shape((QUERIES, 128), F32), (stats, logits, noise))
 
 
 def solution(mesh):
-    torus = Mesh(mesh.devices.reshape(NZ, NX, NY, NC), MEMBER + TENSOR)
+    torus = Mesh(mesh.devices.reshape(NZ, 2, 2, NY, NC), MEMBER + TENSOR)
     placed = (
         P(None, MEMBER, None),
         P(None, None, MEMBER, None),

time: 158 us -> 155 us (0.981)
  waiting for transfers between devices: 36.2 us -> 30.6 us
  blocking collectives: 37.3 us -> 39.9 us
    ppermute x7 -> x8, waiting for transfers between devices: 27.6 us -> 15.7 us  [shift(): lax.ppermute(array, axis, [(i, (i + step) % count) for i in range(count)])]
    all_to_all x4, waiting for transfers between devices: 8.56 us -> 14.9 us  [exchange(): return lax.all_to_all(array, axes, 0, 0, tiled=True)]
    ppermute x7 -> x8, starting transfers between devices: 26.1 us -> 31.2 us  [shift(): lax.ppermute(array, axis, [(i, (i + step) % count) for i in range(count)])]
    all_to_all x4, starting transfers between devices: 38.2 us -> 34.8 us  [exchange(): return lax.all_to_all(array, axes, 0, 0, tiled=True)]
    all_to_all x3, blocking collectives: 37.3 us -> 39.9 us  [exchange(): return lax.all_to_all(array, axes, 0, 0, tiled=True)]
  transfers between devices with their start and end apart: 11 -> 12, of which waited for: 8 -> 7; matrix products, arithmetic and copies ran while one was open for 3% -> 2% of each run, Pallas kernels for 1% -> 1%
where the time goes in v5:
time: 155 us; the launch traced here: 154 us
  starting transfers between devices  65.9 us (43%)
  blocking collectives  39.9 us (26%)
  waiting for transfers between devices  30.6 us (20%)
  Pallas kernels  10.7 us (7%)
  local copies, waits for them, and re-layouts  3.69 us (2%)
  other arithmetic  2.42 us (2%)
    all_to_all x3, blocking collectives, exchange(): return lax.all_to_all(array, axes, 0, 0, tiled=True)  39.9 us
    all_to_all x4, starting transfers between devices, exchange(): return lax.all_to_all(array, axes, 0, 0, tiled=True)  34.8 us
    ppermute x8, starting transfers between devices, shift(): lax.ppermute(array, axis, [(i, (i + step) % count) for i in range(count)])  31.2 us
    ppermute x8, waiting for transfers between devices, shift(): lax.ppermute(array, axis, [(i, (i + step) % count) for i in range(count)])  15.7 us
    all_to_all x4, waiting for transfers between devices, exchange(): return lax.all_to_all(array, axes, 0, 0, tiled=True)  14.9 us
    pallas_call x9, Pallas kernels, call(): pl.pallas_call(body, out_shape=out_shape, in_specs=[kinds[s] for s in spa...  10.7 us
  transfers between devices with their start and end apart: 12, of which 7 were waited for; matrix products, arithmetic and copies ran while one was open for 2% of the time, Pallas kernels for 1%

profile of v5, /device:TPU:1, one launch (start us, length us, event | category | flops | bytes accessed | tf_op | source)
XLA Modules:
  0.0 154.4 jit_solution(10855576136559789395)
XLA Ops:
  0.8 3.7 %shard_map.91 = bf16[16,80,128]{2,1,0:T(8,128)(2,1)} custom-call(s32[1]{0:T(128)S(6)} %copy.11.length_ref, bf16[16,8192]{1,0:T(8,128)(2,1)} %bitcast.24, bf16[2,16,1024]{2,1,0:T(8,128)(2,1)} %bitcast.26, bf16[2,64,1024]{2,1,0:T(8,128)(2,1)} %bitcast.25), custom_call_target="tpu_custom_call" | custom-call | tf_op jit(solution)/shard_map/pallas_call | solution.py:37
  4.6 10.3 %all-to-all-start = ((bf16[16,80,128]{2,1,0:T(8,128)(2,1)}), bf16[16,80,128]{2,1,0:T(8,128)(2,1)S(1)}, u32[]{:S(2)}, u32[]{:S(2)}) async-start(bf16[16,80,128]{2,1,0:T(8,128)(2,1)} %shard_map.91), calls=%async_computation | async-start | bytes 655360 | tf_op jit(solution)/shard_map/all_to_all | solution.py:286
  14.8 1.9 %collective-permute-start.1 = (bf16[512,256]{1,0:T(8,128)(2,1)S(1)}, bf16[512,256]{1,0:T(8,128)(2,1)S(1)}, u32[]{:S(2)}, u32[]{:S(2)}) collective-permute-start(bf16[512,256]{1,0:T(8,128)(2,1)S(1)} %copy-done.4), channel_id=1, source_target_pairs={{0,16},{16,0},{1,17},{17,1},{2,18},{18,2},{3,19},{19,3},{4,20},{20... | collective-permute-start | bytes 786440 | tf_op jit(solution)/shard_map/ppermute | solution.py:282
  16.8 3.6 %collective-permute-start = (f32[1,256]{1,0:T(1,128)S(1)}, f32[1,256]{1,0:T(1,128)S(1)}, u32[]{:S(2)}, u32[]{:S(2)}) collective-permute-start(f32[1,256]{1,0:T(1,128)S(1)} %bitcast.27), channel_id=1, source_target_pairs={{0,64},{64,128},{128,192},{192,256},{256,320},{320,384},{384,448},... | collective-permute-start | bytes 3080 | tf_op jit(solution)/shard_map/ppermute | solution.py:282
  20.4 7.6 %collective-permute-done._ = f32[1,256]{1,0:T(1,128)S(1)} collective-permute-done((f32[1,256]{1,0:T(1,128)S(1)}, f32[1,256]{1,0:T(1,128)S(1)}, u32[]{:S(2)}, u32[]{:S(2)}) %collective-permute-start) | collective-permute-done | bytes 1056 | tf_op jit(solution)/shard_map/ppermute | solution.py:282
  29.1 8.5 %all-to-all-start.1 = ((bf16[16,64,128]{2,1,0:T(8,128)(2,1)}), bf16[16,64,128]{2,1,0:T(8,128)(2,1)S(1)}, u32[]{:S(2)}, u32[]{:S(2)}) async-start(bf16[16,64,128]{2,1,0:T(8,128)(2,1)} %shard_map.92), calls=%async_computation.1 | async-start | bytes 524288 | tf_op jit(solution)/shard_map/all_to_all | solution.py:286
  38.9 4.7 %collective-permute-start.2 = (bf16[8,256,128]{2,1,0:T(8,128)(2,1)}, bf16[8,256,128]{2,1,0:T(8,128)(2,1)S(1)}, u32[]{:S(2)}, u32[]{:S(2)}) collective-permute-start(bf16[8,256,128]{2,1,0:T(8,128)(2,1)} %get-tuple-element.21), channel_id=1, source_target_pairs={{0,32},{16,48},{32,0},{48,16},{1,33},{17,49},{33,1},{49,17},{2,34}... | collective-permute-start | bytes 1572872 | tf_op jit(solution)/shard_map/ppermute | solution.py:282
  43.6 3.4 %all-to-all-done.1.attended_ref = bf16[16,64,128]{2,1,0:T(8,128)(2,1)S(1)} async-done(((bf16[16,64,128]{2,1,0:T(8,128)(2,1)}), bf16[16,64,128]{2,1,0:T(8,128)(2,1)S(1)}, u32[]{:S(2)}, u32[]{:S(2)}) %all-to-all-start.1) | async-done | bytes 262176 | tf_op jit(solution)/shard_map/all_to_all | solution.py:286
  49.0 9.0 %all-to-all-start.2 = ((bf16[32,32,128]{2,1,0:T(8,128)(2,1)}), bf16[32,32,128]{2,1,0:T(8,128)(2,1)S(1)}, u32[]{:S(2)}, u32[]{:S(2)}) async-start(bf16[32,32,128]{2,1,0:T(8,128)(2,1)} %shard_map.93), calls=%async_computation.2 | async-start | bytes 524288 | tf_op jit(solution)/shard_map/all_to_all | solution.py:286
  58.0 3.8 %collective-permute-start.3 = (f32[2,256]{1,0:T(2,128)S(1)}, f32[2,256]{1,0:T(2,128)S(1)}, u32[]{:S(2)}, u32[]{:S(2)}) collective-permute-start(f32[2,256]{1,0:T(2,128)S(1)} %pad_maximum_fusion.3), channel_id=1, source_target_pairs={{0,128},{64,192},{128,256},{192,320},{256,384},{320,448},{384,0},{... | collective-permute-start | bytes 6152 | tf_op jit(solution)/shard_map/ppermute | solution.py:282
  61.9 2.8 %collective-permute-done.3.__ = f32[2,256]{1,0:T(2,128)S(1)} collective-permute-done((f32[2,256]{1,0:T(2,128)S(1)}, f32[2,256]{1,0:T(2,128)S(1)}, u32[]{:S(2)}, u32[]{:S(2)}) %collective-permute-start.3) | collective-permute-done | bytes 2080 | tf_op jit(solution)/shard_map/ppermute | solution.py:282
  64.7 4.4 %all-to-all-done.2.parts_ref = bf16[32,32,128]{2,1,0:T(8,128)(2,1)S(1)} async-done(((bf16[32,32,128]{2,1,0:T(8,128)(2,1)}), bf16[32,32,128]{2,1,0:T(8,128)(2,1)S(1)}, u32[]{:S(2)}, u32[]{:S(2)}) %all-to-all-start.2) | async-done | bytes 262176 | tf_op jit(solution)/shard_map/all_to_all | solution.py:286
  70.2 7.0 %all-to-all-start.3 = ((bf16[64,64,128]{2,1,0:T(8,128)(2,1)}), bf16[64,64,128]{2,1,0:T(8,128)(2,1)S(1)}, u32[]{:S(2)}, u32[]{:S(2)}) async-start(bf16[64,64,128]{2,1,0:T(8,128)(2,1)} %shard_map.94), calls=%async_computation.3 | async-start | bytes 2097152 | tf_op jit(solution)/shard_map/all_to_all | solution.py:286
  77.2 2.0 %collective-permute-start.6 = (bf16[8,256,128]{2,1,0:T(8,128)(2,1)}, bf16[8,256,128]{2,1,0:T(8,128)(2,1)S(1)}, u32[]{:S(2)}, u32[]{:S(2)}) collective-permute-start(bf16[8,256,128]{2,1,0:T(8,128)(2,1)} %get-tuple-element.20), channel_id=1, source_target_pairs={{0,48},{16,0},{32,16},{48,32},{1,49},{17,1},{33,17},{49,33},{2,50}... | collective-permute-start | bytes 1572872 | tf_op jit(solution)/shard_map/ppermute | solution.py:282
  79.3 3.3 %collective-permute-start.5 = (bf16[8,256,128]{2,1,0:T(8,128)(2,1)}, bf16[8,256,128]{2,1,0:T(8,128)(2,1)S(1)}, u32[]{:S(2)}, u32[]{:S(2)}) collective-permute-start(bf16[8,256,128]{2,1,0:T(8,128)(2,1)} %get-tuple-element.19), channel_id=1, source_target_pairs={{0,16},{16,32},{32,48},{48,0},{1,17},{17,33},{33,49},{49,1},{2,18}... | collective-permute-start | bytes 1572872 | tf_op jit(solution)/shard_map/ppermute | solution.py:282
  82.6 6.8 %collective-permute-start.4 = (f32[4,256]{1,0:T(4,128)S(1)}, f32[4,256]{1,0:T(4,128)S(1)}, u32[]{:S(2)}, u32[]{:S(2)}) collective-permute-start(f32[4,256]{1,0:T(4,128)S(1)} %pad_maximum_fusion.2), channel_id=1, source_target_pairs={{0,256},{64,320},{128,384},{192,448},{256,0},{320,64},{384,128},{4... | collective-permute-start | bytes 12296 | tf_op jit(solution)/shard_map/ppermute | solution.py:282
  89.4 3.5 %collective-permute-done.4 = f32[4,256]{1,0:T(4,128)S(1)} collective-permute-done((f32[4,256]{1,0:T(4,128)S(1)}, f32[4,256]{1,0:T(4,128)S(1)}, u32[]{:S(2)}, u32[]{:S(2)}) %collective-permute-start.4) | collective-permute-done | bytes 4128 | tf_op jit(solution)/shard_map/ppermute | solution.py:282
  92.9 1.7 %collective-permute-done.5 = bf16[8,256,128]{2,1,0:T(8,128)(2,1)S(1)} collective-permute-done((bf16[8,256,128]{2,1,0:T(8,128)(2,1)}, bf16[8,256,128]{2,1,0:T(8,128)(2,1)S(1)}, u32[]{:S(2)}, u32[]{:S(2)}) %collective-permute-start.5) | collective-permute-done | bytes 524320 | tf_op jit(solution)/shard_map/ppermute | solution.py:282
  94.6 2.4 %pad_maximum_fusion.swapped_ref = bf16[3,8,256,128]{3,2,1,0:T(8,128)(2,1)} fusion(bf16[1,8,256,128]{3,2,1,0:T(8,128)(2,1)S(1)} %bitcast.22, bf16[1,8,256,128]{3,2,1,0:T(8,128)(2,1)} %bitcast.20, bf16[1,8,256,128]{3,2,1,0:T(8,128)(2,1)S(1)} %bitcast.23), kind=kLoop, calls=%fused_computation | loop fusion | flops 1572864 | bytes 3145728 | tf_op jit(solution)/shard_map/stack | solution.py:335
  97.0 7.2 %all-to-all-done.3.mine_ref = bf16[64,64,128]{2,1,0:T(8,128)(2,1)S(1)} async-done(((bf16[64,64,128]{2,1,0:T(8,128)(2,1)}), bf16[64,64,128]{2,1,0:T(8,128)(2,1)S(1)}, u32[]{:S(2)}, u32[]{:S(2)}) %all-to-all-start.3) | async-done | bytes 1048608 | tf_op jit(solution)/shard_map/all_to_all | solution.py:286
  104.2 5.1 %collective-permute-start.7 = (bf16[64,64,128]{2,1,0:T(8,128)(2,1)S(1)}, bf16[64,64,128]{2,1,0:T(8,128)(2,1)S(1)}, u32[]{:S(2)}, u32[]{:S(2)}) collective-permute-start(bf16[64,64,128]{2,1,0:T(8,128)(2,1)S(1)} %all-to-all-done.3.mine_ref), channel_id=1, source_target_pairs={{0,1},{1,0},{2,3},{3,2},{4,5},{5,4},{6,7},{7,6},{8,9},{9,8},{10,11... | collective-permute-start | bytes 3145736 | tf_op jit(solution)/shard_map/ppermute | solution.py:282
  112.9 11.8 %all_to_all.35.parts_ref = bf16[4,528,128]{2,1,0:T(8,128)(2,1)S(1)} all-to-all(bf16[4,528,128]{2,1,0:T(8,128)(2,1)S(1)} %shard_map.96), channel_id=1, replica_groups=mesh['z'=8,'far'=2,'near'=2,'y'=8,'c'=2] {'far','near'}, dimensions={0} | all-to-all | bytes 1081344 | tf_op jit(solution)/shard_map/all_to_all | solution.py:286
  125.4 13.5 %all_to_all.36.parts_ref = f32[16,8,128]{2,1,0:T(8,128)S(1)} all-to-all(f32[16,8,128]{2,1,0:T(8,128)S(1)} %get-tuple-element.17), channel_id=1, replica_groups=mesh['z'=8,'far'=2,'near'=2,'y'=8,'c'=2] {'c','y'}, dimensions={0} | all-to-all | bytes 131072 | tf_op jit(solution)/shard_map/all_to_all | solution.py:286
  138.9 14.6 %all_to_all.37.parts_ref = f32[32,8,128]{2,1,0:T(8,128)S(1)} all-to-all(f32[32,8,128]{2,1,0:T(8,128)S(1)} %shard_map.98), channel_id=1, replica_groups=mesh['z'=8,'far'=2,'near'=2,'y'=8,'c'=2] {'far','near','z'}, dimensions={0} | all-to-all | bytes 262144 | tf_op jit(solution)/shard_map/all_to_all | solution.py:286
  (35 shorter events, 10.7 us)
Async XLA Ops:
  0.0 61.7 %copy-start = (bf16[16,32,256]{2,1,0:T(8,128)(2,1)S(1)}, bf16[16,32,256]{2,1,0:T(8,128)(2,1)}, u32[]{:S(2)}) copy-start(bf16[16,32,256]{2,1,0:T(8,128)(2,1)} %param.14) | copy-start | bytes 786436
  0.0 14.8 %copy-start.4 = (bf16[512,256]{1,0:T(8,128)(2,1)S(1)}, bf16[512,256]{1,0:T(8,128)(2,1)}, u32[]{:S(2)}) copy-start(bf16[512,256]{1,0:T(8,128)(2,1)} %mine_ref.1) | copy-start | bytes 786436
  0.0 16.8 %copy-start.7 = (f32[256]{0:T(256)S(1)}, f32[256]{0:T(256)}, u32[]{:S(2)}) copy-start(f32[256]{0:T(256)} %param.15) | copy-start | bytes 3076
  0.0 37.7 %copy-start.1 = (bf16[8192,128]{1,0:T(8,128)(2,1)S(1)}, bf16[8192,128]{1,0:T(8,128)(2,1)}, u32[]{:S(2)}) copy-start(bf16[8192,128]{1,0:T(8,128)(2,1)} %param.16) | copy-start | bytes 6291460
  4.6 23.4 %all-to-all-start = ((bf16[16,80,128]{2,1,0:T(8,128)(2,1)}), bf16[16,80,128]{2,1,0:T(8,128)(2,1)S(1)}, u32[]{:S(2)}, u32[]{:S(2)}) async-start(bf16[16,80,128]{2,1,0:T(8,128)(2,1)} %shard_map.91), calls=%async_computation | async-start | bytes 655360 | tf_op jit(solution)/shard_map/all_to_all | solution.py:286
  14.8 13.1 %collective-permute-start.1 = (bf16[512,256]{1,0:T(8,128)(2,1)S(1)}, bf16[512,256]{1,0:T(8,128)(2,1)S(1)}, u32[]{:S(2)}, u32[]{:S(2)}) collective-permute-start(bf16[512,256]{1,0:T(8,128)(2,1)S(1)} %copy-done.4), channel_id=1, source_target_pairs={{0,16},{16,0},{1,17},{17,1},{2,18},{18,2},{3,19},{19,3},{4,20},{20... | collective-permute-start | bytes 786440 | tf_op jit(solution)/shard_map/ppermute | solution.py:282
  16.8 11.2 %collective-permute-start = (f32[1,256]{1,0:T(1,128)S(1)}, f32[1,256]{1,0:T(1,128)S(1)}, u32[]{:S(2)}, u32[]{:S(2)}) collective-permute-start(f32[1,256]{1,0:T(1,128)S(1)} %bitcast.27), channel_id=1, source_target_pairs={{0,64},{64,128},{128,192},{192,256},{256,320},{320,384},{384,448},... | collective-permute-start | bytes 3080 | tf_op jit(solution)/shard_map/ppermute | solution.py:282
  29.1 17.9 %all-to-all-start.1 = ((bf16[16,64,128]{2,1,0:T(8,128)(2,1)}), bf16[16,64,128]{2,1,0:T(8,128)(2,1)S(1)}, u32[]{:S(2)}, u32[]{:S(2)}) async-start(bf16[16,64,128]{2,1,0:T(8,128)(2,1)} %shard_map.92), calls=%async_computation.1 | async-start | bytes 524288 | tf_op jit(solution)/shard_map/all_to_all | solution.py:286
  38.9 25.8 %collective-permute-start.2 = (bf16[8,256,128]{2,1,0:T(8,128)(2,1)}, bf16[8,256,128]{2,1,0:T(8,128)(2,1)S(1)}, u32[]{:S(2)}, u32[]{:S(2)}) collective-permute-start(bf16[8,256,128]{2,1,0:T(8,128)(2,1)} %get-tuple-element.21), channel_id=1, source_target_pairs={{0,32},{16,48},{32,0},{48,16},{1,33},{17,49},{33,1},{49,17},{2,34}... | collective-permute-start | bytes 1572872 | tf_op jit(solution)/shard_map/ppermute | solution.py:282
  47.0 1.0 copy-start.5
  49.0 20.1 %all-to-all-start.2 = ((bf16[32,32,128]{2,1,0:T(8,128)(2,1)}), bf16[32,32,128]{2,1,0:T(8,128)(2,1)S(1)}, u32[]{:S(2)}, u32[]{:S(2)}) async-start(bf16[32,32,128]{2,1,0:T(8,128)(2,1)} %shard_map.93), calls=%async_computation.2 | async-start | bytes 524288 | tf_op jit(solution)/shard_map/all_to_all | solution.py:286
  58.0 6.7 %collective-permute-start.3 = (f32[2,256]{1,0:T(2,128)S(1)}, f32[2,256]{1,0:T(2,128)S(1)}, u32[]{:S(2)}, u32[]{:S(2)}) collective-permute-start(f32[2,256]{1,0:T(2,128)S(1)} %pad_maximum_fusion.3), channel_id=1, source_target_pairs={{0,128},{64,192},{128,256},{192,320},{256,384},{320,448},{384,0},{... | collective-permute-start | bytes 6152 | tf_op jit(solution)/shard_map/ppermute | solution.py:282
  64.7 5.5 %copy-start.3 = (bf16[8,256,128]{2,1,0:T(8,128)(2,1)}, bf16[8,256,128]{2,1,0:T(8,128)(2,1)S(1)}, u32[]{:S(2)}) copy-start(bf16[8,256,128]{2,1,0:T(8,128)(2,1)S(1)} %collective-permute-done.2._) | copy-start | bytes 1572868
  70.2 34.0 %all-to-all-start.3 = ((bf16[64,64,128]{2,1,0:T(8,128)(2,1)}), bf16[64,64,128]{2,1,0:T(8,128)(2,1)S(1)}, u32[]{:S(2)}, u32[]{:S(2)}) async-start(bf16[64,64,128]{2,1,0:T(8,128)(2,1)} %shard_map.94), calls=%async_computation.3 | async-start | bytes 2097152 | tf_op jit(solution)/shard_map/all_to_all | solution.py:286
  77.2 15.6 %collective-permute-start.6 = (bf16[8,256,128]{2,1,0:T(8,128)(2,1)}, bf16[8,256,128]{2,1,0:T(8,128)(2,1)S(1)}, u32[]{:S(2)}, u32[]{:S(2)}) collective-permute-start(bf16[8,256,128]{2,1,0:T(8,128)(2,1)} %get-tuple-element.20), channel_id=1, source_target_pairs={{0,48},{16,0},{32,16},{48,32},{1,49},{17,1},{33,17},{49,33},{2,50}... | collective-permute-start | bytes 1572872 | tf_op jit(solution)/shard_map/ppermute | solution.py:282
  79.3 15.4 %collective-permute-start.5 = (bf16[8,256,128]{2,1,0:T(8,128)(2,1)}, bf16[8,256,128]{2,1,0:T(8,128)(2,1)S(1)}, u32[]{:S(2)}, u32[]{:S(2)}) collective-permute-start(bf16[8,256,128]{2,1,0:T(8,128)(2,1)} %get-tuple-element.19), channel_id=1, source_target_pairs={{0,16},{16,32},{32,48},{48,0},{1,17},{17,33},{33,49},{49,1},{2,18}... | collective-permute-start | bytes 1572872 | tf_op jit(solution)/shard_map/ppermute | solution.py:282
  82.6 10.3 %collective-permute-start.4 = (f32[4,256]{1,0:T(4,128)S(1)}, f32[4,256]{1,0:T(4,128)S(1)}, u32[]{:S(2)}, u32[]{:S(2)}) collective-permute-start(f32[4,256]{1,0:T(4,128)S(1)} %pad_maximum_fusion.2), channel_id=1, source_target_pairs={{0,256},{64,320},{128,384},{192,448},{256,0},{320,64},{384,128},{4... | collective-permute-start | bytes 12296 | tf_op jit(solution)/shard_map/ppermute | solution.py:282
  104.2 7.6 %collective-permute-start.7 = (bf16[64,64,128]{2,1,0:T(8,128)(2,1)S(1)}, bf16[64,64,128]{2,1,0:T(8,128)(2,1)S(1)}, u32[]{:S(2)}, u32[]{:S(2)}) collective-permute-start(bf16[64,64,128]{2,1,0:T(8,128)(2,1)S(1)} %all-to-all-done.3.mine_ref), channel_id=1, source_target_pairs={{0,1},{1,0},{2,3},{3,2},{4,5},{5,4},{6,7},{7,6},{8,9},{9,8},{10,11... | collective-permute-start | bytes 3145736 | tf_op jit(solution)/shard_map/ppermute | solution.py:282
  109.3 1.4 copy-start.2
  112.9 40.6 %copy-start.6 = (f32[16,128]{1,0:T(8,128)S(1)}, f32[16,128]{1,0:T(8,128)}, u32[]{:S(2)}) copy-start(f32[16,128]{1,0:T(8,128)} %noise_ref.1) | copy-start | bytes 24580

commit v6 on v5

--- a/solution.py
+++ b/solution.py
@@ -92,27 +92,33 @@
     stat_row = lax.broadcasted_iota(jnp.int32, (16, 128), 0)
     for copy in copies:
         copy.wait()
+    columns = [slice(g * HD, (g + 1) * HD) for g in range(KVH)]
+    scores = []
     for g in range(KVH):
-        columns = slice(g * HD, (g + 1) * HD)
         heads = [
             query_ref[:, (g * GROUP + r) * HD : (g * GROUP + r + 1) * HD] for r in range(GROUP)
         ]
-        rows = jnp.concatenate(heads, axis=0)
-        keys = jnp.concatenate([cache_ref[0, :, columns], new_ref[0, :, columns]], axis=0)
-        values = jnp.concatenate([cache_ref[1, :, columns], new_ref[1, :, columns]], axis=0)
-        scores = lax.dot_general(
-            keys, rows, (((1,), (1,)), ((), ())), preferred_element_type=F32
-        ) * HD ** (-0.5)
-        scores = jnp.where(valid, scores, LOW)
-        top = jnp.max(scores, axis=0, keepdims=True).astype(BF16).astype(F32)
-        weights = jnp.where(valid, jnp.exp(scores - top), 0.0)
-        high, low = split_pair(jnp.sum(weights, axis=0, keepdims=True))
+        keys = jnp.concatenate([cache_ref[0, :, columns[g]], new_ref[0, :, columns[g]]], axis=0)
+        products = lax.dot_general(
+            keys,
+            jnp.concatenate(heads, axis=0),
+            (((1,), (1,)), ((), ())),
+            preferred_element_type=F32,
+        )
+        scores.append(jnp.where(valid, products * HD ** (-0.5), LOW))
+    tops = [jnp.max(score, axis=0, keepdims=True).astype(BF16).astype(F32) for score in scores]
+    weights = [
+        jnp.where(valid, jnp.exp(score - top), 0.0) for score, top in zip(scores, tops)
+    ]
+    for g in range(KVH):
+        values = jnp.concatenate([cache_ref[1, :, columns[g]], new_ref[1, :, columns[g]]], axis=0)
+        high, low = split_pair(jnp.sum(weights[g], axis=0, keepdims=True))
         totals = lax.dot_general(
-            weights.astype(BF16), values, (((0,), (0,)), ((), ())), preferred_element_type=F32
+            weights[g].astype(BF16), values, (((0,), (0,)), ((), ())), preferred_element_type=F32
         ).astype(BF16)
         stats = jnp.where(
             stat_row == 0,
-            top,
+            tops[g],
             jnp.where(stat_row == 1, high, jnp.where(stat_row == 2, low, 0.0)),
         ).astype(BF16)
         for half in range(2):
@@ -120,7 +126,7 @@
             out_ref[NY * half + g, 64:80, :] = stats
 
 
-def combine_kernel(parts_ref, _, __, out_ref):
+def combine_kernel(parts_ref, gain_ref, _, out_ref):
     core = lax.axis_index("c")
     stats = parts_ref[:, 64:80, :].astype(F32)
     tops, totals = stats[:, 0, :], stats[:, 1, :] + stats[:, 2, :]
@@ -132,14 +138,27 @@
     for source in range(NY * NC):
         attended += scale[:, source : source + 1] * parts_ref[source, 0:64, :].astype(F32)
     attended = attended.astype(BF16)
+    stat_row = lax.broadcasted_iota(jnp.int32, (16, 128), 0)
+    gains = jnp.zeros((16, 128), F32)
+    for half in range(NC):
+        high, low = split_pair(gain_ref[half : half + 1, :])
+        gains = jnp.where(stat_row == half, high, jnp.where(stat_row == NC + half, low, gains))
+    gains = gains.astype(BF16)
     for target in range(2 * NZ):
-        out_ref[target] = attended
-
-
-def project_kernel(attended_ref, mine_ref, other_ref, out_ref):
+        out_ref[target, 0:64, :] = attended
+        out_ref[target, 64:80, :] = gains
+
+
+def project_kernel(attended_ref, mine_ref, other_ref, out_ref, gains_ref):
     features = jnp.concatenate(
         [attended_ref[:, 16 * r : 16 * r + 16, :].reshape(ROWS // 2, HD) for r in range(4)], axis=1
     )
+    first = NZ * lax.axis_index("far")
+    pairs = [attended_ref[first + z, 64:80, :].astype(F32) for z in range(NZ)]
+    for half in range(NC):
+        gains_ref[half] = jnp.concatenate(
+            [pair[half : half + 1] + pair[NC + half : NC + half + 1] for pair in pairs], axis=0
+        )
     near = lax.axis_index("near")
     for target, weight_ref in ((near, mine_ref), (1 - near, other_ref)):
         partial = jnp.dot(features, weight_ref[...], preferred_element_type=F32).astype(BF16)
@@ -153,7 +172,7 @@
                 out_ref[index] = rows[:, 128 * c : 128 * c + 128]
 
 
-def residual_kernel(parts_ref, resid_ref, _, __, out_ref):
+def residual_kernel(parts_ref, resid_ref, _, out_ref):
     sums = []
     for near in range(2):
         total = parts_ref[NC * NY * near].astype(F32)
@@ -169,11 +188,7 @@
 
 
 def scaled_rows(ref, gains_ref, core):
-    table = jnp.where(core == 1, gains_ref[:, 128:], gains_ref[:, :128])
-    back = lax.rem(
-        lax.axis_index("z") + NZ - lax.broadcasted_iota(jnp.int32, (NZ, 128), 0), NZ
-    )
-    gains = [jnp.sum(jnp.where(back == z, table, 0.0), axis=0, keepdims=True) for z in range(NZ)]
+    table = jnp.where(core == 1, gains_ref[1], gains_ref[0])
     rows, squares = [], []
     for y in range(NY):
         total = jnp.zeros((64, 128), F32)
@@ -181,7 +196,7 @@
         for z in range(NZ):
             hidden = ref[NZ * y + z].astype(F32)
             total += hidden * hidden
-            blocks.append((hidden * gains[z]).astype(BF16))
+            blocks.append((hidden * table[z : z + 1]).astype(BF16))
         rows.append(jnp.concatenate(blocks, axis=1))
         squares.append(to_row(jnp.sum(total, axis=1, keepdims=True)))
     return jnp.concatenate(rows, axis=0), jnp.concatenate(squares, axis=0)
@@ -294,10 +309,6 @@
         shift(lax.dynamic_index_in_dim(blocks, (x + k) % NX, 1, keepdims=False), X, k)
         for k in range(1, NX)
     ]
-    gains, arrived = norm_gain.reshape(1, 256), []
-    for step in (1, 2, 4):
-        arrived.append(shift(gains, "z", step))
-        gains = jnp.concatenate([gains, arrived[-1]])
     resid_mine = jnp.swapaxes(
         lax.dynamic_slice(resid, (0, 4 * y, 128 * c), (QUERIES, 4, 128)), 0, 1
     ).reshape(64, 128)
@@ -317,22 +328,27 @@
         60,
     )
     parts = exchange(parts, ("c", "y"))
-    attended = call(combine_kernel, shape((2 * NZ, 64, 128)), (parts, arrived[0], other_w), "vww")
+    attended = call(
+        combine_kernel,
+        shape((2 * NZ, 80, 128)),
+        (parts, norm_gain.reshape(NC, 128), other_w),
+        "vvw",
+    )
     attended = exchange(attended, ("far", "z"))
-    partial = call(
+    partial, gains = call(
         project_kernel,
-        shape((2 * NC * NY, 32, 128)),
+        (shape((2 * NC * NY, 32, 128)), shape((NC, NZ, 128), F32)),
         (attended, w_out, other_w),
     )
     partial = exchange(partial, ("near", "c", "y"))
     hidden = call(
         residual_kernel,
         shape((NZ * NY, 64, 128)),
-        (partial, resid_mine, swapped[1], arrived[1]),
-        "vvww",
+        (partial, resid_mine, swapped[1]),
+        "vvw",
     )
     mine = exchange(hidden, ("y", "z"))
-    mine, gains, swapped = lax.optimization_barrier((mine, gains, jnp.stack(swapped)))
+    mine, swapped = lax.optimization_barrier((mine, jnp.stack(swapped)))
     other = shift(mine, "c", 1)
     scratch = (pltpu.VMEM((NZ, 256, 128), BF16), pltpu.SemaphoreType.DMA)
     near, squares = call(

time: 155 us -> 153 us (0.987)
  waiting for transfers between devices: 30.6 us -> 43.6 us
  starting transfers between devices: 65.9 us -> 54.4 us
  blocking collectives: 39.9 us -> 37.8 us
  Pallas kernels: 10.7 us -> 8.74 us
    ppermute x8 -> x5, starting transfers between devices: 31.2 us -> 17 us  [shift(): lax.ppermute(array, axis, [(i, (i + step) % count) for i in range(count)])]
    all_to_all x4, waiting for transfers between devices: 14.9 us -> 23.4 us  [exchange(): return lax.all_to_all(array, axes, 0, 0, tiled=True)]
    ppermute x8 -> x5, waiting for transfers between devices: 15.7 us -> 20.2 us  [shift(): lax.ppermute(array, axis, [(i, (i + step) % count) for i in range(count)])]
    all_to_all x4, starting transfers between devices: 34.8 us -> 37.4 us  [exchange(): return lax.all_to_all(array, axes, 0, 0, tiled=True)]
    all_to_all x3, blocking collectives: 39.9 us -> 37.8 us  [exchange(): return lax.all_to_all(array, axes, 0, 0, tiled=True)]
    pallas_call x9, Pallas kernels: 10.7 us -> 8.74 us  [call(): pl.pallas_call(body, out_shape=out_shape, in_specs=[kinds[s] for s in spa...]
  transfers between devices with their start and end apart: 12 -> 9, of which waited for: 7 -> 7; matrix products, arithmetic and copies ran while one was open for 2% -> 2% of each run, Pallas kernels for 1% -> 1%
where the time goes in v6:
time: 153 us; the launch traced here: 152 us
  starting transfers between devices  54.4 us (36%)
  waiting for transfers between devices  43.6 us (28%)
  blocking collectives  37.8 us (25%)
  Pallas kernels  8.74 us (6%)
  local copies, waits for them, and re-layouts  4.37 us (3%)
  other arithmetic  2.38 us (2%)
    all_to_all x3, blocking collectives, exchange(): return lax.all_to_all(array, axes, 0, 0, tiled=True)  37.8 us
    all_to_all x4, starting transfers between devices, exchange(): return lax.all_to_all(array, axes, 0, 0, tiled=True)  37.4 us
    all_to_all x4, waiting for transfers between devices, exchange(): return lax.all_to_all(array, axes, 0, 0, tiled=True)  23.4 us
    ppermute x5, waiting for transfers between devices, shift(): lax.ppermute(array, axis, [(i, (i + step) % count) for i in range(count)])  20.2 us
    ppermute x5, starting transfers between devices, shift(): lax.ppermute(array, axis, [(i, (i + step) % count) for i in range(count)])  17 us
    pallas_call x9, Pallas kernels, call(): pl.pallas_call(body, out_shape=out_shape, in_specs=[kinds[s] for s in spa...  8.74 us
    unnamed x18, local copies, waits for them, and re-layouts  3.08 us
  transfers between devices with their start and end apart: 9, of which 7 were waited for; matrix products, arithmetic and copies ran while one was open for 2% of the time, Pallas kernels for 1%

profile of v6, /device:TPU:1, one launch (start us, length us, event | category | flops | bytes accessed | tf_op | source)
XLA Modules:
  0.0 152.2 jit_solution(766900608155632756)
XLA Ops:
  0.7 2.5 %shard_map.91 = bf16[16,80,128]{2,1,0:T(8,128)(2,1)} custom-call(s32[1]{0:T(128)S(6)} %copy.11.length_ref, bf16[16,8192]{1,0:T(8,128)(2,1)} %bitcast.25, bf16[2,16,1024]{2,1,0:T(8,128)(2,1)} %bitcast.27, bf16[2,64,1024]{2,1,0:T(8,128)(2,1)} %bitcast.26), custom_call_target="tpu_custom_call" | custom-call | tf_op jit(solution)/shard_map/pallas_call | solution.py:37
  3.2 10.3 %all-to-all-start = ((bf16[16,80,128]{2,1,0:T(8,128)(2,1)}), bf16[16,80,128]{2,1,0:T(8,128)(2,1)S(1)}, u32[]{:S(2)}, u32[]{:S(2)}) async-start(bf16[16,80,128]{2,1,0:T(8,128)(2,1)} %shard_map.91), calls=%async_computation | async-start | bytes 655360 | tf_op jit(solution)/shard_map/all_to_all | solution.py:301
  13.5 1.9 %collective-permute-start = (bf16[512,256]{1,0:T(8,128)(2,1)S(1)}, bf16[512,256]{1,0:T(8,128)(2,1)S(1)}, u32[]{:S(2)}, u32[]{:S(2)}) collective-permute-start(bf16[512,256]{1,0:T(8,128)(2,1)S(1)} %copy-done.4), channel_id=1, source_target_pairs={{0,16},{16,0},{1,17},{17,1},{2,18},{18,2},{3,19},{19,3},{4,20},{20... | collective-permute-start | bytes 786440 | tf_op jit(solution)/shard_map/ppermute | solution.py:297
  15.4 7.7 %collective-permute-done._.other_ref = bf16[512,256]{1,0:T(8,128)(2,1)S(1)} collective-permute-done((bf16[512,256]{1,0:T(8,128)(2,1)S(1)}, bf16[512,256]{1,0:T(8,128)(2,1)S(1)}, u32[]{:S(2)}, u32[]{:S(2)}) %collective-permute-start) | collective-permute-done | bytes 262176 | tf_op jit(solution)/shard_map/ppermute | solution.py:297
  24.2 1.2 shard_map.92
  25.4 10.9 %all-to-all-start.1 = ((bf16[16,80,128]{2,1,0:T(8,128)(2,1)}), bf16[16,80,128]{2,1,0:T(8,128)(2,1)S(1)}, u32[]{:S(2)}, u32[]{:S(2)}) async-start(bf16[16,80,128]{2,1,0:T(8,128)(2,1)} %shard_map.92), calls=%async_computation.1 | async-start | bytes 655360 | tf_op jit(solution)/shard_map/all_to_all | solution.py:301
  36.4 1.2 dynamic-slice_bitcast_fusion.1
  37.6 4.7 %collective-permute-start.1 = (bf16[8,256,128]{2,1,0:T(8,128)(2,1)}, bf16[8,256,128]{2,1,0:T(8,128)(2,1)S(1)}, u32[]{:S(2)}, u32[]{:S(2)}) collective-permute-start(bf16[8,256,128]{2,1,0:T(8,128)(2,1)} %get-tuple-element.23), channel_id=1, source_target_pairs={{0,32},{16,48},{32,0},{48,16},{1,33},{17,49},{33,1},{49,17},{2,34}... | collective-permute-start | bytes 1572872 | tf_op jit(solution)/shard_map/ppermute | solution.py:297
  42.3 4.5 %all-to-all-done.1.attended_ref = bf16[16,80,128]{2,1,0:T(8,128)(2,1)S(1)} async-done(((bf16[16,80,128]{2,1,0:T(8,128)(2,1)}), bf16[16,80,128]{2,1,0:T(8,128)(2,1)S(1)}, u32[]{:S(2)}, u32[]{:S(2)}) %all-to-all-start.1) | async-done | bytes 327712 | tf_op jit(solution)/shard_map/all_to_all | solution.py:301
  48.8 9.0 %all-to-all-start.2 = ((bf16[32,32,128]{2,1,0:T(8,128)(2,1)}), bf16[32,32,128]{2,1,0:T(8,128)(2,1)S(1)}, u32[]{:S(2)}, u32[]{:S(2)}) async-start(bf16[32,32,128]{2,1,0:T(8,128)(2,1)} %copy-done.6), calls=%async_computation.2 | async-start | bytes 524288 | tf_op jit(solution)/shard_map/all_to_all | solution.py:301
  58.0 11.0 %all-to-all-done.2.parts_ref = bf16[32,32,128]{2,1,0:T(8,128)(2,1)S(1)} async-done(((bf16[32,32,128]{2,1,0:T(8,128)(2,1)}), bf16[32,32,128]{2,1,0:T(8,128)(2,1)S(1)}, u32[]{:S(2)}, u32[]{:S(2)}) %all-to-all-start.2) | async-done | bytes 262176 | tf_op jit(solution)/shard_map/all_to_all | solution.py:301
  69.0 1.1 shard_map.94
  70.1 7.2 %all-to-all-start.3 = ((bf16[64,64,128]{2,1,0:T(8,128)(2,1)}), bf16[64,64,128]{2,1,0:T(8,128)(2,1)S(1)}, u32[]{:S(2)}, u32[]{:S(2)}) async-start(bf16[64,64,128]{2,1,0:T(8,128)(2,1)} %shard_map.94), calls=%async_computation.3 | async-start | bytes 2097152 | tf_op jit(solution)/shard_map/all_to_all | solution.py:301
  77.3 2.1 %collective-permute-start.3 = (bf16[8,256,128]{2,1,0:T(8,128)(2,1)}, bf16[8,256,128]{2,1,0:T(8,128)(2,1)S(1)}, u32[]{:S(2)}, u32[]{:S(2)}) collective-permute-start(bf16[8,256,128]{2,1,0:T(8,128)(2,1)} %get-tuple-element.22), channel_id=1, source_target_pairs={{0,48},{16,0},{32,16},{48,32},{1,49},{17,1},{33,17},{49,33},{2,50}... | collective-permute-start | bytes 1572872 | tf_op jit(solution)/shard_map/ppermute | solution.py:297
  79.3 3.2 %collective-permute-start.2 = (bf16[8,256,128]{2,1,0:T(8,128)(2,1)}, bf16[8,256,128]{2,1,0:T(8,128)(2,1)S(1)}, u32[]{:S(2)}, u32[]{:S(2)}) collective-permute-start(bf16[8,256,128]{2,1,0:T(8,128)(2,1)} %get-tuple-element.21), channel_id=1, source_target_pairs={{0,16},{16,32},{32,48},{48,0},{1,17},{17,33},{33,49},{49,1},{2,18}... | collective-permute-start | bytes 1572872 | tf_op jit(solution)/shard_map/ppermute | solution.py:297
  82.6 9.6 %collective-permute-done.3 = bf16[8,256,128]{2,1,0:T(8,128)(2,1)S(1)} collective-permute-done((bf16[8,256,128]{2,1,0:T(8,128)(2,1)}, bf16[8,256,128]{2,1,0:T(8,128)(2,1)S(1)}, u32[]{:S(2)}, u32[]{:S(2)}) %collective-permute-start.3) | collective-permute-done | bytes 524320 | tf_op jit(solution)/shard_map/ppermute | solution.py:297
  92.2 2.9 %collective-permute-done.2 = bf16[8,256,128]{2,1,0:T(8,128)(2,1)S(1)} collective-permute-done((bf16[8,256,128]{2,1,0:T(8,128)(2,1)}, bf16[8,256,128]{2,1,0:T(8,128)(2,1)S(1)}, u32[]{:S(2)}, u32[]{:S(2)}) %collective-permute-start.2) | collective-permute-done | bytes 524320 | tf_op jit(solution)/shard_map/ppermute | solution.py:297
  95.0 2.4 %pad_maximum_fusion.swapped_ref = bf16[3,8,256,128]{3,2,1,0:T(8,128)(2,1)} fusion(bf16[1,8,256,128]{3,2,1,0:T(8,128)(2,1)S(1)} %bitcast.23, bf16[1,8,256,128]{3,2,1,0:T(8,128)(2,1)} %bitcast.20, bf16[1,8,256,128]{3,2,1,0:T(8,128)(2,1)S(1)} %bitcast.24), kind=kLoop, calls=%fused_computation | loop fusion | flops 1572864 | bytes 3145728 | tf_op jit(solution)/shard_map/stack | solution.py:351
  97.4 6.8 %all-to-all-done.3.mine_ref = bf16[64,64,128]{2,1,0:T(8,128)(2,1)S(1)} async-done(((bf16[64,64,128]{2,1,0:T(8,128)(2,1)}), bf16[64,64,128]{2,1,0:T(8,128)(2,1)S(1)}, u32[]{:S(2)}, u32[]{:S(2)}) %all-to-all-start.3) | async-done | bytes 1048608 | tf_op jit(solution)/shard_map/all_to_all | solution.py:301
  104.2 5.1 %collective-permute-start.4 = (bf16[64,64,128]{2,1,0:T(8,128)(2,1)S(1)}, bf16[64,64,128]{2,1,0:T(8,128)(2,1)S(1)}, u32[]{:S(2)}, u32[]{:S(2)}) collective-permute-start(bf16[64,64,128]{2,1,0:T(8,128)(2,1)S(1)} %all-to-all-done.3.mine_ref), channel_id=1, source_target_pairs={{0,1},{1,0},{2,3},{3,2},{4,5},{5,4},{6,7},{7,6},{8,9},{9,8},{10,11... | collective-permute-start | bytes 3145736 | tf_op jit(solution)/shard_map/ppermute | solution.py:297
  109.3 1.4 copy-done.2
  112.9 11.7 %all_to_all.35.parts_ref = bf16[4,528,128]{2,1,0:T(8,128)(2,1)S(1)} all-to-all(bf16[4,528,128]{2,1,0:T(8,128)(2,1)S(1)} %shard_map.96), channel_id=1, replica_groups=mesh['z'=8,'far'=2,'near'=2,'y'=8,'c'=2] {'far','near'}, dimensions={0} | all-to-all | bytes 1081344 | tf_op jit(solution)/shard_map/all_to_all | solution.py:301
  125.3 13.5 %all_to_all.36.parts_ref = f32[16,8,128]{2,1,0:T(8,128)S(1)} all-to-all(f32[16,8,128]{2,1,0:T(8,128)S(1)} %get-tuple-element.19), channel_id=1, replica_groups=mesh['z'=8,'far'=2,'near'=2,'y'=8,'c'=2] {'c','y'}, dimensions={0} | all-to-all | bytes 131072 | tf_op jit(solution)/shard_map/all_to_all | solution.py:301
  138.8 12.6 %all_to_all.37.parts_ref = f32[32,8,128]{2,1,0:T(8,128)S(1)} all-to-all(f32[32,8,128]{2,1,0:T(8,128)S(1)} %shard_map.98), channel_id=1, replica_groups=mesh['z'=8,'far'=2,'near'=2,'y'=8,'c'=2] {'far','near','z'}, dimensions={0} | all-to-all | bytes 262144 | tf_op jit(solution)/shard_map/all_to_all | solution.py:301
  (28 shorter events, 6.8 us)
Async XLA Ops:
  0.0 57.8 %copy-start = (bf16[16,32,256]{2,1,0:T(8,128)(2,1)S(1)}, bf16[16,32,256]{2,1,0:T(8,128)(2,1)}, u32[]{:S(2)}) copy-start(bf16[16,32,256]{2,1,0:T(8,128)(2,1)} %param.14) | copy-start | bytes 786436
  0.0 13.5 %copy-start.4 = (bf16[512,256]{1,0:T(8,128)(2,1)S(1)}, bf16[512,256]{1,0:T(8,128)(2,1)}, u32[]{:S(2)}) copy-start(bf16[512,256]{1,0:T(8,128)(2,1)} %mine_ref.1) | copy-start | bytes 786436
  0.0 24.2 %copy-start.8 = (f32[256]{0:T(256)S(1)}, f32[256]{0:T(256)}, u32[]{:S(2)}) copy-start(f32[256]{0:T(256)} %param.15) | copy-start | bytes 3076
  0.7 35.7 %copy-start.1 = (bf16[8192,128]{1,0:T(8,128)(2,1)S(1)}, bf16[8192,128]{1,0:T(8,128)(2,1)}, u32[]{:S(2)}) copy-start(bf16[8192,128]{1,0:T(8,128)(2,1)} %param.16) | copy-start | bytes 6291460
  3.2 21.0 %all-to-all-start = ((bf16[16,80,128]{2,1,0:T(8,128)(2,1)}), bf16[16,80,128]{2,1,0:T(8,128)(2,1)S(1)}, u32[]{:S(2)}, u32[]{:S(2)}) async-start(bf16[16,80,128]{2,1,0:T(8,128)(2,1)} %shard_map.91), calls=%async_computation | async-start | bytes 655360 | tf_op jit(solution)/shard_map/all_to_all | solution.py:301
  13.5 9.6 %collective-permute-start = (bf16[512,256]{1,0:T(8,128)(2,1)S(1)}, bf16[512,256]{1,0:T(8,128)(2,1)S(1)}, u32[]{:S(2)}, u32[]{:S(2)}) collective-permute-start(bf16[512,256]{1,0:T(8,128)(2,1)S(1)} %copy-done.4), channel_id=1, source_target_pairs={{0,16},{16,0},{1,17},{17,1},{2,18},{18,2},{3,19},{19,3},{4,20},{20... | collective-permute-start | bytes 786440 | tf_op jit(solution)/shard_map/ppermute | solution.py:297
  25.4 21.4 %all-to-all-start.1 = ((bf16[16,80,128]{2,1,0:T(8,128)(2,1)}), bf16[16,80,128]{2,1,0:T(8,128)(2,1)S(1)}, u32[]{:S(2)}, u32[]{:S(2)}) async-start(bf16[16,80,128]{2,1,0:T(8,128)(2,1)} %shard_map.92), calls=%async_computation.1 | async-start | bytes 655360 | tf_op jit(solution)/shard_map/all_to_all | solution.py:301
  37.6 20.4 %collective-permute-start.1 = (bf16[8,256,128]{2,1,0:T(8,128)(2,1)}, bf16[8,256,128]{2,1,0:T(8,128)(2,1)S(1)}, u32[]{:S(2)}, u32[]{:S(2)}) collective-permute-start(bf16[8,256,128]{2,1,0:T(8,128)(2,1)} %get-tuple-element.23), channel_id=1, source_target_pairs={{0,32},{16,48},{32,0},{48,16},{1,33},{17,49},{33,1},{49,17},{2,34}... | collective-permute-start | bytes 1572872 | tf_op jit(solution)/shard_map/ppermute | solution.py:297
  46.8 1.0 copy-start.5
  48.1 0.7 copy-start.6
  48.8 20.2 %all-to-all-start.2 = ((bf16[32,32,128]{2,1,0:T(8,128)(2,1)}), bf16[32,32,128]{2,1,0:T(8,128)(2,1)S(1)}, u32[]{:S(2)}, u32[]{:S(2)}) async-start(bf16[32,32,128]{2,1,0:T(8,128)(2,1)} %copy-done.6), calls=%async_computation.2 | async-start | bytes 524288 | tf_op jit(solution)/shard_map/all_to_all | solution.py:301
  58.0 12.2 %copy-start.3 = (bf16[8,256,128]{2,1,0:T(8,128)(2,1)}, bf16[8,256,128]{2,1,0:T(8,128)(2,1)S(1)}, u32[]{:S(2)}) copy-start(bf16[8,256,128]{2,1,0:T(8,128)(2,1)S(1)} %collective-permute-done.1._) | copy-start | bytes 1572868
  70.1 34.1 %all-to-all-start.3 = ((bf16[64,64,128]{2,1,0:T(8,128)(2,1)}), bf16[64,64,128]{2,1,0:T(8,128)(2,1)S(1)}, u32[]{:S(2)}, u32[]{:S(2)}) async-start(bf16[64,64,128]{2,1,0:T(8,128)(2,1)} %shard_map.94), calls=%async_computation.3 | async-start | bytes 2097152 | tf_op jit(solution)/shard_map/all_to_all | solution.py:301
  77.3 14.9 %collective-permute-start.3 = (bf16[8,256,128]{2,1,0:T(8,128)(2,1)}, bf16[8,256,128]{2,1,0:T(8,128)(2,1)S(1)}, u32[]{:S(2)}, u32[]{:S(2)}) collective-permute-start(bf16[8,256,128]{2,1,0:T(8,128)(2,1)} %get-tuple-element.22), channel_id=1, source_target_pairs={{0,48},{16,0},{32,16},{48,32},{1,49},{17,1},{33,17},{49,33},{2,50}... | collective-permute-start | bytes 1572872 | tf_op jit(solution)/shard_map/ppermute | solution.py:297
  79.3 15.7 %collective-permute-start.2 = (bf16[8,256,128]{2,1,0:T(8,128)(2,1)}, bf16[8,256,128]{2,1,0:T(8,128)(2,1)S(1)}, u32[]{:S(2)}, u32[]{:S(2)}) collective-permute-start(bf16[8,256,128]{2,1,0:T(8,128)(2,1)} %get-tuple-element.21), channel_id=1, source_target_pairs={{0,16},{16,32},{32,48},{48,0},{1,17},{17,33},{33,49},{49,1},{2,18}... | collective-permute-start | bytes 1572872 | tf_op jit(solution)/shard_map/ppermute | solution.py:297
  104.2 7.6 %collective-permute-start.4 = (bf16[64,64,128]{2,1,0:T(8,128)(2,1)S(1)}, bf16[64,64,128]{2,1,0:T(8,128)(2,1)S(1)}, u32[]{:S(2)}, u32[]{:S(2)}) collective-permute-start(bf16[64,64,128]{2,1,0:T(8,128)(2,1)S(1)} %all-to-all-done.3.mine_ref), channel_id=1, source_target_pairs={{0,1},{1,0},{2,3},{3,2},{4,5},{5,4},{6,7},{7,6},{8,9},{9,8},{10,11... | collective-permute-start | bytes 3145736 | tf_op jit(solution)/shard_map/ppermute | solution.py:297
  109.3 1.4 copy-start.2
  112.9 38.4 %copy-start.7 = (f32[16,128]{1,0:T(8,128)S(1)}, f32[16,128]{1,0:T(8,128)}, u32[]{:S(2)}) copy-start(f32[16,128]{1,0:T(8,128)} %noise_ref.1) | copy-start | bytes 24580

commit v7 on v6

--- a/solution.py
+++ b/solution.py
@@ -248,7 +248,7 @@
     for source in range(1, NX):
         stats += parts_ref[source, ROWS : ROWS + 16, :].astype(F32)
     factor = lax.rsqrt((stats[0:NY] + stats[NY:]) / D + 1e-05)
-    tops, totals = [], []
+    masses = []
     for block in range(4):
         rows = slice(128 * block, 128 * block + 128)
         logits = parts_ref[0, rows, :].astype(F32)
@@ -260,34 +260,31 @@
         logits = logits * column
         logits_ref[rows, :] = logits
         top = jnp.max(logits, axis=1, keepdims=True)
-        tops.append(to_row(top))
-        totals.append(to_row(jnp.sum(jnp.exp(logits - top), axis=1, keepdims=True)))
-    packed = jnp.concatenate(tops + totals, axis=0)
+        total = jnp.sum(jnp.exp(logits - top), axis=1, keepdims=True)
+        masses.append(to_row(top + jnp.log(total)))
+    packed = jnp.concatenate(masses, axis=0)
     for target in range(NY * NC):
         out_ref[target] = packed
 
 
-def merge_stats(parts):
-    tops = parts[:, 0:4, :]
-    top = jnp.max(tops, axis=0)
-    total = jnp.sum(jnp.exp(tops - top[None]) * parts[:, 4:8, :], axis=0)
-    return top, total
+def merge_masses(masses):
+    top = jnp.max(masses, axis=0)
+    return top + jnp.log(jnp.sum(jnp.exp(masses - top[None]), axis=0))
 
 
 def merge_kernel(parts_ref, out_ref):
-    top, total = merge_stats(parts_ref[...])
-    packed = jnp.concatenate([top, total], axis=0)
+    merged = merge_masses(parts_ref[...])
     for target in range(NZ * NX):
-        out_ref[target] = packed
+        out_ref[target] = merged
 
 
 def vote_kernel(parts_ref, logits_ref, noise_ref, out_ref):
-    top, total = merge_stats(parts_ref[...])
+    merged = merge_masses(parts_ref[...])
     averaged = jnp.zeros((QUERIES, 128), F32)
     for block in range(4):
         mass = jnp.exp(
-            logits_ref[128 * block : 128 * block + 128, :] - to_column(top[block : block + 1])
-        ) / to_column(total[block : block + 1])
+            logits_ref[128 * block : 128 * block + 128, :] - to_column(merged[block : block + 1])
+        )
         averaged += jnp.sum(mass.reshape(8, QUERIES, 128), axis=0)
     out_ref[...] = jnp.log(VOCAB * (averaged / PROMPTS)) + noise_ref[...]
 
@@ -369,10 +366,10 @@
     )
     logits = exchange(logits, X)
     logits, stats = call(
-        logit_kernel, (shape((ROWS, 128), F32), shape((NY * NC, 8, 128), F32)), (logits,)
+        logit_kernel, (shape((ROWS, 128), F32), shape((NY * NC, 4, 128), F32)), (logits,)
     )
     stats = exchange(stats, ("c", "y"))
-    stats = call(merge_kernel, shape((NZ * NX, 8, 128), F32), (stats,))
+    stats = call(merge_kernel, shape((NZ * NX, 4, 128), F32), (stats,))
     stats = exchange(stats, X + ("z",))
     return call(vote_kernel, shape((QUERIES, 128), F32), (stats, logits, noise))
 

time: 153 us -> 153 us (level)
  no operation moved by 1% of the time
where the time goes in v7:
time: 153 us; the launch traced here: 152 us
  starting transfers between devices  54.4 us (36%)
  waiting for transfers between devices  43.6 us (28%)
  blocking collectives  37.3 us (24%)
  Pallas kernels  8.73 us (6%)
  local copies, waits for them, and re-layouts  4.37 us (3%)
  other arithmetic  2.38 us (2%)
    all_to_all x4, starting transfers between devices, exchange(): return lax.all_to_all(array, axes, 0, 0, tiled=True)  37.4 us
    all_to_all x3, blocking collectives, exchange(): return lax.all_to_all(array, axes, 0, 0, tiled=True)  37.3 us
    all_to_all x4, waiting for transfers between devices, exchange(): return lax.all_to_all(array, axes, 0, 0, tiled=True)  23.4 us
    ppermute x5, waiting for transfers between devices, shift(): lax.ppermute(array, axis, [(i, (i + step) % count) for i in range(count)])  20.2 us
    ppermute x5, starting transfers between devices, shift(): lax.ppermute(array, axis, [(i, (i + step) % count) for i in range(count)])  17 us
    pallas_call x9, Pallas kernels, call(): pl.pallas_call(body, out_shape=out_shape, in_specs=[kinds[s] for s in spa...  8.73 us
    unnamed x18, local copies, waits for them, and re-layouts  3.08 us
  transfers between devices with their start and end apart: 9, of which 7 were waited for; matrix products, arithmetic and copies ran while one was open for 2% of the time, Pallas kernels for 1%

profile of v7, /device:TPU:1, one launch (start us, length us, event | category | flops | bytes accessed | tf_op | source)
XLA Modules:
  0.0 151.7 jit_solution(11830499531319737027)
XLA Ops:
  0.7 2.5 %shard_map.91 = bf16[16,80,128]{2,1,0:T(8,128)(2,1)} custom-call(s32[1]{0:T(128)S(6)} %copy.11.length_ref, bf16[16,8192]{1,0:T(8,128)(2,1)} %bitcast.25, bf16[2,16,1024]{2,1,0:T(8,128)(2,1)} %bitcast.27, bf16[2,64,1024]{2,1,0:T(8,128)(2,1)} %bitcast.26), custom_call_target="tpu_custom_call" | custom-call | tf_op jit(solution)/shard_map/pallas_call | solution.py:37
  3.2 10.3 %all-to-all-start = ((bf16[16,80,128]{2,1,0:T(8,128)(2,1)}), bf16[16,80,128]{2,1,0:T(8,128)(2,1)S(1)}, u32[]{:S(2)}, u32[]{:S(2)}) async-start(bf16[16,80,128]{2,1,0:T(8,128)(2,1)} %shard_map.91), calls=%async_computation | async-start | bytes 655360 | tf_op jit(solution)/shard_map/all_to_all | solution.py:298
  13.5 1.9 %collective-permute-start = (bf16[512,256]{1,0:T(8,128)(2,1)S(1)}, bf16[512,256]{1,0:T(8,128)(2,1)S(1)}, u32[]{:S(2)}, u32[]{:S(2)}) collective-permute-start(bf16[512,256]{1,0:T(8,128)(2,1)S(1)} %copy-done.4), channel_id=1, source_target_pairs={{0,16},{16,0},{1,17},{17,1},{2,18},{18,2},{3,19},{19,3},{4,20},{20... | collective-permute-start | bytes 786440 | tf_op jit(solution)/shard_map/ppermute | solution.py:294
  15.4 7.7 %collective-permute-done._.other_ref = bf16[512,256]{1,0:T(8,128)(2,1)S(1)} collective-permute-done((bf16[512,256]{1,0:T(8,128)(2,1)S(1)}, bf16[512,256]{1,0:T(8,128)(2,1)S(1)}, u32[]{:S(2)}, u32[]{:S(2)}) %collective-permute-start) | collective-permute-done | bytes 262176 | tf_op jit(solution)/shard_map/ppermute | solution.py:294
  24.2 1.2 shard_map.92
  25.4 10.9 %all-to-all-start.1 = ((bf16[16,80,128]{2,1,0:T(8,128)(2,1)}), bf16[16,80,128]{2,1,0:T(8,128)(2,1)S(1)}, u32[]{:S(2)}, u32[]{:S(2)}) async-start(bf16[16,80,128]{2,1,0:T(8,128)(2,1)} %shard_map.92), calls=%async_computation.1 | async-start | bytes 655360 | tf_op jit(solution)/shard_map/all_to_all | solution.py:298
  36.4 1.2 dynamic-slice_bitcast_fusion.1
  37.6 4.7 %collective-permute-start.1 = (bf16[8,256,128]{2,1,0:T(8,128)(2,1)}, bf16[8,256,128]{2,1,0:T(8,128)(2,1)S(1)}, u32[]{:S(2)}, u32[]{:S(2)}) collective-permute-start(bf16[8,256,128]{2,1,0:T(8,128)(2,1)} %get-tuple-element.23), channel_id=1, source_target_pairs={{0,32},{16,48},{32,0},{48,16},{1,33},{17,49},{33,1},{49,17},{2,34}... | collective-permute-start | bytes 1572872 | tf_op jit(solution)/shard_map/ppermute | solution.py:294
  42.3 4.5 %all-to-all-done.1.attended_ref = bf16[16,80,128]{2,1,0:T(8,128)(2,1)S(1)} async-done(((bf16[16,80,128]{2,1,0:T(8,128)(2,1)}), bf16[16,80,128]{2,1,0:T(8,128)(2,1)S(1)}, u32[]{:S(2)}, u32[]{:S(2)}) %all-to-all-start.1) | async-done | bytes 327712 | tf_op jit(solution)/shard_map/all_to_all | solution.py:298
  48.8 9.0 %all-to-all-start.2 = ((bf16[32,32,128]{2,1,0:T(8,128)(2,1)}), bf16[32,32,128]{2,1,0:T(8,128)(2,1)S(1)}, u32[]{:S(2)}, u32[]{:S(2)}) async-start(bf16[32,32,128]{2,1,0:T(8,128)(2,1)} %copy-done.6), calls=%async_computation.2 | async-start | bytes 524288 | tf_op jit(solution)/shard_map/all_to_all | solution.py:298
  58.0 11.0 %all-to-all-done.2.parts_ref = bf16[32,32,128]{2,1,0:T(8,128)(2,1)S(1)} async-done(((bf16[32,32,128]{2,1,0:T(8,128)(2,1)}), bf16[32,32,128]{2,1,0:T(8,128)(2,1)S(1)}, u32[]{:S(2)}, u32[]{:S(2)}) %all-to-all-start.2) | async-done | bytes 262176 | tf_op jit(solution)/shard_map/all_to_all | solution.py:298
  69.0 1.1 shard_map.94
  70.1 7.2 %all-to-all-start.3 = ((bf16[64,64,128]{2,1,0:T(8,128)(2,1)}), bf16[64,64,128]{2,1,0:T(8,128)(2,1)S(1)}, u32[]{:S(2)}, u32[]{:S(2)}) async-start(bf16[64,64,128]{2,1,0:T(8,128)(2,1)} %shard_map.94), calls=%async_computation.3 | async-start | bytes 2097152 | tf_op jit(solution)/shard_map/all_to_all | solution.py:298
  77.3 2.1 %collective-permute-start.3 = (bf16[8,256,128]{2,1,0:T(8,128)(2,1)}, bf16[8,256,128]{2,1,0:T(8,128)(2,1)S(1)}, u32[]{:S(2)}, u32[]{:S(2)}) collective-permute-start(bf16[8,256,128]{2,1,0:T(8,128)(2,1)} %get-tuple-element.22), channel_id=1, source_target_pairs={{0,48},{16,0},{32,16},{48,32},{1,49},{17,1},{33,17},{49,33},{2,50}... | collective-permute-start | bytes 1572872 | tf_op jit(solution)/shard_map/ppermute | solution.py:294
  79.3 3.2 %collective-permute-start.2 = (bf16[8,256,128]{2,1,0:T(8,128)(2,1)}, bf16[8,256,128]{2,1,0:T(8,128)(2,1)S(1)}, u32[]{:S(2)}, u32[]{:S(2)}) collective-permute-start(bf16[8,256,128]{2,1,0:T(8,128)(2,1)} %get-tuple-element.21), channel_id=1, source_target_pairs={{0,16},{16,32},{32,48},{48,0},{1,17},{17,33},{33,49},{49,1},{2,18}... | collective-permute-start | bytes 1572872 | tf_op jit(solution)/shard_map/ppermute | solution.py:294
  82.6 9.6 %collective-permute-done.3 = bf16[8,256,128]{2,1,0:T(8,128)(2,1)S(1)} collective-permute-done((bf16[8,256,128]{2,1,0:T(8,128)(2,1)}, bf16[8,256,128]{2,1,0:T(8,128)(2,1)S(1)}, u32[]{:S(2)}, u32[]{:S(2)}) %collective-permute-start.3) | collective-permute-done | bytes 524320 | tf_op jit(solution)/shard_map/ppermute | solution.py:294
  92.2 2.9 %collective-permute-done.2 = bf16[8,256,128]{2,1,0:T(8,128)(2,1)S(1)} collective-permute-done((bf16[8,256,128]{2,1,0:T(8,128)(2,1)}, bf16[8,256,128]{2,1,0:T(8,128)(2,1)S(1)}, u32[]{:S(2)}, u32[]{:S(2)}) %collective-permute-start.2) | collective-permute-done | bytes 524320 | tf_op jit(solution)/shard_map/ppermute | solution.py:294
  95.0 2.4 %pad_maximum_fusion.swapped_ref = bf16[3,8,256,128]{3,2,1,0:T(8,128)(2,1)} fusion(bf16[1,8,256,128]{3,2,1,0:T(8,128)(2,1)S(1)} %bitcast.23, bf16[1,8,256,128]{3,2,1,0:T(8,128)(2,1)} %bitcast.20, bf16[1,8,256,128]{3,2,1,0:T(8,128)(2,1)S(1)} %bitcast.24), kind=kLoop, calls=%fused_computation | loop fusion | flops 1572864 | bytes 3145728 | tf_op jit(solution)/shard_map/stack | solution.py:348
  97.4 6.8 %all-to-all-done.3.mine_ref = bf16[64,64,128]{2,1,0:T(8,128)(2,1)S(1)} async-done(((bf16[64,64,128]{2,1,0:T(8,128)(2,1)}), bf16[64,64,128]{2,1,0:T(8,128)(2,1)S(1)}, u32[]{:S(2)}, u32[]{:S(2)}) %all-to-all-start.3) | async-done | bytes 1048608 | tf_op jit(solution)/shard_map/all_to_all | solution.py:298
  104.2 5.1 %collective-permute-start.4 = (bf16[64,64,128]{2,1,0:T(8,128)(2,1)S(1)}, bf16[64,64,128]{2,1,0:T(8,128)(2,1)S(1)}, u32[]{:S(2)}, u32[]{:S(2)}) collective-permute-start(bf16[64,64,128]{2,1,0:T(8,128)(2,1)S(1)} %all-to-all-done.3.mine_ref), channel_id=1, source_target_pairs={{0,1},{1,0},{2,3},{3,2},{4,5},{5,4},{6,7},{7,6},{8,9},{9,8},{10,11... | collective-permute-start | bytes 3145736 | tf_op jit(solution)/shard_map/ppermute | solution.py:294
  109.3 1.4 copy-done.2
  112.9 11.7 %all_to_all.35.parts_ref = bf16[4,528,128]{2,1,0:T(8,128)(2,1)S(1)} all-to-all(bf16[4,528,128]{2,1,0:T(8,128)(2,1)S(1)} %shard_map.96), channel_id=1, replica_groups=mesh['z'=8,'far'=2,'near'=2,'y'=8,'c'=2] {'far','near'}, dimensions={0} | all-to-all | bytes 1081344 | tf_op jit(solution)/shard_map/all_to_all | solution.py:298
  125.3 13.3 %all_to_all.36.parts_ref = f32[16,4,128]{2,1,0:T(4,128)S(1)} all-to-all(f32[16,4,128]{2,1,0:T(4,128)S(1)} %get-tuple-element.19), channel_id=1, replica_groups=mesh['z'=8,'far'=2,'near'=2,'y'=8,'c'=2] {'c','y'}, dimensions={0} | all-to-all | bytes 65536 | tf_op jit(solution)/shard_map/all_to_all | solution.py:298
  138.7 12.2 %all_to_all.37.parts_ref = f32[32,4,128]{2,1,0:T(4,128)S(1)} all-to-all(f32[32,4,128]{2,1,0:T(4,128)S(1)} %shard_map.98), channel_id=1, replica_groups=mesh['z'=8,'far'=2,'near'=2,'y'=8,'c'=2] {'far','near','z'}, dimensions={0} | all-to-all | bytes 131072 | tf_op jit(solution)/shard_map/all_to_all | solution.py:298
  (28 shorter events, 6.8 us)
Async XLA Ops:
  0.0 57.8 %copy-start = (bf16[16,32,256]{2,1,0:T(8,128)(2,1)S(1)}, bf16[16,32,256]{2,1,0:T(8,128)(2,1)}, u32[]{:S(2)}) copy-start(bf16[16,32,256]{2,1,0:T(8,128)(2,1)} %param.14) | copy-start | bytes 786436
  0.0 13.5 %copy-start.4 = (bf16[512,256]{1,0:T(8,128)(2,1)S(1)}, bf16[512,256]{1,0:T(8,128)(2,1)}, u32[]{:S(2)}) copy-start(bf16[512,256]{1,0:T(8,128)(2,1)} %mine_ref.1) | copy-start | bytes 786436
  0.0 24.2 %copy-start.8 = (f32[256]{0:T(256)S(1)}, f32[256]{0:T(256)}, u32[]{:S(2)}) copy-start(f32[256]{0:T(256)} %param.15) | copy-start | bytes 3076
  0.7 35.7 %copy-start.1 = (bf16[8192,128]{1,0:T(8,128)(2,1)S(1)}, bf16[8192,128]{1,0:T(8,128)(2,1)}, u32[]{:S(2)}) copy-start(bf16[8192,128]{1,0:T(8,128)(2,1)} %param.16) | copy-start | bytes 6291460
  3.2 21.0 %all-to-all-start = ((bf16[16,80,128]{2,1,0:T(8,128)(2,1)}), bf16[16,80,128]{2,1,0:T(8,128)(2,1)S(1)}, u32[]{:S(2)}, u32[]{:S(2)}) async-start(bf16[16,80,128]{2,1,0:T(8,128)(2,1)} %shard_map.91), calls=%async_computation | async-start | bytes 655360 | tf_op jit(solution)/shard_map/all_to_all | solution.py:298
  13.5 9.6 %collective-permute-start = (bf16[512,256]{1,0:T(8,128)(2,1)S(1)}, bf16[512,256]{1,0:T(8,128)(2,1)S(1)}, u32[]{:S(2)}, u32[]{:S(2)}) collective-permute-start(bf16[512,256]{1,0:T(8,128)(2,1)S(1)} %copy-done.4), channel_id=1, source_target_pairs={{0,16},{16,0},{1,17},{17,1},{2,18},{18,2},{3,19},{19,3},{4,20},{20... | collective-permute-start | bytes 786440 | tf_op jit(solution)/shard_map/ppermute | solution.py:294
  25.4 21.4 %all-to-all-start.1 = ((bf16[16,80,128]{2,1,0:T(8,128)(2,1)}), bf16[16,80,128]{2,1,0:T(8,128)(2,1)S(1)}, u32[]{:S(2)}, u32[]{:S(2)}) async-start(bf16[16,80,128]{2,1,0:T(8,128)(2,1)} %shard_map.92), calls=%async_computation.1 | async-start | bytes 655360 | tf_op jit(solution)/shard_map/all_to_all | solution.py:298
  37.6 20.4 %collective-permute-start.1 = (bf16[8,256,128]{2,1,0:T(8,128)(2,1)}, bf16[8,256,128]{2,1,0:T(8,128)(2,1)S(1)}, u32[]{:S(2)}, u32[]{:S(2)}) collective-permute-start(bf16[8,256,128]{2,1,0:T(8,128)(2,1)} %get-tuple-element.23), channel_id=1, source_target_pairs={{0,32},{16,48},{32,0},{48,16},{1,33},{17,49},{33,1},{49,17},{2,34}... | collective-permute-start | bytes 1572872 | tf_op jit(solution)/shard_map/ppermute | solution.py:294
  46.8 1.0 copy-start.5
  48.1 0.7 copy-start.6
  48.8 20.2 %all-to-all-start.2 = ((bf16[32,32,128]{2,1,0:T(8,128)(2,1)}), bf16[32,32,128]{2,1,0:T(8,128)(2,1)S(1)}, u32[]{:S(2)}, u32[]{:S(2)}) async-start(bf16[32,32,128]{2,1,0:T(8,128)(2,1)} %copy-done.6), calls=%async_computation.2 | async-start | bytes 524288 | tf_op jit(solution)/shard_map/all_to_all | solution.py:298
  58.0 12.2 %copy-start.3 = (bf16[8,256,128]{2,1,0:T(8,128)(2,1)}, bf16[8,256,128]{2,1,0:T(8,128)(2,1)S(1)}, u32[]{:S(2)}) copy-start(bf16[8,256,128]{2,1,0:T(8,128)(2,1)S(1)} %collective-permute-done.1._) | copy-start | bytes 1572868
  70.1 34.1 %all-to-all-start.3 = ((bf16[64,64,128]{2,1,0:T(8,128)(2,1)}), bf16[64,64,128]{2,1,0:T(8,128)(2,1)S(1)}, u32[]{:S(2)}, u32[]{:S(2)}) async-start(bf16[64,64,128]{2,1,0:T(8,128)(2,1)} %shard_map.94), calls=%async_computation.3 | async-start | bytes 2097152 | tf_op jit(solution)/shard_map/all_to_all | solution.py:298
  77.3 14.9 %collective-permute-start.3 = (bf16[8,256,128]{2,1,0:T(8,128)(2,1)}, bf16[8,256,128]{2,1,0:T(8,128)(2,1)S(1)}, u32[]{:S(2)}, u32[]{:S(2)}) collective-permute-start(bf16[8,256,128]{2,1,0:T(8,128)(2,1)} %get-tuple-element.22), channel_id=1, source_target_pairs={{0,48},{16,0},{32,16},{48,32},{1,49},{17,1},{33,17},{49,33},{2,50}... | collective-permute-start | bytes 1572872 | tf_op jit(solution)/shard_map/ppermute | solution.py:294
  79.3 15.7 %collective-permute-start.2 = (bf16[8,256,128]{2,1,0:T(8,128)(2,1)}, bf16[8,256,128]{2,1,0:T(8,128)(2,1)S(1)}, u32[]{:S(2)}, u32[]{:S(2)}) collective-permute-start(bf16[8,256,128]{2,1,0:T(8,128)(2,1)} %get-tuple-element.21), channel_id=1, source_target_pairs={{0,16},{16,32},{32,48},{48,0},{1,17},{17,33},{33,49},{49,1},{2,18}... | collective-permute-start | bytes 1572872 | tf_op jit(solution)/shard_map/ppermute | solution.py:294
  104.2 7.6 %collective-permute-start.4 = (bf16[64,64,128]{2,1,0:T(8,128)(2,1)S(1)}, bf16[64,64,128]{2,1,0:T(8,128)(2,1)S(1)}, u32[]{:S(2)}, u32[]{:S(2)}) collective-permute-start(bf16[64,64,128]{2,1,0:T(8,128)(2,1)S(1)} %all-to-all-done.3.mine_ref), channel_id=1, source_target_pairs={{0,1},{1,0},{2,3},{3,2},{4,5},{5,4},{6,7},{7,6},{8,9},{9,8},{10,11... | collective-permute-start | bytes 3145736 | tf_op jit(solution)/shard_map/ppermute | solution.py:294
  109.3 1.4 copy-start.2
  112.9 38.0 %copy-start.7 = (f32[16,128]{1,0:T(8,128)S(1)}, f32[16,128]{1,0:T(8,128)}, u32[]{:S(2)}) copy-start(f32[16,128]{1,0:T(8,128)} %noise_ref.1) | copy-start | bytes 24580

commit v8 on v7

--- a/solution.py
+++ b/solution.py
@@ -202,22 +202,31 @@
     return jnp.concatenate(rows, axis=0), jnp.concatenate(squares, axis=0)
 
 
-def head_block(refs, start):
+def head_block(own_ref, swapped_ref, start, pair):
     rows = pl.ds(pl.multiple_of(start, 128), 128)
-    return jnp.concatenate([ref[:, rows, :].reshape(NZ * 128, 128) for ref in refs], axis=1)
+    parts = [
+        own_ref[...] if k == 0 else swapped_ref[k - 1, :, rows, :]
+        for k in (2 * pair, 2 * pair + 1)
+    ]
+    return jnp.concatenate([part.reshape(NZ * 128, 128) for part in parts], axis=1)
+
+
+def fetch_own(head_ref, x, start, block_ref, semaphore):
+    rows = pl.ds(pl.multiple_of(start, 128), 128)
+    fetch = pltpu.make_async_copy(head_ref.at[:, x, rows], block_ref, semaphore)
+    fetch.start()
+    return fetch
 
 
 def near_kernel(mine_ref, gains_ref, head_ref, swapped_ref, out_ref, squares_ref, block_ref, semaphore):
-    fetch = pltpu.make_async_copy(head_ref.at[:, x_index()], block_ref, semaphore)
-    fetch.start()
     core = lax.axis_index("c")
     start = core * 128
+    fetch = fetch_own(head_ref, x_index(), start, block_ref, semaphore)
     mine, squares_ref[...] = scaled_rows(mine_ref, gains_ref, core)
     fetch.wait()
-    blocks = [block_ref] + [swapped_ref.at[k] for k in range(NX - 1)]
     for pair in range(NX // 2):
         out_ref[pair] = jnp.dot(
-            mine, head_block(blocks[2 * pair : 2 * pair + 2], start), preferred_element_type=F32
+            mine, head_block(block_ref, swapped_ref, start, pair), preferred_element_type=F32
         )
 
 
@@ -225,16 +234,14 @@
     other_ref, gains_ref, near_ref, squares_ref, head_ref, swapped_ref, out_ref, block_ref, semaphore
 ):
     x, core = x_index(), 1 - lax.axis_index("c")
-    fetch = pltpu.make_async_copy(head_ref.at[:, x], block_ref, semaphore)
-    fetch.start()
     start = core * 128
+    fetch = fetch_own(head_ref, x, start, block_ref, semaphore)
     other, squares = scaled_rows(other_ref, gains_ref, core)
     stats = jnp.concatenate(split_pair(squares + squares_ref[...]), axis=0).astype(BF16)
     fetch.wait()
-    blocks = [block_ref] + [swapped_ref.at[k] for k in range(NX - 1)]
     for pair in range(NX // 2):
         partial = near_ref[pair] + jnp.dot(
-            other, head_block(blocks[2 * pair : 2 * pair + 2], start), preferred_element_type=F32
+            other, head_block(block_ref, swapped_ref, start, pair), preferred_element_type=F32
         )
         partial = partial.astype(BF16)
         for k in range(2):
@@ -347,7 +354,7 @@
     mine = exchange(hidden, ("y", "z"))
     mine, swapped = lax.optimization_barrier((mine, jnp.stack(swapped)))
     other = shift(mine, "c", 1)
-    scratch = (pltpu.VMEM((NZ, 256, 128), BF16), pltpu.SemaphoreType.DMA)
+    scratch = (pltpu.VMEM((NZ, 128, 128), BF16), pltpu.SemaphoreType.DMA)
     near, squares = call(
         near_kernel,
         (shape((NX // 2, ROWS, 256), F32), shape((NY, 128), F32)),

time: 153 us -> 153 us (level)
  no operation moved by 1% of the time
where the time goes in v8:
time: 153 us; the launch traced here: 152 us
  starting transfers between devices  54.4 us (36%)
  waiting for transfers between devices  43.6 us (28%)
  blocking collectives  37.3 us (24%)
  Pallas kernels  8.7 us (6%)
  local copies, waits for them, and re-layouts  4.37 us (3%)
  other arithmetic  2.38 us (2%)
    all_to_all x4, starting transfers between devices, exchange(): return lax.all_to_all(array, axes, 0, 0, tiled=True)  37.4 us
    all_to_all x3, blocking collectives, exchange(): return lax.all_to_all(array, axes, 0, 0, tiled=True)  37.3 us
    all_to_all x4, waiting for transfers between devices, exchange(): return lax.all_to_all(array, axes, 0, 0, tiled=True)  23.4 us
    ppermute x5, waiting for transfers between devices, shift(): lax.ppermute(array, axis, [(i, (i + step) % count) for i in range(count)])  20.2 us
    ppermute x5, starting transfers between devices, shift(): lax.ppermute(array, axis, [(i, (i + step) % count) for i in range(count)])  17 us
    pallas_call x9, Pallas kernels, call(): pl.pallas_call(body, out_shape=out_shape, in_specs=[kinds[s] for s in spa...  8.7 us
    unnamed x18, local copies, waits for them, and re-layouts  3.08 us
  transfers between devices with their start and end apart: 9, of which 7 were waited for; matrix products, arithmetic and copies ran while one was open for 2% of the time, Pallas kernels for 1%

profile of v8, /device:TPU:1, one launch (start us, length us, event | category | flops | bytes accessed | tf_op | source)
XLA Modules:
  0.0 151.7 jit_solution(12861844209639198860)
XLA Ops:
  0.7 2.5 %shard_map.91 = bf16[16,80,128]{2,1,0:T(8,128)(2,1)} custom-call(s32[1]{0:T(128)S(6)} %copy.11.length_ref, bf16[16,8192]{1,0:T(8,128)(2,1)} %bitcast.25, bf16[2,16,1024]{2,1,0:T(8,128)(2,1)} %bitcast.27, bf16[2,64,1024]{2,1,0:T(8,128)(2,1)} %bitcast.26), custom_call_target="tpu_custom_call" | custom-call | tf_op jit(solution)/shard_map/pallas_call | solution.py:37
  3.2 10.3 %all-to-all-start = ((bf16[16,80,128]{2,1,0:T(8,128)(2,1)}), bf16[16,80,128]{2,1,0:T(8,128)(2,1)S(1)}, u32[]{:S(2)}, u32[]{:S(2)}) async-start(bf16[16,80,128]{2,1,0:T(8,128)(2,1)} %shard_map.91), calls=%async_computation | async-start | bytes 655360 | tf_op jit(solution)/shard_map/all_to_all | solution.py:305
  13.5 1.9 %collective-permute-start = (bf16[512,256]{1,0:T(8,128)(2,1)S(1)}, bf16[512,256]{1,0:T(8,128)(2,1)S(1)}, u32[]{:S(2)}, u32[]{:S(2)}) collective-permute-start(bf16[512,256]{1,0:T(8,128)(2,1)S(1)} %copy-done.4), channel_id=1, source_target_pairs={{0,16},{16,0},{1,17},{17,1},{2,18},{18,2},{3,19},{19,3},{4,20},{20... | collective-permute-start | bytes 786440 | tf_op jit(solution)/shard_map/ppermute | solution.py:301
  15.4 7.7 %collective-permute-done._.other_ref = bf16[512,256]{1,0:T(8,128)(2,1)S(1)} collective-permute-done((bf16[512,256]{1,0:T(8,128)(2,1)S(1)}, bf16[512,256]{1,0:T(8,128)(2,1)S(1)}, u32[]{:S(2)}, u32[]{:S(2)}) %collective-permute-start) | collective-permute-done | bytes 262176 | tf_op jit(solution)/shard_map/ppermute | solution.py:301
  24.2 1.2 shard_map.92
  25.4 10.9 %all-to-all-start.1 = ((bf16[16,80,128]{2,1,0:T(8,128)(2,1)}), bf16[16,80,128]{2,1,0:T(8,128)(2,1)S(1)}, u32[]{:S(2)}, u32[]{:S(2)}) async-start(bf16[16,80,128]{2,1,0:T(8,128)(2,1)} %shard_map.92), calls=%async_computation.1 | async-start | bytes 655360 | tf_op jit(solution)/shard_map/all_to_all | solution.py:305
  36.4 1.2 dynamic-slice_bitcast_fusion.1
  37.6 4.7 %collective-permute-start.1 = (bf16[8,256,128]{2,1,0:T(8,128)(2,1)}, bf16[8,256,128]{2,1,0:T(8,128)(2,1)S(1)}, u32[]{:S(2)}, u32[]{:S(2)}) collective-permute-start(bf16[8,256,128]{2,1,0:T(8,128)(2,1)} %get-tuple-element.23), channel_id=1, source_target_pairs={{0,32},{16,48},{32,0},{48,16},{1,33},{17,49},{33,1},{49,17},{2,34}... | collective-permute-start | bytes 1572872 | tf_op jit(solution)/shard_map/ppermute | solution.py:301
  42.3 4.5 %all-to-all-done.1.attended_ref = bf16[16,80,128]{2,1,0:T(8,128)(2,1)S(1)} async-done(((bf16[16,80,128]{2,1,0:T(8,128)(2,1)}), bf16[16,80,128]{2,1,0:T(8,128)(2,1)S(1)}, u32[]{:S(2)}, u32[]{:S(2)}) %all-to-all-start.1) | async-done | bytes 327712 | tf_op jit(solution)/shard_map/all_to_all | solution.py:305
  48.8 9.0 %all-to-all-start.2 = ((bf16[32,32,128]{2,1,0:T(8,128)(2,1)}), bf16[32,32,128]{2,1,0:T(8,128)(2,1)S(1)}, u32[]{:S(2)}, u32[]{:S(2)}) async-start(bf16[32,32,128]{2,1,0:T(8,128)(2,1)} %copy-done.6), calls=%async_computation.2 | async-start | bytes 524288 | tf_op jit(solution)/shard_map/all_to_all | solution.py:305
  58.0 11.0 %all-to-all-done.2.parts_ref = bf16[32,32,128]{2,1,0:T(8,128)(2,1)S(1)} async-done(((bf16[32,32,128]{2,1,0:T(8,128)(2,1)}), bf16[32,32,128]{2,1,0:T(8,128)(2,1)S(1)}, u32[]{:S(2)}, u32[]{:S(2)}) %all-to-all-start.2) | async-done | bytes 262176 | tf_op jit(solution)/shard_map/all_to_all | solution.py:305
  69.0 1.1 shard_map.94
  70.1 7.2 %all-to-all-start.3 = ((bf16[64,64,128]{2,1,0:T(8,128)(2,1)}), bf16[64,64,128]{2,1,0:T(8,128)(2,1)S(1)}, u32[]{:S(2)}, u32[]{:S(2)}) async-start(bf16[64,64,128]{2,1,0:T(8,128)(2,1)} %shard_map.94), calls=%async_computation.3 | async-start | bytes 2097152 | tf_op jit(solution)/shard_map/all_to_all | solution.py:305
  77.3 2.1 %collective-permute-start.3 = (bf16[8,256,128]{2,1,0:T(8,128)(2,1)}, bf16[8,256,128]{2,1,0:T(8,128)(2,1)S(1)}, u32[]{:S(2)}, u32[]{:S(2)}) collective-permute-start(bf16[8,256,128]{2,1,0:T(8,128)(2,1)} %get-tuple-element.22), channel_id=1, source_target_pairs={{0,48},{16,0},{32,16},{48,32},{1,49},{17,1},{33,17},{49,33},{2,50}... | collective-permute-start | bytes 1572872 | tf_op jit(solution)/shard_map/ppermute | solution.py:301
  79.3 3.2 %collective-permute-start.2 = (bf16[8,256,128]{2,1,0:T(8,128)(2,1)}, bf16[8,256,128]{2,1,0:T(8,128)(2,1)S(1)}, u32[]{:S(2)}, u32[]{:S(2)}) collective-permute-start(bf16[8,256,128]{2,1,0:T(8,128)(2,1)} %get-tuple-element.21), channel_id=1, source_target_pairs={{0,16},{16,32},{32,48},{48,0},{1,17},{17,33},{33,49},{49,1},{2,18}... | collective-permute-start | bytes 1572872 | tf_op jit(solution)/shard_map/ppermute | solution.py:301
  82.6 9.6 %collective-permute-done.3 = bf16[8,256,128]{2,1,0:T(8,128)(2,1)S(1)} collective-permute-done((bf16[8,256,128]{2,1,0:T(8,128)(2,1)}, bf16[8,256,128]{2,1,0:T(8,128)(2,1)S(1)}, u32[]{:S(2)}, u32[]{:S(2)}) %collective-permute-start.3) | collective-permute-done | bytes 524320 | tf_op jit(solution)/shard_map/ppermute | solution.py:301
  92.2 2.9 %collective-permute-done.2 = bf16[8,256,128]{2,1,0:T(8,128)(2,1)S(1)} collective-permute-done((bf16[8,256,128]{2,1,0:T(8,128)(2,1)}, bf16[8,256,128]{2,1,0:T(8,128)(2,1)S(1)}, u32[]{:S(2)}, u32[]{:S(2)}) %collective-permute-start.2) | collective-permute-done | bytes 524320 | tf_op jit(solution)/shard_map/ppermute | solution.py:301
  95.0 2.4 %pad_maximum_fusion.swapped_ref = bf16[3,8,256,128]{3,2,1,0:T(8,128)(2,1)} fusion(bf16[1,8,256,128]{3,2,1,0:T(8,128)(2,1)S(1)} %bitcast.23, bf16[1,8,256,128]{3,2,1,0:T(8,128)(2,1)} %bitcast.20, bf16[1,8,256,128]{3,2,1,0:T(8,128)(2,1)S(1)} %bitcast.24), kind=kLoop, calls=%fused_computation | loop fusion | flops 1572864 | bytes 3145728 | tf_op jit(solution)/shard_map/stack | solution.py:355
  97.4 6.8 %all-to-all-done.3.mine_ref = bf16[64,64,128]{2,1,0:T(8,128)(2,1)S(1)} async-done(((bf16[64,64,128]{2,1,0:T(8,128)(2,1)}), bf16[64,64,128]{2,1,0:T(8,128)(2,1)S(1)}, u32[]{:S(2)}, u32[]{:S(2)}) %all-to-all-start.3) | async-done | bytes 1048608 | tf_op jit(solution)/shard_map/all_to_all | solution.py:305
  104.2 5.1 %collective-permute-start.4 = (bf16[64,64,128]{2,1,0:T(8,128)(2,1)S(1)}, bf16[64,64,128]{2,1,0:T(8,128)(2,1)S(1)}, u32[]{:S(2)}, u32[]{:S(2)}) collective-permute-start(bf16[64,64,128]{2,1,0:T(8,128)(2,1)S(1)} %all-to-all-done.3.mine_ref), channel_id=1, source_target_pairs={{0,1},{1,0},{2,3},{3,2},{4,5},{5,4},{6,7},{7,6},{8,9},{9,8},{10,11... | collective-permute-start | bytes 3145736 | tf_op jit(solution)/shard_map/ppermute | solution.py:301
  109.3 1.4 copy-done.2
  112.9 11.7 %all_to_all.35.parts_ref = bf16[4,528,128]{2,1,0:T(8,128)(2,1)S(1)} all-to-all(bf16[4,528,128]{2,1,0:T(8,128)(2,1)S(1)} %shard_map.96), channel_id=1, replica_groups=mesh['z'=8,'far'=2,'near'=2,'y'=8,'c'=2] {'far','near'}, dimensions={0} | all-to-all | bytes 1081344 | tf_op jit(solution)/shard_map/all_to_all | solution.py:305
  125.3 13.3 %all_to_all.36.parts_ref = f32[16,4,128]{2,1,0:T(4,128)S(1)} all-to-all(f32[16,4,128]{2,1,0:T(4,128)S(1)} %get-tuple-element.19), channel_id=1, replica_groups=mesh['z'=8,'far'=2,'near'=2,'y'=8,'c'=2] {'c','y'}, dimensions={0} | all-to-all | bytes 65536 | tf_op jit(solution)/shard_map/all_to_all | solution.py:305
  138.6 12.2 %all_to_all.37.parts_ref = f32[32,4,128]{2,1,0:T(4,128)S(1)} all-to-all(f32[32,4,128]{2,1,0:T(4,128)S(1)} %shard_map.98), channel_id=1, replica_groups=mesh['z'=8,'far'=2,'near'=2,'y'=8,'c'=2] {'far','near','z'}, dimensions={0} | all-to-all | bytes 131072 | tf_op jit(solution)/shard_map/all_to_all | solution.py:305
  (28 shorter events, 6.8 us)
Async XLA Ops:
  0.0 57.8 %copy-start = (bf16[16,32,256]{2,1,0:T(8,128)(2,1)S(1)}, bf16[16,32,256]{2,1,0:T(8,128)(2,1)}, u32[]{:S(2)}) copy-start(bf16[16,32,256]{2,1,0:T(8,128)(2,1)} %param.14) | copy-start | bytes 786436
  0.0 13.5 %copy-start.4 = (bf16[512,256]{1,0:T(8,128)(2,1)S(1)}, bf16[512,256]{1,0:T(8,128)(2,1)}, u32[]{:S(2)}) copy-start(bf16[512,256]{1,0:T(8,128)(2,1)} %mine_ref.1) | copy-start | bytes 786436
  0.0 24.2 %copy-start.8 = (f32[256]{0:T(256)S(1)}, f32[256]{0:T(256)}, u32[]{:S(2)}) copy-start(f32[256]{0:T(256)} %param.15) | copy-start | bytes 3076
  0.7 35.7 %copy-start.1 = (bf16[8192,128]{1,0:T(8,128)(2,1)S(1)}, bf16[8192,128]{1,0:T(8,128)(2,1)}, u32[]{:S(2)}) copy-start(bf16[8192,128]{1,0:T(8,128)(2,1)} %param.16) | copy-start | bytes 6291460
  3.2 21.0 %all-to-all-start = ((bf16[16,80,128]{2,1,0:T(8,128)(2,1)}), bf16[16,80,128]{2,1,0:T(8,128)(2,1)S(1)}, u32[]{:S(2)}, u32[]{:S(2)}) async-start(bf16[16,80,128]{2,1,0:T(8,128)(2,1)} %shard_map.91), calls=%async_computation | async-start | bytes 655360 | tf_op jit(solution)/shard_map/all_to_all | solution.py:305
  13.5 9.6 %collective-permute-start = (bf16[512,256]{1,0:T(8,128)(2,1)S(1)}, bf16[512,256]{1,0:T(8,128)(2,1)S(1)}, u32[]{:S(2)}, u32[]{:S(2)}) collective-permute-start(bf16[512,256]{1,0:T(8,128)(2,1)S(1)} %copy-done.4), channel_id=1, source_target_pairs={{0,16},{16,0},{1,17},{17,1},{2,18},{18,2},{3,19},{19,3},{4,20},{20... | collective-permute-start | bytes 786440 | tf_op jit(solution)/shard_map/ppermute | solution.py:301
  25.4 21.4 %all-to-all-start.1 = ((bf16[16,80,128]{2,1,0:T(8,128)(2,1)}), bf16[16,80,128]{2,1,0:T(8,128)(2,1)S(1)}, u32[]{:S(2)}, u32[]{:S(2)}) async-start(bf16[16,80,128]{2,1,0:T(8,128)(2,1)} %shard_map.92), calls=%async_computation.1 | async-start | bytes 655360 | tf_op jit(solution)/shard_map/all_to_all | solution.py:305
  37.6 20.4 %collective-permute-start.1 = (bf16[8,256,128]{2,1,0:T(8,128)(2,1)}, bf16[8,256,128]{2,1,0:T(8,128)(2,1)S(1)}, u32[]{:S(2)}, u32[]{:S(2)}) collective-permute-start(bf16[8,256,128]{2,1,0:T(8,128)(2,1)} %get-tuple-element.23), channel_id=1, source_target_pairs={{0,32},{16,48},{32,0},{48,16},{1,33},{17,49},{33,1},{49,17},{2,34}... | collective-permute-start | bytes 1572872 | tf_op jit(solution)/shard_map/ppermute | solution.py:301
  46.8 1.0 copy-start.5
  48.1 0.7 copy-start.6
  48.8 20.2 %all-to-all-start.2 = ((bf16[32,32,128]{2,1,0:T(8,128)(2,1)}), bf16[32,32,128]{2,1,0:T(8,128)(2,1)S(1)}, u32[]{:S(2)}, u32[]{:S(2)}) async-start(bf16[32,32,128]{2,1,0:T(8,128)(2,1)} %copy-done.6), calls=%async_computation.2 | async-start | bytes 524288 | tf_op jit(solution)/shard_map/all_to_all | solution.py:305
  58.0 12.2 %copy-start.3 = (bf16[8,256,128]{2,1,0:T(8,128)(2,1)}, bf16[8,256,128]{2,1,0:T(8,128)(2,1)S(1)}, u32[]{:S(2)}) copy-start(bf16[8,256,128]{2,1,0:T(8,128)(2,1)S(1)} %collective-permute-done.1._) | copy-start | bytes 1572868
  70.1 34.1 %all-to-all-start.3 = ((bf16[64,64,128]{2,1,0:T(8,128)(2,1)}), bf16[64,64,128]{2,1,0:T(8,128)(2,1)S(1)}, u32[]{:S(2)}, u32[]{:S(2)}) async-start(bf16[64,64,128]{2,1,0:T(8,128)(2,1)} %shard_map.94), calls=%async_computation.3 | async-start | bytes 2097152 | tf_op jit(solution)/shard_map/all_to_all | solution.py:305
  77.3 14.9 %collective-permute-start.3 = (bf16[8,256,128]{2,1,0:T(8,128)(2,1)}, bf16[8,256,128]{2,1,0:T(8,128)(2,1)S(1)}, u32[]{:S(2)}, u32[]{:S(2)}) collective-permute-start(bf16[8,256,128]{2,1,0:T(8,128)(2,1)} %get-tuple-element.22), channel_id=1, source_target_pairs={{0,48},{16,0},{32,16},{48,32},{1,49},{17,1},{33,17},{49,33},{2,50}... | collective-permute-start | bytes 1572872 | tf_op jit(solution)/shard_map/ppermute | solution.py:301
  79.3 15.7 %collective-permute-start.2 = (bf16[8,256,128]{2,1,0:T(8,128)(2,1)}, bf16[8,256,128]{2,1,0:T(8,128)(2,1)S(1)}, u32[]{:S(2)}, u32[]{:S(2)}) collective-permute-start(bf16[8,256,128]{2,1,0:T(8,128)(2,1)} %get-tuple-element.21), channel_id=1, source_target_pairs={{0,16},{16,32},{32,48},{48,0},{1,17},{17,33},{33,49},{49,1},{2,18}... | collective-permute-start | bytes 1572872 | tf_op jit(solution)/shard_map/ppermute | solution.py:301
  104.2 7.6 %collective-permute-start.4 = (bf16[64,64,128]{2,1,0:T(8,128)(2,1)S(1)}, bf16[64,64,128]{2,1,0:T(8,128)(2,1)S(1)}, u32[]{:S(2)}, u32[]{:S(2)}) collective-permute-start(bf16[64,64,128]{2,1,0:T(8,128)(2,1)S(1)} %all-to-all-done.3.mine_ref), channel_id=1, source_target_pairs={{0,1},{1,0},{2,3},{3,2},{4,5},{5,4},{6,7},{7,6},{8,9},{9,8},{10,11... | collective-permute-start | bytes 3145736 | tf_op jit(solution)/shard_map/ppermute | solution.py:301
  109.3 1.4 copy-start.2
  112.9 38.0 %copy-start.7 = (f32[16,128]{1,0:T(8,128)S(1)}, f32[16,128]{1,0:T(8,128)}, u32[]{:S(2)}) copy-start(f32[16,128]{1,0:T(8,128)} %noise_ref.1) | copy-start | bytes 24580
